TPU v7x, 32 devices: a whole 2x2x4 slice. The times are simulated.
32 devices in a mesh: page: 4 (over y, x), rows: 8 (over z, core).
Axes of the slice: x: 2, y: 2, z: 4, core: 2. Of those that a mesh axis runs over, the one named last changes fastest.
Arguments:
- patches: bfloat16 [8, 80, 120, 512], P('page', 'rows'), may hold values from -6 to 6
- out_grad: bfloat16 [8, 80, 120, 512], P('page', 'rows'), may hold values from -6 to 6
- page_windows: int32 [8], P('page'), may hold values from 6 to 12, as said below
- region_ids: int32 [8, 80, 120], P('page', 'rows'), may hold values from 0 to 3
- offset_index: int32 [100, 100], replicated, may hold values from 0 to 360
- weights_in: bfloat16 [512, 4096], replicated, may hold values from -0.25 to 0.25
- weights_out: bfloat16 [2048, 512], replicated, may hold values from -0.125 to 0.125
- norm_gains: float32 [2, 512], replicated, may hold values from 0.5 to 1.5
- biases: float32 [5120], replicated, may hold values from -1.75 to 1.75
- bias_table: float32 [361, 16], replicated, may hold values from -6 to 6
- master_in: float32 [512, 4096], P('rows'), may hold values from -0.25 to 0.25
- master_out: float32 [2048, 512], P('rows'), may hold values from -0.125 to 0.125
- first_in: float32 [512, 4096], P('rows'), may hold values from -96 to 96
- second_in: float32 [512, 4096], P('rows'), may hold values from 15.36 to 76.8
- first_out: float32 [2048, 512], P('rows'), may hold values from -96 to 96
- second_out: float32 [2048, 512], P('rows'), may hold values from 15.36 to 76.8
- first_small: float32 [11920], replicated, may hold values from -80 to 80
- second_small: float32 [11920], replicated, may hold values from 7.68 to 38.4
Outputs:
- mixed: bfloat16 [8, 80, 120, 512], P('page', 'rows')
- patch_grad: bfloat16 [8, 80, 120, 512], P('page', 'rows')
- new_in: float32 [512, 4096], P('rows')
- moment_in: float32 [512, 4096], P('rows')
- square_in: float32 [512, 4096], P('rows')
- new_out: float32 [2048, 512], P('rows')
- moment_out: float32 [2048, 512], P('rows')
- square_out: float32 [2048, 512], P('rows')
- new_small: float32 [11920], replicated
- moment_small: float32 [11920], replicated
- square_small: float32 [11920], replicated
Inputs may be any that keep to these rules, and one draw needn't show every extreme that they name: `page_windows`: some page is 12 windows wide and some (12 + 1) // 2.
All inputs are finite; a program needn't handle non-finite values.
Results may differ from a plain program's by a relative error of at most 0.0085.
Values may be sent and summed in bfloat16 or wider, within the bound.
A program may use at most 256 MiB of HBM per device.

v0:
```python
import jax
import jax.numpy as jnp
from jax import lax
from jax.sharding import PartitionSpec as P

STEP = 10


NORM_EPS = 1e-05
BETA_ONE = 0.9
BETA_TWO = 0.999
LEARN_RATE = 0.04
WEIGHT_DECAY = 0.05
ADAM_EPS = 1e-08
MASK_VALUE = -1000000000.0
HIGH = lax.Precision.HIGHEST


def from_behind(shard, axis, by):
    peers = lax.axis_size(axis)
    return lax.ppermute(shard, axis, [(i, (i + by) % peers) for i in range(peers)])


def layer_norm(value, gain, offset):
    centre = jnp.mean(value, axis=-1, keepdims=True)
    centered = value - centre
    spread = lax.rsqrt(jnp.mean(centered * centered, axis=-1, keepdims=True) + NORM_EPS)
    return centered * spread * gain + offset


def exact_gelu(value):
    return jax.nn.gelu(value, approximate=False)


def to_windows(field, window):
    pages, height, width = (field.shape[0], field.shape[1], field.shape[2])
    count = width // window
    rest = field.shape[3:]
    shaped = field.reshape((pages, height // window, window, count, window) + rest)
    order = (0, 1, 3, 2, 4) + tuple(range(5, 5 + len(rest)))
    return shaped.transpose(order).reshape(
        (pages * (height // window) * count, window * window) + rest
    )


def from_windows(tiles, pages, height, width, window):
    count = width // window
    rest = tiles.shape[2:]
    shaped = tiles.reshape((pages, height // window, count, window, window) + rest)
    order = (0, 1, 3, 2, 4) + tuple(range(5, 5 + len(rest)))
    return shaped.transpose(order).reshape((pages, height, width) + rest)


def column_tables(page_windows, width, window, offset):
    columns = jnp.arange(width, dtype=jnp.int32)[None, :]
    live_width = page_windows[:, None] * window
    inside = columns < live_width
    forward_cols = jnp.where(inside, (columns + offset) % live_width, columns)
    backward_cols = jnp.where(inside, (columns - offset) % live_width, columns)
    return (inside, forward_cols, backward_cols)


def pick_columns(field, table):
    return jax.vmap(lambda page, cols: page[:, cols])(field, table)


def adam_update(master, first, second, grad):
    moment = BETA_ONE * first + (1.0 - BETA_ONE) * grad
    square = BETA_TWO * second + (1.0 - BETA_TWO) * grad * grad
    fix_one = 1.0 - BETA_ONE**STEP
    fix_two = 1.0 - BETA_TWO**STEP
    fresh = master - LEARN_RATE * (
        moment / fix_one / (jnp.sqrt(square / fix_two) + ADAM_EPS) + WEIGHT_DECAY * master
    )
    return (fresh, moment, square)


def shards(
    patches,
    out_grad,
    page_windows,
    region_ids,
    offset_index,
    weights_in,
    weights_out,
    norm_gains,
    biases,
    bias_table,
    master_in,
    master_out,
    first_in,
    second_in,
    first_out,
    second_out,
    first_small,
    second_small,
):
    f32 = jnp.float32
    b16 = jnp.bfloat16
    pages, window, width, model = patches.shape
    half = window // 2
    heads = bias_table.shape[1]
    size_head = model // heads
    ratio = size_head ** (-0.5)
    place = lax.axis_index("rows")
    inside, forward_cols, backward_cols = column_tables(page_windows, width, window, half)
    live_tiles = to_windows(jnp.broadcast_to(inside[:, None, :], (pages, window, width)), window)
    live_rows = live_tiles[..., None]
    labels = to_windows(region_ids, window)
    same = labels[:, :, None] == labels[:, None, :]
    table_bias = bias_table[offset_index].transpose(2, 0, 1)
    w_qkv = weights_in[:, : 3 * model]
    w_proj = weights_in[:, 3 * model : 4 * model]
    w_up = weights_in[:, 4 * model :]
    bias_qkv = jnp.concatenate(
        [biases[model : 2 * model], jnp.zeros((model,), f32), biases[2 * model : 3 * model]]
    )
    below = from_behind(patches[:, :half], "rows", -1)
    shifted = pick_columns(jnp.concatenate([patches[:, half:], below], axis=1), forward_cols)
    tiles = to_windows(shifted, window).astype(f32)
    groups, tokens = (tiles.shape[0], tiles.shape[1])
    norm_one, back_one = jax.vjp(layer_norm, tiles, norm_gains[0], biases[:model])
    low_one = norm_one.astype(b16)
    qkv = (jnp.einsum("gtd,de->gte", low_one, w_qkv, preferred_element_type=f32) + bias_qkv).astype(
        b16
    )
    split = qkv.reshape(groups, tokens, 3, heads, size_head)
    query, key_part, value = (split[:, :, 0], split[:, :, 1], split[:, :, 2])
    scores = (
        jnp.einsum("gqhe,gkhe->ghqk", query, key_part, preferred_element_type=f32) * ratio
        + table_bias[None]
    )
    scores = jnp.where(same[:, None], scores, MASK_VALUE)
    probs = jax.nn.softmax(scores, axis=-1)
    low_probs = probs.astype(b16)
    attended = (
        jnp.einsum("ghqk,gkhe->gqhe", low_probs, value, preferred_element_type=f32)
        .astype(b16)
        .reshape(groups, tokens, model)
    )
    branch = (
        jnp.einsum("gtd,de->gte", attended, w_proj, preferred_element_type=f32)
        + biases[3 * model : 4 * model]
    )
    first = tiles + branch
    norm_two, back_two = jax.vjp(layer_norm, first, norm_gains[1], biases[4 * model : 5 * model])
    low_two = norm_two.astype(b16)
    pre_act = (
        jnp.einsum("gtd,df->gtf", low_two, w_up, preferred_element_type=f32) + biases[6 * model :]
    )
    activated, back_act = jax.vjp(exact_gelu, pre_act)
    low_act = activated.astype(b16)
    result = (
        first
        + jnp.einsum("gtf,fd->gtd", low_act, weights_out, preferred_element_type=f32)
        + biases[5 * model : 6 * model]
    )
    framed = from_windows(
        jnp.where(live_rows, result, 0.0).astype(b16), pages, window, width, window
    )
    framed = pick_columns(framed, backward_cols)
    above = from_behind(framed[:, half:], "rows", 1)
    mixed = jnp.concatenate([above, framed[:, :half]], axis=1)
    below_grad = from_behind(out_grad[:, :half], "rows", -1)
    grad_frame = pick_columns(
        jnp.concatenate([out_grad[:, half:], below_grad], axis=1), forward_cols
    )
    cotangent = jnp.where(live_rows, to_windows(grad_frame, window).astype(f32), 0.0)
    grad_mlp = cotangent.astype(b16)
    grad_w_out = jnp.einsum("gtf,gtd->fd", low_act, grad_mlp, preferred_element_type=f32)
    grad_b_out = jnp.sum(grad_mlp, axis=(0, 1), dtype=f32)
    grad_act = jnp.einsum("gtd,fd->gtf", grad_mlp, weights_out, preferred_element_type=f32)
    grad_pre = back_act(grad_act)[0].astype(b16)
    grad_w_up = jnp.einsum("gtd,gtf->df", low_two, grad_pre, preferred_element_type=f32)
    grad_b_up = jnp.sum(grad_pre, axis=(0, 1), dtype=f32)
    grad_norm_two = jnp.einsum("gtf,df->gtd", grad_pre, w_up, preferred_element_type=f32)
    grad_first_norm, grad_gain_two, grad_beta_two = back_two(grad_norm_two)
    grad_first = cotangent + grad_first_norm
    grad_branch = grad_first.astype(b16)
    grad_w_proj = jnp.einsum("gtd,gte->de", attended, grad_branch, preferred_element_type=f32)
    grad_b_proj = jnp.sum(grad_branch, axis=(0, 1), dtype=f32)
    grad_attended = jnp.einsum(
        "gte,de->gtd", grad_branch, w_proj, preferred_element_type=f32
    ).astype(b16)
    grad_attended = grad_attended.reshape(groups, tokens, heads, size_head)
    grad_probs = jnp.einsum("gqhe,gkhe->ghqk", grad_attended, value, preferred_element_type=f32)
    grad_value = jnp.einsum("ghqk,gqhe->gkhe", low_probs, grad_attended, preferred_element_type=f32)
    grad_scores = (
        probs * (grad_probs - jnp.sum(probs * grad_probs, axis=-1, keepdims=True))
    ).astype(b16)
    grad_query = (
        jnp.einsum("ghqk,gkhe->gqhe", grad_scores, key_part, preferred_element_type=f32) * ratio
    )
    grad_key = jnp.einsum("ghqk,gqhe->gkhe", grad_scores, query, preferred_element_type=f32) * ratio
    score_sum = jnp.sum(grad_scores, axis=0, dtype=f32).reshape(heads, tokens * tokens)
    table_rows = bias_table.shape[0]
    one_hot = (
        offset_index.reshape(-1)[:, None] == jnp.arange(table_rows, dtype=jnp.int32)[None, :]
    ).astype(f32)
    grad_table = jnp.einsum("nt,hn->th", one_hot, score_sum, precision=HIGH)
    grad_qkv = (
        jnp.stack([grad_query, grad_key, grad_value], axis=2)
        .astype(b16)
        .reshape(groups, tokens, 3 * model)
    )
    grad_w_qkv = jnp.einsum("gtd,gte->de", low_one, grad_qkv, preferred_element_type=f32)
    grad_b_qkv = jnp.sum(grad_qkv, axis=(0, 1), dtype=f32)
    grad_norm_one = jnp.einsum("gte,de->gtd", grad_qkv, w_qkv, preferred_element_type=f32)
    grad_tiles_norm, grad_gain_one, grad_beta_one = back_one(grad_norm_one)
    grad_tiles = jnp.where(live_rows, grad_first + grad_tiles_norm, 0.0)
    grad_framed = from_windows(grad_tiles.astype(b16), pages, window, width, window)
    grad_framed = pick_columns(grad_framed, backward_cols)
    above_grad = from_behind(grad_framed[:, half:], "rows", 1)
    patch_grad = jnp.concatenate([above_grad, grad_framed[:, :half]], axis=1)
    grad_in = jnp.concatenate([grad_w_qkv, grad_w_proj, grad_w_up], axis=1)
    grad_small = jnp.concatenate(
        [
            grad_gain_one,
            grad_gain_two,
            grad_beta_one,
            grad_b_qkv[:model],
            grad_b_qkv[2 * model :],
            grad_b_proj,
            grad_beta_two,
            grad_b_out,
            grad_b_up,
            grad_table.reshape(-1),
        ]
    )
    share_in = master_in.shape[0]
    share_out = master_out.shape[0]
    total_in, total_out, total_small = lax.psum((grad_in, grad_w_out, grad_small), ("page", "rows"))
    part_in = lax.dynamic_slice_in_dim(total_in, place * share_in, share_in, 0)
    part_out = lax.dynamic_slice_in_dim(total_out, place * share_out, share_out, 0)
    small_master = jnp.concatenate([norm_gains.reshape(-1), biases, bias_table.reshape(-1)])
    new_in, moment_in, square_in = adam_update(master_in, first_in, second_in, part_in)
    new_out, moment_out, square_out = adam_update(master_out, first_out, second_out, part_out)
    new_small, moment_small, square_small = adam_update(
        small_master, first_small, second_small, total_small
    )
    return (
        mixed,
        patch_grad,
        new_in,
        moment_in,
        square_in,
        new_out,
        moment_out,
        square_out,
        new_small,
        moment_small,
        square_small,
    )


def solution(mesh):
    return jax.shard_map(
        shards,
        mesh=mesh,
        in_specs=(
            P("page", "rows", None, None),
            P("page", "rows", None, None),
            P("page"),
            P("page", "rows", None),
            P(),
            P(),
            P(),
            P(),
            P(),
            P(),
            P("rows", None),
            P("rows", None),
            P("rows", None),
            P("rows", None),
            P("rows", None),
            P("rows", None),
            P(),
            P(),
        ),
        out_specs=(
            P("page", "rows", None, None),
            P("page", "rows", None, None),
            P("rows", None),
            P("rows", None),
            P("rows", None),
            P("rows", None),
            P("rows", None),
            P("rows", None),
            P(),
            P(),
            P(),
        ),
        check_vma=False,
    )
```

profile of v0, /device:TPU:0, one launch (start us, length us, event | category | flops | bytes accessed | tf_op | source)
XLA Modules:
  0.0 822.5 jit_solution(12869719144075473480)
XLA Ops:
  30.7 22.0 %gather_fusion = f32[10000,16]{1,0:T(8,128)} fusion(f32[361,16]{1,0:T(8,128)S(1)} %copy.171, s32[10240]{0:T(1024)} %pad_clamp_fusion), kind=kCustom, calls=%fused_computation | custom fusion | bytes 1320000 | tf_op jit(solution)/shard_map/gather | solution.py:111
  72.4 6.9 copy.157
  121.4 7.0 copy.188
  129.5 8.1 add_convert_fusion.1
  137.6 11.8 %copy.164 = bf16[24,100,1536]{1,2,0:T(8,128)(2,1)} copy(bf16[24,100,1536]{2,1,0:T(8,128)(2,1)} %add_convert_fusion.1) | data formatting | bytes 14745600 | tf_op jit(solution)/shard_map/convert_element_type | solution.py:124
  162.9 15.2 %fusion.30 = f32[24,16,100,100]{2,3,1,0:T(8,128)} fusion(bf16[24,100,3,16,32]{1,4,3,2,0:T(8,128)(2,1)} %bitcast.184), kind=kOutput, calls=%fused_computation.87 | convolution fusion | flops 245760000 | bytes 21651456 | tf_op jit(solution)/shard_map/gqhe,gkhe->ghqk/dot_general | solution.py:130
  178.2 27.8 %fusion.103 = (f32[24,16,100]{2,1,0:T(8,128)S(1)}, f32[24,16,100,100]{2,3,1,0:T(8,128)}) fusion(f32[24,16,100,100]{2,3,1,0:T(8,128)} %fusion.30, f32[16,100,100]{1,2,0:T(8,128)S(1)} %copy-done.23, pred[24,100,100]{1,2,0:T(8,128)(4,1)S(1)} %copy-done.25), kind=kOutput, calls=%fused_computation.196 | output fusion | flops 30720100 | bytes 31753600 | tf_op jit(solution)/shard_map/sub | solution.py:134
  206.0 12.2 %fusion.44 = bf16[24,16,32,100]{3,2,1,0:T(8,128)(2,1)} fusion(bf16[24,100,3,16,32]{1,4,3,2,0:T(8,128)(2,1)} %bitcast.185, f32[24,16,100,100]{2,3,1,0:T(8,128)} %get-tuple-element.96, f32[24,16,100]{2,1,0:T(8,128)S(1)} %get-tuple-element.95), kind=kOutput, calls=%fused_computation.101 | convolution fusion | flops 254668800 | bytes 26204160 | tf_op jit(solution)/shard_map/ghqk,gkhe->gqhe/dot_general | solution.py:137
  222.9 7.1 fusion.104
  239.7 14.8 %convert_reduce_fusion.1 = (u32[100,2048]{1,0:T(8,128)}, u32[100,2048]{1,0:T(8,128)}, f32[24,100,2048]{2,1,0:T(8,128)S(1)}) fusion(f32[2048]{0:T(1024)S(1)} %slice.96, bf16[512,4096]{1,0:T(8,128)(2,1)} %param.25, bf16[24,100,512]{2,0,1:T(8,128)(2,1)} %add_convert_fusion.3), kind=kOutput, calls=%fused_computation.12 | convolution fusion | flops 5091737600 | bytes 25862144 | tf_op jit(solution)/shard_map/gtd,df->gtf/dot_general | solution.py:149
  254.5 48.6 %multiply_convert_fusion.1 = (bf16[24,100,2048]{2,1,0:T(8,128)(2,1)}, f32[24,100,2048]{2,1,0:T(8,128)}) fusion(f32[24,100,2048]{2,1,0:T(8,128)S(1)} %get-tuple-element.99, f32[2048]{0:T(1024)S(1)} %slice.96, u32[100,2048]{1,0:T(8,128)} %get-tuple-element.46, u32[100,2048]{1,0:T(8,128)} %get-tuple-element.45), kind=kLoop, calls=%fused_computation.18 | loop fusion | flops 339148800 | bytes 50798592 | tf_op jit(solution)/shard_map/convert_element_type | solution.py:152
  303.2 23.0 %convert_reduce_fusion.3 = (f32[2048]{0:T(1024)}, bf16[24,100,2048]{2,1,0:T(8,128)(2,1)}) fusion(f32[24,100,2048]{2,1,0:T(8,128)} %get-tuple-element.71, bf16[2048,512]{1,0:T(8,128)(2,1)S(1)} %copy-done, bf16[24,100,512]{2,0,1:T(8,128)(2,1)S(1)} %select_convert_fusion.2, f32[24,100,2048]{2,1,0:T(8,128)} %copy-done.4, f32[2048]{0:T(1024)S(1)} %slice.96), kind=kOutput, calls=%fused_computation.14 | convolution fusion | flops 5116721152 | bytes 53723136 | tf_op jit(solution)/shard_map/gtd,fd->gtf/dot_general | solution.py:172
  326.2 14.4 %fusion.25 = f32[512,2048]{1,0:T(8,128)} fusion(bf16[24,100,512]{2,0,1:T(8,128)(2,1)} %add_convert_fusion.3, bf16[24,100,2048]{2,1,0:T(8,128)(2,1)} %get-tuple-element.107), kind=kOutput, calls=%fused_computation.79 | convolution fusion | flops 5033164800 | bytes 16482304 | tf_op jit(solution)/shard_map/gtd,gtf->df/dot_general | solution.py:174
  340.6 9.4 %fusion.106 = (f32[512]{0:T(512)}, f32[24,100,512]{2,1,0:T(8,128)S(1)}) fusion(bf16[24,100,2048]{2,1,0:T(8,128)(2,1)} %get-tuple-element.107, bf16[512,4096]{1,0:T(8,128)(2,1)S(1)} %copy-done.35), kind=kOutput, calls=%fused_computation.199 | convolution fusion | flops 5034393088 | bytes 16844800 | tf_op jit(solution)/shard_map/gtf,df->gtd/dot_general | solution.py:176
  350.1 7.8 convolution_bitcast_fusion
  357.9 7.3 fusion.48
  370.5 14.3 %fusion.94 = (f32[24,100]{0,1:T(8,128)S(1)}, f32[24,100,512]{2,0,1:T(8,128)}, bf16[24,100,512]{2,0,1:T(8,128)(2,1)}) fusion(f32[24,100]{0,1:T(8,128)S(1)} %copy.193, f32[24,100,512]{2,0,1:T(8,128)} %get-tuple-element.98, f32[24,100]{0,1:T(8,128)S(1)} %copy.178, f32[24,100]{0,1:T(8,128)S(1)} %copy.180, f32[512]{0:T(512)S(1)} %bitcast.218, ...), kind=kLoop, calls=%fused_computation.188 | loop fusion | flops 13514400 | bytes 22163296 | tf_op jit(solution)/shard_map/transpose(jvp())/reduce_sum | solution.py:26
  401.9 11.7 %fusion.32 = bf16[24,100,1,16,32]{1,4,3,0,2:T(8,128)(2,1)} fusion(bf16[24,100,16,32]{1,3,2,0:T(8,128)(2,1)} %bitcast.208, f32[24,16,100,100]{2,3,1,0:T(8,128)} %get-tuple-element.96, f32[24,16,100]{2,1,0:T(8,128)S(1)} %get-tuple-element.95), kind=kOutput, calls=%fused_computation.89 | convolution fusion | flops 253440000 | bytes 20428800 | tf_op jit(solution)/shard_map/ghqk,gqhe->gkhe/dot_general | solution.py:187
  413.6 15.6 %multiply_reduce_fusion = (f32[24,16,100]{2,1,0:T(8,128)S(1)}, f32[24,16,100,100]{2,3,1,0:T(8,128)}) fusion(f32[24,16,100,100]{2,3,1,0:T(8,128)} %get-tuple-element.96, f32[24,16,100]{2,1,0:T(8,128)S(1)} %get-tuple-element.95, bf16[24,100,16,32]{1,3,2,0:T(8,128)(2,1)} %bitcast.209, bf16[24,100,3,16,32]{1,4,3,2,0:T(8,128)(2,1)} %bitcast.186), kind=kOutput, calls=%fused_computation.16 | convolution fusion | flops 257241600 | bytes 42405888 | tf_op jit(solution)/shard_map/gqhe,gkhe->ghqk/dot_general | solution.py:186
  429.2 18.2 %convert_reduce_fusion.2 = (f32[16,100,100]{1,2,0:T(8,128)S(1)}, bf16[24,16,100,100]{2,3,1,0:T(8,128)(2,1)}) fusion(f32[24,16,100,100]{2,3,1,0:T(8,128)} %get-tuple-element.101, f32[24,16,100]{2,1,0:T(8,128)S(1)} %get-tuple-element.100, f32[24,16,100,100]{2,3,1,0:T(8,128)} %get-tuple-element.96, f32[24,16,100]{2,1,0:T(8,128)S(1)} %get-tuple-element.95), kind=kLoop, calls=%fused_computation.13 | loop fusion | flops 22880000 | bytes 39347200 | tf_op jit(solution)/shard_map/reduce_sum | solution.py:195
  447.3 12.0 %multiply_bitcast_fusion = bf16[24,100,1,16,32]{1,4,3,0,2:T(8,128)(2,1)} fusion(bf16[24,16,100,100]{2,3,1,0:T(8,128)(2,1)} %get-tuple-element.57, bf16[24,100,3,16,32]{1,4,3,2,0:T(8,128)(2,1)} %bitcast.187), kind=kOutput, calls=%fused_computation.51 | convolution fusion | flops 248217600 | bytes 15826944 | tf_op jit(solution)/shard_map/ghqk,gqhe->gkhe/dot_general | solution.py:194
  459.3 7.9 multiply_bitcast_fusion.1
  467.2 7.1 convert_reduce_fusion.4
  474.3 10.4 %copy.201 = bf16[24,100,3,16,32]{1,4,3,2,0:T(8,128)(2,1)} copy(bf16[24,100,3,16,32]{1,4,3,0,2:T(8,128)(2,1)} %get-tuple-element.61) | data formatting | bytes 14745600 | tf_op jit(solution)/shard_map/convert_element_type | solution.py:203
  484.7 11.6 %fusion.105 = (f32[512]{0:T(512)S(1)}, f32[24,100,512]{2,1,0:T(8,128)}) fusion(bf16[24,100,1536]{1,2,0:T(8,128)(2,1)} %bitcast.193, bf16[512,4096]{1,0:T(8,128)(2,1)} %param.25), kind=kOutput, calls=%fused_computation.198 | convolution fusion | flops 3776101888 | bytes 15927296 | tf_op jit(solution)/shard_map/gte,de->gtd/dot_general | solution.py:208
  496.3 12.5 %copy.213 = bf16[24,100,1536]{2,0,1:T(8,128)(2,1)} copy(bf16[24,100,1536]{1,2,0:T(8,128)(2,1)} %bitcast.194) | data formatting | bytes 14745600 | tf_op jit(solution)/shard_map/convert_element_type | solution.py:203
  561.8 7.2 multiply_reduce_fusion.3
  569.2 9.2 %multiply_reduce_fusion.2 = (f32[512]{0:T(512)S(1)}, f32[24,100]{0,1:T(8,128)S(1)}) fusion(f32[24,100,512]{2,1,0:T(8,128)} %get-tuple-element.103, f32[24,100,512]{2,0,1:T(8,128)} %reshape.246, f32[24,100]{0,1:T(8,128)S(1)} %copy-done.22, f32[24,100]{0,1:T(8,128)S(1)} %copy-done.18, f32[24,100]{0,1:T(8,128)S(1)} %copy.206, f32[512]{0:T(512)S(1)} %bitcast.214), kind=kLoop, calls=%fused_computation.65 | loop fusion | flops 12285088 | bytes 9872896 | tf_op jit(solution)/shard_map/transpose(jvp())/reduce_sum | solution.py:28
  578.6 11.1 %select_convert_fusion.1 = bf16[24,100,512]{2,0,1:T(8,128)(2,1)} fusion(f32[24,100]{0,1:T(8,128)S(1)} %copy.208, pred[24,100]{0,1:T(8,128)(4,1)S(1)} %copy.154, f32[24,100,512]{2,0,1:T(8,128)} %get-tuple-element.69, f32[24,100]{0,1:T(8,128)S(1)} %copy.195, f32[24,100,512]{2,0,1:T(8,128)} %reshape.247, f32[24,100]{0,1:T(8,128)S(1)} %copy.206, ...), kind=kLoop, calls=%fused_computation.67 | loop fusion | flops 15974400 | bytes 22170848 | tf_op jit(solution)/shard_map/convert_element_type | solution.py:211
  614.0 10.1 %fusion.15 = f32[361,16]{1,0:T(8,128)S(1)} fusion(f32[16,10000]{1,0:T(8,128)S(1)} %copy-done.24, s32[10000]{0:T(1024)S(1)} %copy-done.41), kind=kOutput, calls=%fused_computation.47 | convolution fusion | flops 700339968 | bytes 703104 | tf_op jit(solution)/shard_map/nt,hn->th/dot_general | solution.py:200
  626.6 43.2 %psum.23 = f32[11920]{0:T(1024)S(1)} all-reduce(f32[11920]{0:T(1024)S(1)} %constant_dynamic-update-slice_fusion.1), channel_id=1, replica_groups=mesh['page'=4,'rows'=8] {'page','rows'}, use_global_device_ids=true, to_apply=%region_22.24 | all-reduce | flops 11920 | bytes 95360 | tf_op jit(solution)/shard_map/psum | solution.py:232
  676.9 131.4 %all-reduce.3.cloned.1.call-done = (f32[512,4096]{1,0:T(8,128)}, f32[2048,512]{1,0:T(8,128)}) async-done(((f32[512,4096]{1,0:T(8,128)}, f32[2048,512]{1,0:T(8,128)}), (f32[512,4096]{1,0:T(8,128)}, f32[2048,512]{1,0:T(8,128)})) %all-reduce.3.cloned.1.call-update) | async-done | bytes 12582928 | tf_op jit(solution)/shard_map/psum | solution.py:232
  (269 shorter events, 230.3 us)
Async XLA Ops:
  7.2 296.0 %copy-start = (bf16[2048,512]{1,0:T(8,128)(2,1)S(1)}, bf16[2048,512]{1,0:T(8,128)(2,1)}, u32[]{:S(2)}) copy-start(bf16[2048,512]{1,0:T(8,128)(2,1)} %param.26) | copy-start | bytes 6291460
  7.2 12.5 %copy-start.44 = (f32[2,512]{1,0:T(2,128)S(1)}, f32[2,512]{1,0:T(2,128)}, u32[]{:S(2)}) copy-start(f32[2,512]{1,0:T(2,128)} %param.27) | copy-start | bytes 12292
  7.2 801.1 %all-reduce.3.cloned.1.call-start = ((), (), s32[]{:S(2)}) async-start(), calls=%async_computation | async-start | bytes 25165824 | tf_op jit(solution)/shard_map/psum | solution.py:232
  10.3 51.1 %collective-permute-start = (bf16[2,5,120,512]{3,2,1,0:T(8,128)(2,1)}, bf16[2,5,120,512]{3,2,1,0:T(8,128)(2,1)}, u32[]{:S(2)}, u32[]{:S(2)}) collective-permute-start(bf16[2,5,120,512]{3,2,1,0:T(8,128)(2,1)} %get-tuple-element.80), channel_id=1, source_target_pairs={{0,7},{1,0},{2,1},{3,2},{4,3},{5,4},{6,5},{7,6},{8,15},{9,8},{10,9... | collective-permute-start | bytes 3686408 | tf_op jit(solution)/shard_map/ppermute | solution.py:21
  16.5 92.4 %collective-permute-start.2 = (bf16[2,5,120,512]{3,2,1,0:T(8,128)(2,1)}, bf16[2,5,120,512]{3,2,1,0:T(8,128)(2,1)}, u32[]{:S(2)}, u32[]{:S(2)}) collective-permute-start(bf16[2,5,120,512]{3,2,1,0:T(8,128)(2,1)} %get-tuple-element.76), channel_id=1, source_target_pairs={{0,7},{1,0},{2,1},{3,2},{4,3},{5,4},{6,5},{7,6},{8,15},{9,8},{10,9... | collective-permute-start | bytes 3686408 | tf_op jit(solution)/shard_map/ppermute | solution.py:21
  60.1 68.3 %copy-start.42 = (f32[512]{0:T(512)}, f32[512]{0:T(512)S(1)}, u32[]{:S(2)}) copy-start(f32[512]{0:T(512)S(1)} %get-tuple-element.90) | copy-start | bytes 6148
  60.2 68.2 %copy-start.33 = (f32[1,512]{1,0:T(1,128)}, f32[1,512]{1,0:T(1,128)S(1)}, u32[]{:S(2)}) copy-start(f32[1,512]{1,0:T(1,128)S(1)} %get-tuple-element.92) | copy-start | bytes 6148
  91.8 36.5 %copy-start.17 = (f32[24,100]{0,1:T(8,128)}, f32[24,100]{0,1:T(8,128)S(1)}, u32[]{:S(2)}) copy-start(f32[24,100]{0,1:T(8,128)S(1)} %div.92) | copy-start | bytes 28804
  102.1 26.2 %copy-start.21 = (f32[24,100]{0,1:T(8,128)}, f32[24,100]{0,1:T(8,128)S(1)}, u32[]{:S(2)}) copy-start(f32[24,100]{0,1:T(8,128)S(1)} %copy.162) | copy-start | bytes 28804
  162.9 15.2 %copy-start.23 = (f32[16,100,100]{1,2,0:T(8,128)S(1)}, f32[16,100,100]{1,2,0:T(8,128)}, u32[]{:S(2)}) copy-start(f32[16,100,100]{1,2,0:T(8,128)} %copy.173) | copy-start | bytes 1920004
  162.9 15.2 %copy-start.25 = (pred[24,100,100]{1,2,0:T(8,128)(4,1)S(1)}, pred[24,100,100]{1,2,0:T(8,128)(4,1)}, u32[]{:S(2)}) copy-start(pred[24,100,100]{1,2,0:T(8,128)(4,1)} %broadcast_compare_fusion) | copy-start | bytes 720004
  254.5 48.6 %copy-start.4 = (f32[24,100,2048]{2,1,0:T(8,128)}, f32[24,100,2048]{2,1,0:T(8,128)S(1)}, u32[]{:S(2)}) copy-start(f32[24,100,2048]{2,1,0:T(8,128)S(1)} %get-tuple-element.99) | copy-start | bytes 58982404
  326.2 14.4 %copy-start.35 = (bf16[512,4096]{1,0:T(8,128)(2,1)S(1)}, bf16[512,4096]{1,0:T(8,128)(2,1)}, u32[]{:S(2)}) copy-start(bf16[512,4096]{1,0:T(8,128)(2,1)} %param.25) | copy-start | bytes 12582916
  326.2 23.8 %slice-start.6 = ((s8[10223616]{0:T(1024)(128)(4,1)}), s8[4194304]{0:T(1024)(128)(4,1)S(1)}, s32[]{:S(2)}) async-start(s8[10223616]{0:T(1024)(128)(4,1)} %bitcast.199), calls=%async_computation.7 | async-start | bytes 8388608
  326.2 23.8 %slice-start.7 = ((s8[10223616]{0:T(1024)(128)(4,1)}), s8[4194304]{0:T(1024)(128)(4,1)S(1)}, s32[]{:S(2)}) async-start(s8[10223616]{0:T(1024)(128)(4,1)} %bitcast.199), calls=%async_computation.8 | async-start | bytes 8388608
  340.6 24.6 %slice-start.2 = ((s8[4915200]{0:T(1024)(128)(4,1)}), s8[720896]{0:T(1024)(128)(4,1)S(1)}, s32[]{:S(2)}) async-start(s8[4915200]{0:T(1024)(128)(4,1)} %bitcast.182), calls=%async_computation.3 | async-start | bytes 1441792
  350.1 15.1 %copy-start.5 = (f32[24,100,512]{2,1,0:T(8,128)}, f32[24,100,512]{2,1,0:T(8,128)S(1)}, u32[]{:S(2)}) copy-start(f32[24,100,512]{2,1,0:T(8,128)S(1)} %get-tuple-element.105) | copy-start | bytes 14745604
  350.1 15.1 %slice-start.3 = ((s8[4915200]{0:T(1024)(128)(4,1)}), s8[4194304]{0:T(1024)(128)(4,1)S(1)}, s32[]{:S(2)}) async-start(s8[4915200]{0:T(1024)(128)(4,1)} %bitcast.182), calls=%async_computation.4 | async-start | bytes 8388608
  496.3 12.5 %copy-start.7 = (f32[2,12,10,10]{0,3,1,2:T(8,128)S(1)}, f32[2,12,10,10]{0,3,1,2:T(8,128)}, u32[]{:S(2)}) copy-start(f32[2,12,10,10]{0,3,1,2:T(8,128)} %copy-done.6) | copy-start | bytes 28804
  496.3 12.5 %copy-start.11 = (f32[2,12,10,10]{0,3,1,2:T(8,128)S(1)}, f32[2,12,10,10]{0,3,1,2:T(8,128)}, u32[]{:S(2)}) copy-start(f32[2,12,10,10]{0,3,1,2:T(8,128)} %get-tuple-element.81) | copy-start | bytes 28804
  496.3 12.5 %copy-start.34 = (f32[1,512]{1,0:T(1,128)S(1)}, f32[1,512]{1,0:T(1,128)}, u32[]{:S(2)}) copy-start(f32[1,512]{1,0:T(1,128)} %copy-done.33) | copy-start | bytes 6148
  496.3 12.5 %copy-start.43 = (f32[512]{0:T(512)S(1)}, f32[512]{0:T(512)}, u32[]{:S(2)}) copy-start(f32[512]{0:T(512)} %copy-done.42) | copy-start | bytes 6148
  560.1 110.4 %collective-permute-start.1 = (bf16[2,5,120,512]{3,2,0,1:T(8,128)(2,1)}, bf16[2,5,120,512]{3,2,0,1:T(8,128)(2,1)}, u32[]{:S(2)}, u32[]{:S(2)}) collective-permute-start(bf16[2,5,120,512]{3,2,0,1:T(8,128)(2,1)} %get-tuple-element.77), channel_id=1, source_target_pairs={{0,1},{1,2},{2,3},{3,4},{4,5},{5,6},{6,7},{7,0},{8,9},{9,10},{10,1... | collective-permute-start | bytes 3686408 | tf_op jit(solution)/shard_map/ppermute | solution.py:21
  612.5 11.7 %slice-start.4 = ((s8[4915200]{0:T(1024)(128)(4,1)}), s8[4194304]{0:T(1024)(128)(4,1)S(1)}, s32[]{:S(2)}) async-start(s8[4915200]{0:T(1024)(128)(4,1)} %bitcast.190), calls=%async_computation.5 | async-start | bytes 8388608
  613.7 60.0 %collective-permute-start.3 = (bf16[2,5,120,512]{3,2,0,1:T(8,128)(2,1)}, bf16[2,5,120,512]{3,2,0,1:T(8,128)(2,1)}, u32[]{:S(2)}, u32[]{:S(2)}) collective-permute-start(bf16[2,5,120,512]{3,2,0,1:T(8,128)(2,1)} %get-tuple-element.73), channel_id=1, source_target_pairs={{0,1},{1,2},{2,3},{3,4},{4,5},{5,6},{6,7},{7,0},{8,9},{9,10},{10,1... | collective-permute-start | bytes 3686408 | tf_op jit(solution)/shard_map/ppermute | solution.py:21
  614.0 12.6 %copy-start.50 = (f32[512]{0:T(512)S(1)}, f32[512]{0:T(512)}, u32[]{:S(2)}) copy-start(f32[512]{0:T(512)} %get-tuple-element.58) | copy-start | bytes 6148
  614.0 12.6 %copy-start.51 = (f32[512]{0:T(512)S(1)}, f32[512]{0:T(512)}, u32[]{:S(2)}) copy-start(f32[512]{0:T(512)} %get-tuple-element.104) | copy-start | bytes 6148
  614.0 12.6 %copy-start.49 = (f32[2048]{0:T(1024)S(1)}, f32[2048]{0:T(1024)}, u32[]{:S(2)}) copy-start(f32[2048]{0:T(1024)} %get-tuple-element.106) | copy-start | bytes 24580
  614.0 55.9 %copy-start.37 = (f32[11920]{0:T(1024)S(1)}, f32[11920]{0:T(1024)}, u32[]{:S(2)}) copy-start(f32[11920]{0:T(1024)} %copy-done.36) | copy-start | bytes 143044
  614.0 55.9 %copy-start.39 = (f32[11920]{0:T(1024)S(1)}, f32[11920]{0:T(1024)}, u32[]{:S(2)}) copy-start(f32[11920]{0:T(1024)} %param.36) | copy-start | bytes 143044
  614.0 55.9 %copy-start.40 = (f32[11920]{0:T(1024)S(1)}, f32[11920]{0:T(1024)}, u32[]{:S(2)}) copy-start(f32[11920]{0:T(1024)} %param.37) | copy-start | bytes 143044
  675.2 133.1 %copy-start.20 = (f32[64,4096]{1,0:T(8,128)S(1)}, f32[64,4096]{1,0:T(8,128)}, u32[]{:S(2)}) copy-start(f32[64,4096]{1,0:T(8,128)} %param.30) | copy-start | bytes 3145732
  (35 other events, 232.5 us)
Sparse Core Ops, SparseCore 0:
  557.4 250.8 all-reduce.2
where the time goes:
time: 829 us; the launch traced here: 822 us
  local copies, waits for them, and re-layouts  216 us (26%)
  other arithmetic  209 us (25%)
  matrix products  202 us (24%)
  waiting for transfers between devices  131 us (16%)
  blocking collectives  43.2 us (5%)
  between operations  15.2 us (2%)
    psum x1, waiting for transfers between devices, shards(): lax.psum((grad_in, grad_w_out, grad_small), ('page', 'rows'))  131 us
    convert_element_type x1, other arithmetic, shards(): low_act = activated.astype(b16)  48.6 us
    psum x1, blocking collectives, shards(): lax.psum((grad_in, grad_w_out, grad_small), ('page', 'rows'))  43.2 us
    gather x8, local copies, waits for them, and re-layouts, pick_columns(): return jax.vmap(lambda page, cols: page[:, cols])(field, table)  32.9 us
    sub x1, other arithmetic, shards(): probs = jax.nn.softmax(scores, axis=-1)  27.8 us
    gather x3, local copies, waits for them, and re-layouts, shards(): table_bias = bias_table[offset_index].transpose(2, 0, 1)  27.5 us
    dot_general x1, matrix products, shards(): jnp.einsum('gtd,fd->gtf', grad_mlp, weights_out, preferred_element_type=f32)  23 us
    convert_element_type x2, local copies, waits for them, and re-layouts, shards(): grad_qkv = jnp.stack([grad_query, grad_key, grad_value], axis=2).astype(b...  22.9 us
  transfers between devices with their start and end apart: 5, of which 1 were waited for; matrix products, arithmetic and copies ran while one was open for 20% of the time, Pallas kernels for 0%

commit v1 on v0

v1 whole, which is shorter than its diff:
```python
import functools
import math

import jax
import jax.numpy as jnp
from jax import lax
from jax.experimental import pallas as pl
from jax.experimental.pallas import tpu as pltpu
from jax.sharding import PartitionSpec as P

STEP = 10
NORM_EPS = 1e-05
BETA_ONE = 0.9
BETA_TWO = 0.999
LEARN_RATE = 0.04
WEIGHT_DECAY = 0.05
ADAM_EPS = 1e-08
MASK_VALUE = -1000000000.0

F32 = jnp.float32
B16 = jnp.bfloat16
LOG2E = math.log2(math.e)
VMEM_LIMIT = 60 * 2**20

QUAD = 4
SLOT = 128
KEYS = 104


def dot(left, right, form="NN"):
    sides = {
        "NN": ((1,), (0,)),
        "NT": ((1,), (1,)),
        "TN": ((0,), (0,)),
    }[form]
    return lax.dot_general(left, right, (sides, ((), ())), preferred_element_type=F32)


def load_band(band, low_ref, high_ref, live, half, width, window, least):
    band[:half, :width] = low_ref[...].astype(F32)
    band[half:, :width] = high_ref[...].astype(F32)
    band[:, width:] = jnp.zeros((window, band.shape[1] - width, band.shape[2]), F32)
    wrap_band(band, live, half, width, window, least)


def wrap_band(band, live, half, width, window, least):
    for count in range(least, width // window + 1):
        at = slice(count * window, count * window + half)
        band[:, at] = jnp.where(live == count, band[:, :half], band[:, at])


def unwrap_band(band, live, half, width, window, least):
    for count in range(least, width // window + 1):

        @pl.when(live == count)
        def _():
            edge = count * window
            band[:, :half] = band[:, edge : edge + half]
            band[:, edge:] = jnp.zeros((window, band.shape[1] - edge, band.shape[2]), F32)


def piece(band, row, base, place, window, half):
    start = window * place + half
    aligned = start // 8 * 8
    skip = start - aligned
    size = -(-(skip + window) // 8) * 8
    ref = band.at[row, pl.ds(pl.multiple_of(base, 8) + aligned, size), :]
    return ref, skip


def gather_window(band, base, place, window, half):
    parts = []
    for row in range(window):
        ref, skip = piece(band, row, base, place, window, half)
        parts.append(ref[skip : skip + window, :])
    return parts


def norm_stats(value):
    centre = jnp.mean(value, axis=-1, keepdims=True)
    centered = value - centre
    spread = lax.rsqrt(jnp.mean(centered * centered, axis=-1, keepdims=True) + NORM_EPS)
    return centered * spread, spread


def fold(value):
    rows, cols = value.shape
    return jnp.sum(value.reshape(rows // 8, 8, cols), axis=0)


MESH = pl.DeviceIdType.MESH


def remote(src, dst, send, recv, device):
    return pltpu.make_async_remote_copy(
        src_ref=src, dst_ref=dst, send_sem=send, recv_sem=recv, device_id=device, device_id_type=MESH
    )


def attn_forward_kernel(
    sizes,
    live_ref,
    patches_ref,
    grads_ref,
    low_ref,
    label_ref,
    off_ref,
    tab_ref,
    wqkv_ref,
    bqkv_ref,
    wproj_ref,
    vec_ref,
    x_ref,
    n1_ref,
    qkv_ref,
    probs_ref,
    att_ref,
    first_ref,
    n2_ref,
    grad_halo_ref,
    halo,
    send,
    recv,
    band,
    bias,
    scores,
    bdq,
    bdv,
    stacked,
    xs,
    ns,
):
    window, half, width, model, heads, least, pages, rows_count = sizes
    slots = window * window
    size_head = model // heads
    page, quad = pl.program_id(0), pl.program_id(1)
    live = live_ref[page]
    pairs = heads // 2
    row = lax.axis_index("rows")
    behind, ahead = lax.rem(row + rows_count - 1, rows_count), lax.rem(row + 1, rows_count)

    def halo_copy(p):
        return remote(
            patches_ref.at[p, pl.ds(0, half)], halo.at[p], send.at[p], recv.at[p], {"rows": behind}
        )

    def grad_copy(p):
        return remote(
            grads_ref.at[p, pl.ds(0, half)],
            grad_halo_ref.at[p],
            send.at[pages + p],
            recv.at[pages + p],
            {"rows": behind},
        )

    @pl.when(jnp.logical_and(page == 0, quad == 0))
    def _():
        barrier = pltpu.get_barrier_semaphore()
        for neighbour in (behind, ahead):
            pl.semaphore_signal(barrier, inc=1, device_id={"rows": neighbour}, device_id_type=MESH)
        pl.semaphore_wait(barrier, 2)
        for p in range(pages):
            halo_copy(p).start()
        for p in range(pages):
            grad_copy(p).start()
        off = off_ref[...]
        low, high = jnp.bitwise_and(off, 127), jnp.right_shift(off, 7)
        for h in range(heads):
            got = jnp.zeros((KEYS, SLOT), F32)
            for c in range(tab_ref.shape[1] // 128):
                source = jnp.broadcast_to(tab_ref[h : h + 1, 128 * c : 128 * c + 128], (KEYS, SLOT))
                picked = jnp.take_along_axis(source, low, axis=1, mode="promise_in_bounds")
                got = jnp.where(high == c, picked, got)
            bias[h] = got
        bdq[...] = jnp.zeros_like(bdq)
        bdv[...] = jnp.zeros_like(bdv)
        stacked[...] = jnp.zeros_like(stacked)

    for p in range(pages):

        @pl.when(jnp.logical_and(page == p, quad == 0))
        def _():
            halo_copy(p).wait()
            load_band(band, low_ref.at[0], halo.at[p], live, half, width, window, least)

    @pl.when(jnp.logical_and(page == pages - 1, quad == pl.num_programs(1) - 1))
    def _():
        for p in range(pages):
            grad_copy(p).wait()

    base = quad * (QUAD * window)
    for w in range(QUAD):
        for r, part in enumerate(gather_window(band, base, w, window, half)):
            at = slots * w + window * r
            xs[at : at + window, :] = part
    x = xs[...]
    x_ref[...] = x.astype(B16)
    xhat, _ = norm_stats(x)
    ns[...] = xhat * vec_ref[0:1, :] + vec_ref[1:2, :]
    for w in range(QUAD):
        n1_ref[SLOT * w : SLOT * w + slots, :] = ns[slots * w : slots * w + slots, :].astype(B16)
        n1_ref[SLOT * w + slots : SLOT * w + SLOT, :] = jnp.zeros((SLOT - slots, model), B16)
    scale = size_head**-0.5 * LOG2E
    n1 = n1_ref[...]
    for part in range(3):
        rows = slice(part * model, part * model + model)
        got = dot(wqkv_ref[rows, :], n1, "NT") + bqkv_ref[rows, :]
        if part == 0:
            got = got * scale
        qkv_ref[rows, :] = got.astype(B16)

    sames = []
    for w in range(QUAD):
        spread = jnp.broadcast_to(label_ref[0, w : w + 1, :], (SLOT, SLOT))
        sames.append((spread == spread.T)[:KEYS])
    pair = 2 * size_head

    def score(w, g):
        low = pair * g
        lanes = slice(SLOT * w, SLOT * w + SLOT)
        for j in range(2):
            at = slice(low + size_head * j, low + size_head * (j + 1))
            cols = slice(SLOT * j, SLOT * j + SLOT)
            bdq[w % 2, at, cols] = qkv_ref[at, lanes]
            values = slice(2 * model + low + size_head * j, 2 * model + low + size_head * (j + 1))
            bdv[w % 3, at, cols] = qkv_ref[values, lanes]
        keys = qkv_ref[model + low : model + low + pair, SLOT * w : SLOT * w + KEYS]
        scores[w % 2, g] = dot(keys, bdq[w % 2, low : low + pair, :], "TN")

    def soften(w, g):
        for j in range(2):
            cols = slice(SLOT * j, SLOT * j + SLOT)
            s = jnp.where(sames[w], scores[w % 2, g, :, cols] + bias[2 * g + j], MASK_VALUE)
            s = jnp.exp2(s - jnp.max(s, axis=0, keepdims=True))
            low_probs = (s * (1.0 / jnp.sum(s, axis=0, keepdims=True))).astype(B16)
            probs_ref[w, g, :KEYS, cols] = low_probs
            probs_ref[w, g, KEYS:, cols] = jnp.zeros((SLOT - KEYS, SLOT), B16)
            stacked[w % 2, g, SLOT * j : SLOT * j + KEYS, :] = low_probs

    def attend(w, g):
        low = pair * g
        got = dot(bdv[w % 3, low : low + pair, :], stacked[w % 2, g])
        att_ref[low : low + pair, SLOT * w : SLOT * w + SLOT] = got.astype(B16)

    for step in range(QUAD + 2):
        for g in range(pairs):
            if step < QUAD:
                score(step, g)
            if 1 <= step <= QUAD:
                soften(step - 1, g)
            if step >= 2:
                attend(step - 2, g)

    branch = dot(att_ref[...], wproj_ref[...], "TN")
    for w in range(QUAD):
        rows = slice(slots * w, slots * w + slots)
        first_ref[rows, :] = xs[rows, :] + branch[SLOT * w : SLOT * w + slots, :] + vec_ref[2:3, :]
    xhat, _ = norm_stats(first_ref[...])
    n2_ref[...] = (xhat * vec_ref[3:4, :] + vec_ref[4:5, :]).astype(B16)


def attn_forward(live, patches, out_grad, labels, off, tab, wqkv, bqkv, wproj, vecs, least):
    pages, window, width, model = patches.shape
    half = window // 2
    heads = tab.shape[0]
    quads = width // window // QUAD
    tokens = pages * window * width
    slots = window * window
    padded = pages * quads * QUAD * SLOT
    steps = (pages, quads)
    whole = lambda a: pl.BlockSpec(a.shape, lambda p, j: (0,) * a.ndim, pipeline_mode=pl.Buffered(1))
    at = lambda p, j: p * quads + j
    return pl.pallas_call(
        functools.partial(
            attn_forward_kernel,
            (window, half, width, model, heads, least, pages, lax.axis_size("rows")),
        ),
        grid=steps,
        in_specs=[
            pl.BlockSpec(memory_space=pltpu.SMEM),
            pl.BlockSpec(memory_space=pl.ANY),
            pl.BlockSpec(memory_space=pl.ANY),
            pl.BlockSpec((1, half, width, model), lambda p, j: (p, 1, 0, 0)),
            pl.BlockSpec((1, 8, SLOT), lambda p, j: (at(p, j), 0, 0)),
            whole(off),
            whole(tab),
            whole(wqkv),
            whole(bqkv),
            whole(wproj),
            whole(vecs),
        ],
        out_specs=[
            pl.BlockSpec((QUAD * slots, model), lambda p, j: (at(p, j), 0)),
            pl.BlockSpec((QUAD * SLOT, model), lambda p, j: (at(p, j), 0)),
            pl.BlockSpec((3 * model, QUAD * SLOT), lambda p, j: (0, at(p, j))),
            pl.BlockSpec((QUAD, heads // 2, SLOT, 2 * SLOT), lambda p, j: (at(p, j), 0, 0, 0)),
            pl.BlockSpec((model, QUAD * SLOT), lambda p, j: (0, at(p, j))),
            pl.BlockSpec((QUAD * slots, model), lambda p, j: (at(p, j), 0)),
            pl.BlockSpec((QUAD * slots, model), lambda p, j: (at(p, j), 0)),
            pl.BlockSpec(memory_space=pl.ANY),
        ],
        out_shape=[
            jax.ShapeDtypeStruct((tokens, model), B16),
            jax.ShapeDtypeStruct((padded, model), B16),
            jax.ShapeDtypeStruct((3 * model, padded), B16),
            jax.ShapeDtypeStruct((pages * quads * QUAD, heads // 2, SLOT, 2 * SLOT), B16),
            jax.ShapeDtypeStruct((model, padded), B16),
            jax.ShapeDtypeStruct((tokens, model), F32),
            jax.ShapeDtypeStruct((tokens, model), B16),
            jax.ShapeDtypeStruct((pages, half, width, model), B16),
        ],
        scratch_shapes=[
            pltpu.VMEM((pages, half, width, model), B16),
            pltpu.SemaphoreType.DMA((2 * pages,)),
            pltpu.SemaphoreType.DMA((2 * pages,)),
            pltpu.VMEM((window, width + 8, model), F32),
            pltpu.VMEM((heads, KEYS, SLOT), F32),
            pltpu.VMEM((2, heads // 2, KEYS, 2 * SLOT), F32),
            pltpu.VMEM((2, model, 2 * SLOT), B16),
            pltpu.VMEM((3, model, 2 * SLOT), B16),
            pltpu.VMEM((2, heads // 2, 2 * SLOT, SLOT), B16),
            pltpu.VMEM((QUAD * slots, model), F32),
            pltpu.VMEM((QUAD * slots, model), F32),
        ],
        compiler_params=pltpu.CompilerParams(
            vmem_limit_bytes=VMEM_LIMIT, collective_id=1, has_side_effects=True
        ),
    )(live, patches, out_grad, patches, labels, off, tab, wqkv, bqkv, wproj, vecs)


MLP_COLS = 512
MLP_ROWS = 480


def mlp_kernel(
    sizes,
    live_ref,
    low_ref,
    high_ref,
    n2_ref,
    first_ref,
    wup_ref,
    wout_ref,
    bup_ref,
    vec_ref,
    dwup_ref,
    dwout_ref,
    dbup_ref,
    gf_ref,
    own_ref,
    next_ref,
    sums_ref,
    band,
    cot,
    res,
    dn2,
    act_all,
    pre_all,
):
    window, half, width, model, least, share = sizes
    pages = low_ref.shape[0]
    slots = window * window
    count = width // window
    quads = count // QUAD
    chunk = pl.program_id(0)
    tokens = n2_ref.shape[0]
    cols = wup_ref.shape[1]

    @pl.when(chunk == 0)
    def _():
        for page in range(pages):
            live = live_ref[page]
            load_band(band, low_ref.at[page], high_ref.at[page], live, half, width, window, least)

            def body(j, carry):
                for w in range(QUAD):
                    alive = jnp.where(j * QUAD + w < live, 1.0, 0.0)
                    for r, part in enumerate(gather_window(band, j * QUAD * window, w, window, half)):
                        at = slots * w + window * r
                        gf_ref[at : at + window, :] = part * alive
                rows = pl.ds(pl.multiple_of((page * quads + j) * QUAD * slots, 16), QUAD * slots)
                cot[rows, :] = gf_ref[: QUAD * slots, :].astype(B16)
                return carry

            lax.fori_loop(0, quads, body, 0)

    def body(i, total):
        rows = pl.ds(pl.multiple_of(i * MLP_ROWS, 16), MLP_ROWS)
        grad = cot[rows, :]
        pre = dot(n2_ref[rows, :], wup_ref[...]) + bup_ref[...]
        grad_act = dot(grad, wout_ref[...], "NT")
        share = 0.5 * (1.0 + lax.erf(pre * 0.5**0.5))
        act = (pre * share).astype(B16)
        slope = share + pre * (jnp.exp2((-0.5 * LOG2E) * pre * pre) * (2.0 * math.pi) ** -0.5)
        grad_pre = (grad_act * slope).astype(B16)
        act_all[rows, :] = act
        pre_all[rows, :] = grad_pre
        up = dot(act, wout_ref[...])
        down = dot(grad_pre, wup_ref[...], "NT")

        @pl.when(chunk == 0)
        def _():
            res[rows, :] = up
            dn2[rows, :] = down

        @pl.when(chunk > 0)
        def _():
            res[rows, :] += up
            dn2[rows, :] += down

        return total + fold(grad_pre.astype(F32))

    total = lax.fori_loop(0, tokens // MLP_ROWS, body, jnp.zeros((8, cols), F32))
    dbup_ref[...] = jnp.sum(total, axis=0, keepdims=True)
    grad_out = dot(act_all[...], cot[...], "TN").astype(B16)
    for s in range(dwout_ref.shape[0] // share):
        for a in range(dwout_ref.shape[1] // model):
            at = (s * (dwout_ref.shape[1] // model) + a) * share
            dwout_ref[share * s : share * s + share, model * a : model * a + model] = grad_out[at : at + share, :]
    dwup_ref[...] = dot(n2_ref[...], pre_all[...], "TN").astype(B16)

    @pl.when(chunk == pl.num_programs(0) - 1)
    def _():
        sums_ref[...] = jnp.zeros_like(sums_ref)
        for page in range(pages):
            live = live_ref[page]

            def body(j, carry):
                at = pl.multiple_of((page * quads + j) * QUAD * slots, 16)
                rows = pl.ds(at, QUAD * slots)
                first = first_ref[rows, :]
                res[rows, :] += first + vec_ref[1:2, :]
                xhat, spread = norm_stats(first)
                grad = dn2[rows, :]
                given = cot[rows, :].astype(F32)
                scaled = grad * vec_ref[0:1, :]
                mean_one = jnp.mean(scaled, axis=-1, keepdims=True)
                mean_two = jnp.mean(scaled * xhat, axis=-1, keepdims=True)
                whole = given + spread * (scaled - mean_one - xhat * mean_two)
                gf_ref[rows, :] = whole
                sums_ref[0:8, :] += fold(grad * xhat)
                sums_ref[8:16, :] += fold(grad)
                sums_ref[16:24, :] += fold(given)
                sums_ref[24:32, :] += fold(whole)
                for w in range(QUAD):
                    for r in range(window):
                        ref, skip = piece(band, r, j * QUAD * window, w, window, half)
                        ref[skip : skip + window, :] = res[
                            pl.ds(at + slots * w // 8 * 8, slots + 4), :
                        ][slots * w % 8 + window * r : slots * w % 8 + window * r + window, :]
                return carry

            lax.fori_loop(0, quads, body, 0)
            unwrap_band(band, live, half, width, window, least)
            own_ref[page] = band[:half, :width].astype(B16)
            next_ref[page] = band[half:, :width].astype(B16)


def mlp(live, out_grad, halo, n2, first, weights_in, weights_out, bup, vecs, least, share):
    pages, window, width, model = out_grad.shape
    half = window // 2
    tokens = n2.shape[0]
    hidden = weights_out.shape[0]
    skip = (weights_in.shape[1] - hidden) // MLP_COLS
    once = pl.Buffered(1)
    whole = lambda a: pl.BlockSpec(a.shape, lambda c: (0,) * a.ndim, pipeline_mode=once)
    band_block = (pages, half, width, model)
    return pl.pallas_call(
        functools.partial(mlp_kernel, (window, half, width, model, least, share)),
        grid=(hidden // MLP_COLS,),
        in_specs=[
            pl.BlockSpec(memory_space=pltpu.SMEM),
            pl.BlockSpec(band_block, lambda c: (0, 1, 0, 0), pipeline_mode=once),
            pl.BlockSpec(band_block, lambda c: (0, 0, 0, 0), pipeline_mode=once),
            whole(n2),
            whole(first),
            pl.BlockSpec((model, MLP_COLS), lambda c: (0, c + skip)),
            pl.BlockSpec((MLP_COLS, model), lambda c: (c, 0)),
            pl.BlockSpec((1, MLP_COLS), lambda c: (0, c)),
            whole(vecs),
        ],
        out_specs=[
            pl.BlockSpec((model, MLP_COLS), lambda c: (0, c)),
            pl.BlockSpec((model * MLP_COLS // hidden, hidden), lambda c: (c, 0)),
            pl.BlockSpec((1, MLP_COLS), lambda c: (0, c)),
            pl.BlockSpec((tokens, model), lambda c: (0, 0), pipeline_mode=once),
            pl.BlockSpec(band_block, lambda c: (0, 1, 0, 0), pipeline_mode=once),
            pl.BlockSpec(band_block, lambda c: (0, 0, 0, 0), pipeline_mode=once),
            pl.BlockSpec((32, model), lambda c: (0, 0)),
        ],
        out_shape=[
            jax.ShapeDtypeStruct((model, hidden), B16),
            jax.ShapeDtypeStruct((model, hidden), B16),
            jax.ShapeDtypeStruct((1, hidden), F32),
            jax.ShapeDtypeStruct((tokens, model), F32),
            jax.ShapeDtypeStruct(out_grad.shape, B16),
            jax.ShapeDtypeStruct(band_block, B16),
            jax.ShapeDtypeStruct((32, model), F32),
        ],
        scratch_shapes=[
            pltpu.VMEM((window, width + 8, model), F32),
            pltpu.VMEM((tokens, model), B16),
            pltpu.VMEM((tokens, model), F32),
            pltpu.VMEM((tokens, model), F32),
            pltpu.VMEM((tokens, MLP_COLS), B16),
            pltpu.VMEM((tokens, MLP_COLS), B16),
        ],
        compiler_params=pltpu.CompilerParams(vmem_limit_bytes=VMEM_LIMIT),
    )(live, out_grad, halo, n2, first, weights_in, weights_out, bup, vecs)


def attn_backward_kernel(
    sizes,
    live_ref,
    gf_ref,
    x_ref,
    n1_ref,
    qkv_ref,
    probs_ref,
    att_ref,
    wproj_ref,
    wqkv_ref,
    vec_ref,
    dwa_ref,
    dbqkv_ref,
    dscore_ref,
    sums_ref,
    own_ref,
    next_ref,
    band,
    gbp,
    datt,
    dprobs,
    bdq,
    bdk,
    bdo,
    stacked,
    beside,
    dqkv,
    dwq,
    dwp,
    compact,
):
    window, half, width, model, heads, least = sizes
    slots = window * window
    size_head = model // heads
    page, quad = pl.program_id(0), pl.program_id(1)
    live = live_ref[page]
    pairs = heads // 2
    pair = 2 * size_head

    @pl.when(jnp.logical_and(page == 0, quad == 0))
    def _():
        for ref in (bdq, bdk, bdo, stacked, beside, gbp, dwq, dwp, dbqkv_ref, dscore_ref, sums_ref):
            ref[...] = jnp.zeros_like(ref)

    for w in range(QUAD):
        gbp[SLOT * w : SLOT * w + slots, :] = gf_ref[slots * w : slots * w + slots, :].astype(B16)
    datt[...] = dot(wproj_ref[...], gbp[...], "NT").astype(B16)
    dwp[...] += dot(att_ref[...], gbp[...])

    @pl.when(quad * QUAD >= live)
    def _():
        dqkv[...] = jnp.zeros_like(dqkv)

    @pl.when(quad * QUAD < live)
    def _():
        ratio = size_head**-0.5

        def score(w, g):
            low = pair * g
            lanes = slice(SLOT * w, SLOT * w + SLOT)
            for j in range(2):
                at = slice(low + size_head * j, low + size_head * (j + 1))
                keys = slice(model + low + size_head * j, model + low + size_head * (j + 1))
                cols = slice(SLOT * j, SLOT * j + SLOT)
                bdo[w % 3, at, cols] = datt[at, lanes]
                bdq[w % 3, at, cols] = qkv_ref[at, lanes]
                bdk[w % 3, at, cols] = qkv_ref[keys, lanes]
            values = qkv_ref[2 * model + low : 2 * model + low + pair, SLOT * w : SLOT * w + KEYS]
            dprobs[w % 2, g] = dot(values, bdo[w % 3, low : low + pair, :], "TN")

        def soften(w, g):
            probs = probs_ref[w, g, :KEYS, :].astype(F32)
            term = probs * dprobs[w % 2, g]
            grad = term - probs * jnp.sum(term, axis=0, keepdims=True)
            dscore_ref[g] += grad
            low_grad = grad.astype(B16)
            beside[w % 2, g, :KEYS, :] = low_grad
            for j in range(2):
                stacked[w % 2, g, SLOT * j : SLOT * j + KEYS, :] = low_grad[:, SLOT * j : SLOT * j + SLOT]

        def attend(w, g):
            low = pair * g
            lanes = slice(SLOT * w, SLOT * w + SLOT)
            rows = slice(low, low + pair)
            got = dot(bdk[w % 3, rows, :], stacked[w % 2, g]) * ratio
            dqkv[low : low + pair, lanes] = got.astype(B16)
            got = dot(bdq[w % 3, rows, :], beside[w % 2, g], "NT") * (1.0 / LOG2E)
            dqkv[model + low : model + low + pair, lanes] = got.astype(B16)
            got = dot(bdo[w % 3, rows, :], probs_ref[w, g], "NT")
            dqkv[2 * model + low : 2 * model + low + pair, lanes] = got.astype(B16)

        for step in range(QUAD + 2):
            for g in range(pairs):
                if step < QUAD:
                    score(step, g)
                if 1 <= step <= QUAD:
                    soften(step - 1, g)
                if step >= 2:
                    attend(step - 2, g)

    n1 = n1_ref[...]
    for part in range(3):
        rows = slice(part * model, part * model + model)
        grad = dqkv[rows, :]
        dwq[rows, :] += dot(grad, n1)
        wide = grad.astype(F32)
        both = wide[:, :SLOT]
        for w in range(1, QUAD):
            both = both + wide[:, SLOT * w : SLOT * w + SLOT]
        dbqkv_ref[rows, :] += both
    dn1 = dot(dqkv[...], wqkv_ref[...], "TN")
    for w in range(QUAD):
        compact[slots * w : slots * w + slots, :] = dn1[SLOT * w : SLOT * w + slots, :]
    grad = compact[...]
    xhat, spread = norm_stats(x_ref[...].astype(F32))
    scaled = grad * vec_ref[0:1, :]
    mean_one = jnp.mean(scaled, axis=-1, keepdims=True)
    mean_two = jnp.mean(scaled * xhat, axis=-1, keepdims=True)
    sums_ref[0:8, :] += fold(grad * xhat)
    sums_ref[8:16, :] += fold(grad)
    compact[...] = gf_ref[...] + spread * (scaled - mean_one - xhat * mean_two)
    for w in range(QUAD):
        for r in range(window):
            ref, skip = piece(band, r, quad * QUAD * window, w, window, half)
            at = slots * w + window * r
            ref[skip : skip + window, :] = compact[at : at + window, :]

    @pl.when(quad == pl.num_programs(1) - 1)
    def _():
        unwrap_band(band, live, half, width, window, least)
        own_ref[0] = band[:half, :width].astype(B16)
        next_ref[0] = band[half:, :width].astype(B16)

    @pl.when(jnp.logical_and(page == pl.num_programs(0) - 1, quad == pl.num_programs(1) - 1))
    def _():
        dwa_ref[:, 3 * model :] = dwp[...].astype(B16)
        for part in range(3):
            rows = slice(part * model, part * model + model)
            dwa_ref[:, rows] = dwq[rows, :].T.astype(B16)


def attn_backward(live, gf, x, n1, qkv, probs, att, wproj, wqkv, vecs, shape, heads, least):
    pages, window, width, model = shape
    half = window // 2
    quads = width // window // QUAD
    slots = window * window
    once = pl.Buffered(1)
    whole = lambda a: pl.BlockSpec(a.shape, lambda p, j: (0,) * a.ndim, pipeline_mode=once)
    held = lambda s: pl.BlockSpec(s, lambda p, j: (0,) * len(s), pipeline_mode=once)
    at = lambda p, j: p * quads + j
    pairs = heads // 2
    return pl.pallas_call(
        functools.partial(attn_backward_kernel, (window, half, width, model, heads, least)),
        grid=(pages, quads),
        in_specs=[
            pl.BlockSpec(memory_space=pltpu.SMEM),
            pl.BlockSpec((QUAD * slots, model), lambda p, j: (at(p, j), 0)),
            pl.BlockSpec((QUAD * slots, model), lambda p, j: (at(p, j), 0)),
            pl.BlockSpec((QUAD * SLOT, model), lambda p, j: (at(p, j), 0)),
            pl.BlockSpec((3 * model, QUAD * SLOT), lambda p, j: (0, at(p, j))),
            pl.BlockSpec((QUAD, pairs, SLOT, 2 * SLOT), lambda p, j: (at(p, j), 0, 0, 0)),
            pl.BlockSpec((model, QUAD * SLOT), lambda p, j: (0, at(p, j))),
            whole(wproj),
            whole(wqkv),
            whole(vecs),
        ],
        out_specs=[
            held((model, 4 * model)),
            held((3 * model, SLOT)),
            held((pairs, KEYS, 2 * SLOT)),
            held((16, model)),
            pl.BlockSpec((1, half, width, model), lambda p, j: (p, 1, 0, 0)),
            pl.BlockSpec((1, half, width, model), lambda p, j: (p, 0, 0, 0)),
        ],
        out_shape=[
            jax.ShapeDtypeStruct((model, 4 * model), B16),
            jax.ShapeDtypeStruct((3 * model, SLOT), F32),
            jax.ShapeDtypeStruct((pairs, KEYS, 2 * SLOT), F32),
            jax.ShapeDtypeStruct((16, model), F32),
            jax.ShapeDtypeStruct(shape, B16),
            jax.ShapeDtypeStruct((pages, half, width, model), B16),
        ],
        scratch_shapes=[
            pltpu.VMEM((window, width + 8, model), F32),
            pltpu.VMEM((QUAD * SLOT, model), B16),
            pltpu.VMEM((model, QUAD * SLOT), B16),
            pltpu.VMEM((2, pairs, KEYS, 2 * SLOT), F32),
            pltpu.VMEM((3, model, 2 * SLOT), B16),
            pltpu.VMEM((3, model, 2 * SLOT), B16),
            pltpu.VMEM((3, model, 2 * SLOT), B16),
            pltpu.VMEM((2, pairs, 2 * SLOT, SLOT), B16),
            pltpu.VMEM((2, pairs, SLOT, 2 * SLOT), B16),
            pltpu.VMEM((3 * model, QUAD * SLOT), B16),
            pltpu.VMEM((3 * model, model), F32),
            pltpu.VMEM((model, model), F32),
            pltpu.VMEM((QUAD * slots, model), F32),
        ],
        compiler_params=pltpu.CompilerParams(vmem_limit_bytes=VMEM_LIMIT),
    )(live, gf, x, n1, qkv, probs, att, wproj, wqkv, vecs)


def table_sum(off_ref, grad_ref, out_ref):
    heads = grad_ref.shape[0]
    chunks = out_ref.shape[0] // heads
    rows = 128 * chunks
    step = 1024
    names = lax.broadcasted_iota(jnp.int32, (rows, step), 0)
    total = jnp.zeros((3 * heads, rows), F32)
    for i in range(off_ref.shape[1] // step):
        at = slice(step * i, step * i + step)
        hot = jnp.where(names == off_ref[:, at], 1.0, 0.0).astype(B16)
        value = grad_ref[:, at]
        high = value.astype(B16)
        rest = value - high.astype(F32)
        middle = rest.astype(B16)
        low = (rest - middle.astype(F32)).astype(B16)
        total += dot(jnp.concatenate([high, middle, low], axis=0), hot, "NT")
    total = total[:heads] + total[heads : 2 * heads] + total[2 * heads :]
    for c in range(chunks):
        out_ref[heads * c : heads * c + heads, :] = total[:, 128 * c : 128 * c + 128]


def sums_kernel(
    peers,
    ga_ref,
    gb_ref,
    gc_ref,
    small_ref,
    mixed_ref,
    patch_ref,
    off_ref,
    dscore_ref,
    outa_ref,
    outb_ref,
    outc_ref,
    small_out_ref,
    mixed_out_ref,
    patch_out_ref,
    own1,
    rec1,
    s1,
    rec2,
    s2,
    rec3,
    s3,
    rec4,
    small_all,
    small1,
    small2,
    small2s,
    small3,
    small3s,
    local,
    send1,
    recv1,
    send2,
    recv2,
    send3,
    recv3,
    send4,
    recv4,
    tiny_send,
    tiny_recv,
    halo_send,
    halo_recv,
):
    pages, chips, table_at, heads = peers
    grads = (ga_ref, gb_ref, gc_ref)
    outs = (outa_ref, outb_ref, outc_ref)
    page, row = lax.axis_index("page"), lax.axis_index("rows")
    chip, core = row // 2, row % 2
    other = 2 * chip + 1 - core
    share, cols = outa_ref.shape
    piece_cols = cols // pages

    def page_peer(d):
        return lax.rem(page + d, pages)

    def chip_peer(d):
        return lax.rem(chip + d, chips)

    barrier = pltpu.get_barrier_semaphore()
    pl.semaphore_signal(barrier, inc=1, device_id={"rows": other}, device_id_type=MESH)
    for d in range(1, pages):
        pl.semaphore_signal(barrier, inc=1, device_id={"page": page_peer(d)}, device_id_type=MESH)
    for d in range(1, chips):
        pl.semaphore_signal(
            barrier, inc=1, device_id={"rows": 2 * chip_peer(d) + core}, device_id_type=MESH
        )
    behind, ahead = lax.rem(row + 2 * chips - 1, 2 * chips), lax.rem(row + 1, 2 * chips)
    for neighbour in (behind, ahead):
        pl.semaphore_signal(barrier, inc=1, device_id={"rows": neighbour}, device_id_type=MESH)
    pl.semaphore_wait(barrier, pages + chips + 1)

    def rows_of(ref, z, c):
        return ref.at[pl.ds(pl.multiple_of((2 * z + c) * share, 16), share), :]

    started = {}

    def phase_one(m):
        copies = []
        for z in range(chips):
            copy = remote(
                rows_of(grads[m], z, 1 - core),
                rec1.at[m, z],
                send1.at[m, z],
                recv1.at[m, z],
                {"rows": other},
            )
            copy.start()
            mine = pltpu.make_async_copy(rows_of(grads[m], z, core), own1.at[m, z], local.at[m, z])
            mine.start()
            copies += [copy, mine]
        started[1, m] = copies

    def phase_two(m):
        for copy in started[1, m]:
            copy.wait()
        for q in range(pages):
            at = slice(piece_cols * q, piece_cols * q + piece_cols)
            total = own1[m, :, :, at].astype(F32) + rec1[m, :, :, at].astype(F32)
            s1[m, q] = total.astype(B16)
        copies = []
        for d in range(1, pages):
            copy = remote(
                s1.at[m, page_peer(d)],
                rec2.at[m, page],
                send2.at[m, d],
                recv2.at[m, d],
                {"page": page_peer(d)},
            )
            copy.start()
            copies.append(copy)
        rec2[m, page] = s1[m, page]
        started[2, m] = copies

    def phase_three(m):
        for copy in started[2, m]:
            copy.wait()
        total = rec2[m, 0].astype(F32)
        for q in range(1, pages):
            total = total + rec2[m, q].astype(F32)
        s2[m] = total.astype(B16)
        copies = []
        for d in range(1, chips):
            copy = remote(
                s2.at[m, chip_peer(d)],
                rec3.at[m, chip],
                send3.at[m, d],
                recv3.at[m, d],
                {"rows": 2 * chip_peer(d) + core},
            )
            copy.start()
            copies.append(copy)
        rec3[m, chip] = s2[m, chip]
        started[3, m] = copies

    def phase_four(m):
        for copy in started[3, m]:
            copy.wait()
        total = rec3[m, 0].astype(F32)
        for z in range(1, chips):
            total = total + rec3[m, z].astype(F32)
        s3[m] = total.astype(B16)
        copies = []
        for d in range(1, pages):
            copy = remote(
                s3.at[m], rec4.at[m, page], send4.at[m, d], recv4.at[m, d], {"page": page_peer(d)}
            )
            copy.start()
            copies.append(copy)
        rec4[m, page] = s3[m]
        started[4, m] = copies

    def finish(m):
        for copy in started[4, m]:
            copy.wait()
        for q in range(pages):
            outs[m][:, piece_cols * q : piece_cols * q + piece_cols] = rec4[m, q].astype(F32)

    count = len(grads)
    for m in range(count):
        phase_one(m)
    halos = [
        remote(mixed_ref, mixed_out_ref, halo_send.at[0], halo_recv.at[0], {"rows": ahead}),
        remote(patch_ref, patch_out_ref, halo_send.at[1], halo_recv.at[1], {"rows": ahead}),
    ]
    for copy in halos:
        copy.start()
    phase_two(0)
    small_all[...] = small_ref[...]
    table_sum(off_ref, dscore_ref, small_all.at[pl.ds(table_at, small_all.shape[0] - table_at), :])
    tiny = remote(small_all, small1, tiny_send.at[0], tiny_recv.at[0], {"rows": other})
    tiny.start()
    for m in range(1, count):
        phase_two(m)
    tiny.wait()
    small2s[...] = small_all[...] + small1[...]
    small2[page] = small2s[...]
    tinies = []
    for d in range(1, pages):
        copy = remote(small2s, small2.at[page], tiny_send.at[d], tiny_recv.at[d], {"page": page_peer(d)})
        copy.start()
        tinies.append(copy)
    for m in range(count):
        phase_three(m)
    for copy in tinies:
        copy.wait()
    total = small2[0]
    for q in range(1, pages):
        total = total + small2[q]
    small3s[...] = total
    small3[chip] = total
    tinies = []
    for d in range(1, chips):
        copy = remote(
            small3s,
            small3.at[chip],
            tiny_send.at[pages + d],
            tiny_recv.at[pages + d],
            {"rows": 2 * chip_peer(d) + core},
        )
        copy.start()
        tinies.append(copy)
    for m in range(count):
        phase_four(m)
    for copy in tinies:
        copy.wait()
    total = small3[0]
    for z in range(1, chips):
        total = total + small3[z]
    small_out_ref[...] = total
    for m in range(count):
        finish(m)
    for copy in halos:
        copy.wait()


def sums(grads, small, mixed, patch, off, dscore, table_at, pages, rows):
    chips = rows // 2
    model, cols = grads[0].shape
    share, piece_cols = model // rows, cols // pages
    n = len(grads)
    vmem = pl.BlockSpec(memory_space=pltpu.VMEM)
    dma = pltpu.SemaphoreType.DMA
    return pl.pallas_call(
        functools.partial(sums_kernel, (pages, chips, table_at, dscore.shape[0])),
        in_specs=[pl.BlockSpec(memory_space=pl.ANY)] * n
        + [vmem]
        + [pl.BlockSpec(memory_space=pl.ANY)] * 2
        + [vmem] * 2,
        out_specs=[vmem] * (n + 1) + [pl.BlockSpec(memory_space=pl.ANY)] * 2,
        out_shape=[jax.ShapeDtypeStruct((share, cols), F32)] * n
        + [jax.ShapeDtypeStruct(a.shape, a.dtype) for a in (small, mixed, patch)],
        scratch_shapes=[
            pltpu.VMEM((n, chips, share, cols), B16),
            pltpu.VMEM((n, chips, share, cols), B16),
            pltpu.VMEM((n, pages, chips, share, piece_cols), B16),
            pltpu.VMEM((n, pages, chips, share, piece_cols), B16),
            pltpu.VMEM((n, chips, share, piece_cols), B16),
            pltpu.VMEM((n, chips, share, piece_cols), B16),
            pltpu.VMEM((n, share, piece_cols), B16),
            pltpu.VMEM((n, pages, share, piece_cols), B16),
            pltpu.VMEM(small.shape, F32),
            pltpu.VMEM(small.shape, F32),
            pltpu.VMEM((pages,) + small.shape, F32),
            pltpu.VMEM(small.shape, F32),
            pltpu.VMEM((chips,) + small.shape, F32),
            pltpu.VMEM(small.shape, F32),
            dma((n, chips)),
            dma((n, chips)),
            dma((n, chips)),
            dma((n, pages)),
            dma((n, pages)),
            dma((n, chips)),
            dma((n, chips)),
            dma((n, pages)),
            dma((n, pages)),
            dma((pages + chips,)),
            dma((pages + chips,)),
            dma((2,)),
            dma((2,)),
        ],
        compiler_params=pltpu.CompilerParams(
            vmem_limit_bytes=VMEM_LIMIT, collective_id=0, has_side_effects=True
        ),
    )(*grads, small, mixed, patch, off, dscore)


def adam_update(master, first, second, grad):
    moment = BETA_ONE * first + (1.0 - BETA_ONE) * grad
    square = BETA_TWO * second + (1.0 - BETA_TWO) * grad * grad
    fix_one = 1.0 - BETA_ONE**STEP
    fix_two = 1.0 - BETA_TWO**STEP
    fresh = master - LEARN_RATE * (
        moment / fix_one / (jnp.sqrt(square / fix_two) + ADAM_EPS) + WEIGHT_DECAY * master
    )
    return (fresh, moment, square)


def shards(
    patches,
    out_grad,
    page_windows,
    region_ids,
    offset_index,
    weights_in,
    weights_out,
    norm_gains,
    biases,
    bias_table,
    master_in,
    master_out,
    first_in,
    second_in,
    first_out,
    second_out,
    first_small,
    second_small,
):
    pages, window, width, model = patches.shape
    half = window // 2
    count = width // window
    least = (count + 1) // 2
    slots = window * window
    table_rows, heads = bias_table.shape
    hidden = weights_out.shape[0]

    labels = region_ids.reshape(pages, window, count, window).transpose(0, 2, 1, 3)
    labels = labels.reshape(pages * count // QUAD, QUAD, slots).astype(F32)
    labels = jnp.pad(labels, ((0, 0), (0, 8 - QUAD), (0, SLOT - slots)), constant_values=-1.0)
    off = offset_index.T
    off_gather = jnp.pad(off, ((0, KEYS - slots), (0, SLOT - slots)))
    off_scatter = jnp.pad(off, ((0, KEYS - slots), (0, SLOT - slots)), constant_values=-1).reshape(1, -1)
    table_lanes = -(-table_rows // 128) * 128
    tab = jnp.pad(bias_table.T * LOG2E, ((0, 0), (0, table_lanes - table_rows)))
    wqkv = weights_in[:, : 3 * model].T
    wproj = weights_in[:, 3 * model : 4 * model]
    bias_qkv = jnp.concatenate(
        [biases[model : 2 * model], jnp.zeros((model,), F32), biases[2 * model : 3 * model]]
    )[:, None]
    zero = jnp.zeros((model,), F32)
    vec_one = jnp.stack(
        [
            norm_gains[0],
            biases[:model],
            biases[3 * model : 4 * model],
            norm_gains[1],
            biases[4 * model : 5 * model],
            zero,
            zero,
            zero,
        ]
    )
    vec_two = jnp.stack([norm_gains[1], biases[5 * model : 6 * model]] + [zero] * 6)

    x, n1, qkv, probs, att, first, n2, below_grad = attn_forward(
        page_windows, patches, out_grad, labels, off_gather, tab, wqkv, bias_qkv, wproj, vec_one, least
    )
    dwup, dwout, dbup, gf, mixed_own, mixed_next, sums_two = mlp(
        page_windows, out_grad, below_grad, n2, first, weights_in, weights_out,
        biases[None, 6 * model :], vec_two, least, master_in.shape[0],
    )
    dwa, dbqkv, dscore, sums_one, patch_own, patch_next = attn_backward(
        page_windows, gf, x, n1, qkv, probs, att, wproj, wqkv, vec_one, patches.shape, heads, least
    )
    dscore = dscore.reshape(heads // 2, KEYS, 2, SLOT).transpose(0, 2, 1, 3).reshape(heads, KEYS * SLOT)
    sums_one = sums_one.reshape(2, 8, model).sum(1)
    sums_two = sums_two.reshape(4, 8, model).sum(1)
    dbqkv = dbqkv.sum(1)
    grad_small = jnp.concatenate(
        [
            sums_one[0],
            sums_two[0],
            sums_one[1],
            dbqkv[:model],
            dbqkv[2 * model :],
            sums_two[3],
            sums_two[1],
            sums_two[2],
            dbup.reshape(-1),
            jnp.zeros((table_lanes * heads,), F32),
        ]
    ).reshape(-1, 128)
    table_at = grad_small.shape[0] - table_lanes * heads // 128
    total_a, total_up, total_out, total_small, above, above_grad = sums(
        [dwa, dwup, dwout],
        grad_small,
        mixed_next,
        patch_next,
        off_scatter,
        dscore,
        table_at,
        lax.axis_size("page"),
        lax.axis_size("rows"),
    )
    mixed = lax.dynamic_update_slice(mixed_own, above, (0, 0, 0, 0))
    patch_grad = lax.dynamic_update_slice(patch_own, above_grad, (0, 0, 0, 0))
    total_table = total_small[table_at:].reshape(table_lanes // 128, heads, 128).transpose(0, 2, 1)
    total_table = total_table.reshape(table_lanes, heads)[:table_rows]
    total_small = jnp.concatenate([total_small[:table_at].reshape(-1), total_table.reshape(-1)])
    part_in = jnp.concatenate([total_a, total_up], axis=1)
    ratio = hidden // model
    total_out = total_out.reshape(-1, ratio, model).transpose(1, 0, 2).reshape(-1, model)
    small_master = jnp.concatenate([norm_gains.reshape(-1), biases, bias_table.reshape(-1)])
    new_in, moment_in, square_in = adam_update(master_in, first_in, second_in, part_in)
    new_out, moment_out, square_out = adam_update(master_out, first_out, second_out, total_out)
    new_small, moment_small, square_small = adam_update(
        small_master, first_small, second_small, total_small
    )
    return (
        mixed,
        patch_grad,
        new_in,
        moment_in,
        square_in,
        new_out,
        moment_out,
        square_out,
        new_small,
        moment_small,
        square_small,
    )


def solution(mesh):
    return jax.shard_map(
        shards,
        mesh=mesh,
        in_specs=(
            P("page", "rows", None, None),
            P("page", "rows", None, None),
            P("page"),
            P("page", "rows", None),
            P(),
            P(),
            P(),
            P(),
            P(),
            P(),
            P("rows", None),
            P("rows", None),
            P("rows", None),
            P("rows", None),
            P("rows", None),
            P("rows", None),
            P(),
            P(),
        ),
        out_specs=(
            P("page", "rows", None, None),
            P("page", "rows", None, None),
            P("rows", None),
            P("rows", None),
            P("rows", None),
            P("rows", None),
            P("rows", None),
            P("rows", None),
            P(),
            P(),
            P(),
        ),
        check_vma=False,
    )
```

time: 829 us -> 227 us (0.27)
  other arithmetic: 209 us -> 5.35 us
  matrix products: 202 us -> 0 us
  Pallas kernels: 0 us -> 199 us
  local copies, waits for them, and re-layouts: 216 us -> 21.2 us
  waiting for transfers between devices: 131 us -> 0 us
  blocking collectives: 43.2 us -> 0 us
  between operations: 15.2 us -> 1.15 us
    dot_general x19 -> x0, matrix products: 202 us -> none  [the longest x1 23 us: shards(): jnp.einsum('gtd,fd->gtf', grad_mlp, weights_out, preferred_element_type=f32)]
    pallas_call x0 -> x4, Pallas kernels: none -> 199 us  [the longest x1 65 us: sums(): pl.pallas_call(functools.partial(sums_kernel, (pages, chips, table_at, ds...]
    psum x1 -> x0, waiting for transfers between devices: 131 us -> none  [shards(): lax.psum((grad_in, grad_w_out, grad_small), ('page', 'rows'))]
    convert_element_type x12 -> x3, local copies, waits for them, and re-layouts: 88.1 us -> 0.3 us  [shards(): labels = labels.reshape(pages * count // QUAD, QUAD, slots).astype(F32)]
    reduce_sum x11 -> x3, other arithmetic: 82.4 us -> 0.32 us  [the longest x1 0.27 us: shards(): dbqkv = dbqkv.sum(1)]
    convert_element_type x6 -> x1, other arithmetic: 72.3 us -> 0.01 us  [shards(): labels = labels.reshape(pages * count // QUAD, QUAD, slots).astype(F32)]
    gather x11 -> x0, local copies, waits for them, and re-layouts: 60.4 us -> none  [the longest x8 32.9 us: pick_columns(): return jax.vmap(lambda page, cols: page[:, cols])(field, table)]
    psum x1 -> x0, blocking collectives: 43.2 us -> none  [shards(): lax.psum((grad_in, grad_w_out, grad_small), ('page', 'rows'))]
  transfers between devices with their start and end apart: 5 -> 0, of which waited for: 1 -> 0; matrix products, arithmetic and copies ran while one was open for 20% -> 0% of each run, Pallas kernels for 0% -> 0%
where the time goes in v1:
time: 227 us
  Pallas kernels  199 us (88%)
  local copies, waits for them, and re-layouts  21.2 us (9%)
  other arithmetic  5.35 us (2%)
    pallas_call x1, Pallas kernels, sums(): pl.pallas_call(functools.partial(sums_kernel, (pages, chips, table_at, ds...  65 us
    pallas_call x1, Pallas kernels, mlp(): pl.pallas_call(functools.partial(mlp_kernel, (window, half, width, model,...  56.9 us
    pallas_call x1, Pallas kernels, attn_forward(): pl.pallas_call(functools.partial(attn_forward_kernel, (window, half, widt...  41.1 us
    pallas_call x1, Pallas kernels, attn_backward(): pl.pallas_call(functools.partial(attn_backward_kernel, (window, half, wid...  36.1 us
    unnamed x68, local copies, waits for them, and re-layouts  8.43 us

profile of v1, /device:TPU:0, one launch (start us, length us, event | category | flops | bytes accessed | tf_op | source)
XLA Modules:
  0.0 226.8 jit_solution(11186920433741683468)
XLA Ops:
  0.7 0.9 fusion.9
  1.5 0.8 fusion.12
  2.3 0.6 stack.24.vec_ref
  3.0 1.2 broadcast_in_dim.16.bqkv_ref
  4.1 1.6 copy.43
  5.8 1.9 slice.70.wproj_ref
  7.7 0.7 fusion.8
  8.7 0.6 pad.15.label_ref
  9.3 0.6 pad.17.tab_ref
  10.0 41.1 %shard_map.257 = (bf16[2400,512]{1,0:T(8,128)(2,1)}, bf16[3072,512]{1,0:T(8,128)(2,1)}, bf16[1536,3072]{1,0:T(8,128)(2,1)}, bf16[24,8,128,256]{3,2,1,0:T(8,128)(...) custom-call(s32[2]{0:T(128)} %live_ref.5, ...), custom_call_target="tpu_custom_call" | custom-call | tf_op jit(solution)/shard_map/pallas_call | solution.py:273
  51.2 0.7 maximum_maximum_fusion.vec_ref
  51.9 0.6 slice.76
  52.5 56.9 %shard_map.258 = (bf16[512,2048]{1,0:T(8,128)(2,1)}, bf16[512,2048]{1,0:T(8,128)(2,1)}, f32[1,2048]{1,0:T(1,128)}, f32[2400,512]{1,0:T(8,128)}, bf16[2,10,120,51...) custom-call(s32[2]{0:T(128)} %live_ref.5, bf16[2,10,120,512]{3,2,1,0:T(8,128)(2,1)} %low_ref.3, ...), custom_call_target="tpu_custom_call" | custom-call | tf_op jit(solution)/shard_map/pallas_call | solution.py:468
  109.4 36.1 %shard_map.259 = (bf16[512,2048]{1,0:T(8,128)(2,1)}, f32[1536,128]{1,0:T(8,128)}, f32[8,104,256]{2,1,0:T(8,128)}, f32[16,512]{1,0:T(8,128)}, bf16[2,10,120,512]{...) custom-call(s32[2]{0:T(128)} %live_ref.5, f32[2400,512]{1,0:T(8,128)} %get-tuple-element.42.gf_ref, ...), custom_call_target="tpu_custom_call" | custom-call | tf_op jit(solution)/shard_map/pallas_call | solution.py:664
  145.5 1.3 copy_bitcast_fusion.1
  146.8 1.1 copy.51
  148.0 0.3 reduce_sum.29
  148.4 0.6 copy-done.14
  149.0 65.0 %shard_map.260 = (f32[64,2048]{1,0:T(8,128)}, f32[64,2048]{1,0:T(8,128)}, f32[64,2048]{1,0:T(8,128)}, f32[96,128]{1,0:T(8,128)}, bf16[2,5,120,512]{3,2,1,0:T(8,128)(2,1)}, /*index=5*/bf16[2,5,120,512]{3,2,1,0:T(8,128)(2,1)}) custom-call(bf16[512,2048]{1,0:T(8,128)(2,1)} %get-tuple-element.48.ga_ref, bf16[512,2048]{1,0:T(8,128)(2,1)} %get-tuple-element.49.gb_ref, ...), custom_call_target="tpu_custom_call" | custom-call | tf_op jit(solution)/shard_map/pallas_call | solution.py:958
  214.1 0.9 slice_bitcast_fusion
  215.6 0.7 multiply_subtract_fusion.2
  216.3 1.1 constant_dynamic-update-slice_fusion.2
  217.4 1.2 constant_dynamic-update-slice_fusion.1
  218.7 2.2 multiply_subtract_fusion
  220.9 0.3 copy-done.1
  221.2 1.1 copy-done.21
  222.4 0.2 constant_dynamic-update-slice_fusion.14
  222.6 1.4 copy-done.22
  224.0 0.8 copy-done.24
  224.8 0.3 reshape.78
  225.2 0.2 copy.39
  225.4 1.4 multiply_subtract_fusion.1
  (84 shorter events, 1.2 us)
Async XLA Ops:
  0.6 3.5 %slice-start = ((bf16[512,4096]{1,0:T(8,128)(2,1)}), bf16[512,1536]{1,0:T(8,128)(2,1)S(1)}, s32[]{:S(2)}) async-start(bf16[512,4096]{1,0:T(8,128)(2,1)} %wup_ref.1), calls=%async_computation | async-start | bytes 3145728 | tf_op jit(solution)/shard_map/slice | solution.py:1049
  4.1 3.5 %copy-start.13 = (s32[100,100]{1,0:T(8,128)S(1)}, s32[100,100]{1,0:T(8,128)}, u32[]{:S(2)}) copy-start(s32[100,100]{1,0:T(8,128)} %param.22) | copy-start | bytes 120004
  4.1 4.3 %copy-start.19 = (s32[2,10,120]{2,0,1:T(2,128)S(1)}, s32[2,10,120]{2,0,1:T(2,128)}, u32[]{:S(2)}) copy-start(s32[2,10,120]{2,0,1:T(2,128)} %param.21) | copy-start | bytes 28804
  4.1 5.2 %copy-start.10 = (f32[361,16]{0,1:T(8,128)S(1)}, f32[361,16]{0,1:T(8,128)}, u32[]{:S(2)}) copy-start(f32[361,16]{0,1:T(8,128)} %param.27) | copy-start | bytes 69316
  10.0 41.9 %copy-start.11 = (f32[5120]{0:T(1024)S(1)}, f32[5120]{0:T(1024)}, u32[]{:S(2)}) copy-start(f32[5120]{0:T(1024)} %param.26) | copy-start | bytes 61444
  145.5 2.4 %copy-start.17 = (f32[16,512]{1,0:T(8,128)S(1)}, f32[16,512]{1,0:T(8,128)}, u32[]{:S(2)}) copy-start(f32[16,512]{1,0:T(8,128)} %get-tuple-element.51) | copy-start | bytes 98308
  145.5 2.5 %copy-start.12 = (f32[32,512]{1,0:T(8,128)S(1)}, f32[32,512]{1,0:T(8,128)}, u32[]{:S(2)}) copy-start(f32[32,512]{1,0:T(8,128)} %get-tuple-element.52) | copy-start | bytes 196612
  145.5 2.5 %copy-start.5 = (f32[1536,128]{1,0:T(8,128)S(1)}, f32[1536,128]{1,0:T(8,128)}, u32[]{:S(2)}) copy-start(f32[1536,128]{1,0:T(8,128)} %get-tuple-element.53) | copy-start | bytes 2359300
  145.5 2.9 %copy-start.20 = (f32[1,2048]{1,0:T(1,128)S(1)}, f32[1,2048]{1,0:T(1,128)}, u32[]{:S(2)}) copy-start(f32[1,2048]{1,0:T(1,128)} %get-tuple-element.54) | copy-start | bytes 24580
  148.4 0.6 copy-start.14
  149.0 66.5 %copy-start.18 = (f32[2,512]{1,0:T(2,128)S(1)}, f32[2,512]{1,0:T(2,128)}, u32[]{:S(2)}) copy-start(f32[2,512]{1,0:T(2,128)} %param.25) | copy-start | bytes 12292
  149.0 66.5 %copy-start.15 = (f32[11920]{0:T(1024)S(1)}, f32[11920]{0:T(1024)}, u32[]{:S(2)}) copy-start(f32[11920]{0:T(1024)} %param.34) | copy-start | bytes 143044
  149.0 66.6 %copy-start.16 = (f32[11920]{0:T(1024)S(1)}, f32[11920]{0:T(1024)}, u32[]{:S(2)}) copy-start(f32[11920]{0:T(1024)} %param.35) | copy-start | bytes 143044
  214.1 4.6 %copy-start.2 = (f32[64,4096]{1,0:T(8,128)S(1)}, f32[64,4096]{1,0:T(8,128)}, u32[]{:S(2)}) copy-start(f32[64,4096]{1,0:T(8,128)} %param.28) | copy-start | bytes 3145732
  214.1 4.6 %copy-start.3 = (f32[64,4096]{1,0:T(8,128)S(1)}, f32[64,4096]{1,0:T(8,128)}, u32[]{:S(2)}) copy-start(f32[64,4096]{1,0:T(8,128)} %param.30) | copy-start | bytes 3145732
  214.1 4.5 %copy-start.4 = (f32[64,4096]{1,0:T(8,128)S(1)}, f32[64,4096]{1,0:T(8,128)}, u32[]{:S(2)}) copy-start(f32[64,4096]{1,0:T(8,128)} %param.31) | copy-start | bytes 3145732
  217.4 3.5 %copy-start.23 = (bf16[2,10,120,512]{3,2,1,0:T(8,128)(2,1)S(1)}, bf16[2,10,120,512]{3,2,1,0:T(8,128)(2,1)}, u32[]{:S(2)}) copy-start(bf16[2,10,120,512]{3,2,1,0:T(8,128)(2,1)} %get-tuple-element.59) | copy-start | bytes 7372804
  218.6 2.3 %copy-start = (bf16[2,5,120,512]{3,2,1,0:T(8,128)(2,1)S(1)}, bf16[2,5,120,512]{3,2,1,0:T(8,128)(2,1)}, u32[]{:S(2)}) copy-start(bf16[2,5,120,512]{3,2,1,0:T(8,128)(2,1)} %get-tuple-element.58) | copy-start | bytes 3686404
  218.6 2.5 %copy-start.1 = (bf16[2,5,120,512]{3,2,1,0:T(8,128)(2,1)S(1)}, bf16[2,5,120,512]{3,2,1,0:T(8,128)(2,1)}, u32[]{:S(2)}) copy-start(bf16[2,5,120,512]{3,2,1,0:T(8,128)(2,1)} %get-tuple-element.60) | copy-start | bytes 3686404
  218.7 3.7 %copy-start.21 = (bf16[2,10,120,512]{3,2,1,0:T(8,128)(2,1)S(1)}, bf16[2,10,120,512]{3,2,1,0:T(8,128)(2,1)}, u32[]{:S(2)}) copy-start(bf16[2,10,120,512]{3,2,1,0:T(8,128)(2,1)} %get-tuple-element.41) | copy-start | bytes 7372804
  222.3 2.5 %copy-start.9 = (f32[64,2048]{1,0:T(8,128)S(1)}, f32[64,2048]{1,0:T(8,128)}, u32[]{:S(2)}) copy-start(f32[64,2048]{1,0:T(8,128)} %get-tuple-element.63) | copy-start | bytes 1572868
  222.3 3.0 %copy-start.6 = (f32[256,512]{1,0:T(8,128)S(1)}, f32[256,512]{1,0:T(8,128)}, u32[]{:S(2)}) copy-start(f32[256,512]{1,0:T(8,128)} %param.29) | copy-start | bytes 1572868
  222.3 3.0 %copy-start.7 = (f32[256,512]{1,0:T(8,128)S(1)}, f32[256,512]{1,0:T(8,128)}, u32[]{:S(2)}) copy-start(f32[256,512]{1,0:T(8,128)} %param.32) | copy-start | bytes 1572868
  222.3 3.0 %copy-start.8 = (f32[256,512]{1,0:T(8,128)S(1)}, f32[256,512]{1,0:T(8,128)}, u32[]{:S(2)}) copy-start(f32[256,512]{1,0:T(8,128)} %param.33) | copy-start | bytes 1572868
  222.6 1.4 copy-start.22
  222.6 2.2 copy-start.24

commit v2 on v1

--- a/solution.py
+++ b/solution.py
@@ -50,13 +50,14 @@
 
 
 def unwrap_band(band, live, half, width, window, least):
+    front = band[:, :half]
     for count in range(least, width // window + 1):
-
-        @pl.when(live == count)
-        def _():
-            edge = count * window
-            band[:, :half] = band[:, edge : edge + half]
-            band[:, edge:] = jnp.zeros((window, band.shape[1] - edge, band.shape[2]), F32)
+        at = slice(count * window, count * window + half)
+        front = jnp.where(live == count, band[:, at], front)
+    band[:, :half] = front
+    edge = least * window // 8 * 8
+    columns = lax.broadcasted_iota(jnp.int32, (window, width - edge, band.shape[2]), 1) + edge
+    band[:, edge:width] = jnp.where(columns < live * window, band[:, edge:width], 0.0)
 
 
 def piece(band, row, base, place, window, half):
@@ -509,9 +510,214 @@
     )(live, out_grad, halo, n2, first, weights_in, weights_out, bup, vecs)
 
 
+def table_sum(off_ref, grad_ref, out_ref, at, heads, chunks):
+    rows = 128 * chunks
+    keys = grad_ref.shape[1]
+    names = lax.broadcasted_iota(jnp.int32, (rows, SLOT), 0)
+    total = jnp.zeros((3 * heads, rows), F32)
+    grad = jnp.swapaxes(grad_ref[...], 0, 1)
+    for k in range(0, keys, 8):
+        hot = jnp.concatenate(
+            [jnp.where(names == off_ref[i : i + 1, :], 1.0, 0.0).astype(B16) for i in range(k, k + 8)], axis=1
+        )
+        value = jnp.concatenate([grad[i] for i in range(k, k + 8)], axis=1)
+        high = value.astype(B16)
+        rest = value - high.astype(F32)
+        middle = rest.astype(B16)
+        low = (rest - middle.astype(F32)).astype(B16)
+        total += dot(jnp.concatenate([high, middle, low], axis=0), hot, "NT")
+    total = total[:heads] + total[heads : 2 * heads] + total[2 * heads :]
+    for c in range(chunks):
+        out_ref[at + heads * c : at + heads * c + heads, :] = total[:, 128 * c : 128 * c + 128]
+
+
+class Exchange:
+    def __init__(self, pages, chips, share, bufs, sems):
+        self.pages, self.chips, self.share = pages, chips, share
+        self.rec1, self.s1, self.rec2, self.s2, self.rec3, self.s3, self.rec4 = bufs
+        self.send1, self.recv1, self.send2, self.recv2, self.send3, self.recv3, self.send4, self.recv4 = sems
+        self.page, row = lax.axis_index("page"), lax.axis_index("rows")
+        self.chip, self.core = row // 2, row % 2
+        self.other = 2 * self.chip + 1 - self.core
+        self.cols = self.s3.shape[-1]
+
+    def page_peer(self, d):
+        return lax.rem(self.page + d, self.pages)
+
+    def chip_peer(self, d):
+        return lax.rem(self.chip + d, self.chips)
+
+    def along(self, d):
+        return {"rows": 2 * self.chip_peer(d) + self.core}
+
+    def rows_of(self, ref, z, c):
+        return ref.at[pl.ds(pl.multiple_of((2 * z + c) * self.share, 16), self.share), :]
+
+    def one(self, m, grad):
+        return [
+            remote(
+                self.rows_of(grad, z, 1 - self.core),
+                self.rec1.at[m, z],
+                self.send1.at[m, z],
+                self.recv1.at[m, z],
+                {"rows": self.other},
+            )
+            for z in range(self.chips)
+        ]
+
+    def two(self, m):
+        return [
+            remote(
+                self.s1.at[m, self.page_peer(d)],
+                self.rec2.at[m, self.page],
+                self.send2.at[m, d],
+                self.recv2.at[m, d],
+                {"page": self.page_peer(d)},
+            )
+            for d in range(1, self.pages)
+        ]
+
+    def three(self, m):
+        return [
+            remote(
+                self.s2.at[m, self.chip_peer(d)],
+                self.rec3.at[m, self.chip],
+                self.send3.at[m, d],
+                self.recv3.at[m, d],
+                self.along(d),
+            )
+            for d in range(1, self.chips)
+        ]
+
+    def four(self, m):
+        return [
+            remote(
+                self.s3.at[m],
+                self.rec4.at[m, self.page],
+                self.send4.at[m, d],
+                self.recv4.at[m, d],
+                {"page": self.page_peer(d)},
+            )
+            for d in range(1, self.pages)
+        ]
+
+    def start_one(self, m, grad):
+        start(self.one(m, grad))
+
+    def start_two(self, m, grad, own):
+        wait(self.one(m, grad))
+        for q in range(self.pages):
+            at = slice(self.cols * q, self.cols * q + self.cols)
+            for z in range(self.chips):
+                self.s1[m, q, z] = (own(z)[:, at].astype(F32) + self.rec1[m, z, :, at].astype(F32)).astype(B16)
+        start(self.two(m))
+        self.rec2[m, self.page] = self.s1[m, self.page]
+
+    def start_three(self, m):
+        wait(self.two(m))
+        total = self.rec2[m, 0].astype(F32)
+        for q in range(1, self.pages):
+            total = total + self.rec2[m, q].astype(F32)
+        self.s2[m] = total.astype(B16)
+        start(self.three(m))
+        self.rec3[m, self.chip] = self.s2[m, self.chip]
+
+    def start_four(self, m):
+        wait(self.three(m))
+        total = self.rec3[m, 0].astype(F32)
+        for z in range(1, self.chips):
+            total = total + self.rec3[m, z].astype(F32)
+        self.s3[m] = total.astype(B16)
+        start(self.four(m))
+        self.rec4[m, self.page] = self.s3[m]
+
+    def finish(self, m, out_ref):
+        wait(self.four(m))
+        for q in range(self.pages):
+            out_ref[:, self.cols * q : self.cols * q + self.cols] = self.rec4[m, q]
+
+
+class SmallExchange:
+    def __init__(self, big, bufs, sems):
+        self.big = big
+        self.mine, self.one_in, self.two_out, self.two_in, self.three_out, self.three_in = bufs
+        self.send, self.recv = sems
+
+    def one(self):
+        return [remote(self.mine, self.one_in, self.send.at[0], self.recv.at[0], {"rows": self.big.other})]
+
+    def two(self):
+        big = self.big
+        return [
+            remote(
+                self.two_out,
+                self.two_in.at[big.page],
+                self.send.at[d],
+                self.recv.at[d],
+                {"page": big.page_peer(d)},
+            )
+            for d in range(1, big.pages)
+        ]
+
+    def three(self):
+        big = self.big
+        return [
+            remote(
+                self.three_out,
+                self.three_in.at[big.chip],
+                self.send.at[big.pages + d],
+                self.recv.at[big.pages + d],
+                big.along(d),
+            )
+            for d in range(1, big.chips)
+        ]
+
+    def start_one(self):
+        start(self.one())
+
+    def start_two(self):
+        wait(self.one())
+        total = self.mine[...] + self.one_in[...]
+        self.two_out[...] = total
+        start(self.two())
+        self.two_in[self.big.page] = total
+
+    def start_three(self):
+        wait(self.two())
+        total = self.two_in[0]
+        for q in range(1, self.big.pages):
+            total = total + self.two_in[q]
+        self.three_out[...] = total
+        start(self.three())
+        self.three_in[self.big.chip] = total
+
+    def finish(self, out_ref, at):
+        wait(self.three())
+        total = self.three_in[0]
+        for z in range(1, self.big.chips):
+            total = total + self.three_in[z]
+        out_ref[at : at + total.shape[0], :] = total
+
+
+def start(copies):
+    for copy in copies:
+        copy.start()
+
+
+def wait(copies):
+    for copy in copies:
+        copy.wait()
+
+
+LATE = 8
+
+
 def attn_backward_kernel(
     sizes,
     live_ref,
+    up_ref,
+    out_ref,
+    mixed_ref,
     gf_ref,
     x_ref,
     n1_ref,
@@ -521,12 +727,15 @@
     wproj_ref,
     wqkv_ref,
     vec_ref,
-    dwa_ref,
-    dbqkv_ref,
-    dscore_ref,
-    sums_ref,
+    off_ref,
+    early_ref,
+    suma_ref,
+    sumu_ref,
+    sumo_ref,
+    small_ref,
     own_ref,
-    next_ref,
+    mixed_halo_ref,
+    patch_halo_ref,
     band,
     gbp,
     datt,
@@ -540,32 +749,90 @@
     dwq,
     dwp,
     compact,
+    dscore,
+    dbqkv,
+    sums,
+    dwa,
+    edge,
+    own1,
+    *rest,
 ):
-    window, half, width, model, heads, least = sizes
+    window, half, width, model, heads, least, pages, devices, share = sizes
     slots = window * window
     size_head = model // heads
-    page, quad = pl.program_id(0), pl.program_id(1)
+    sweep, page, quad = pl.program_id(0), pl.program_id(1), pl.program_id(2)
+    quads = pl.num_programs(2)
+    step = page * quads + quad
     live = live_ref[page]
     pairs = heads // 2
     pair = 2 * size_head
-
-    @pl.when(jnp.logical_and(page == 0, quad == 0))
+    big = Exchange(devices[0], devices[1] // 2, share, rest[:7], rest[7:15])
+    early = SmallExchange(big, (rest[15],) + rest[16:21], rest[21:23])
+    late = SmallExchange(big, (rest[23],) + rest[24:29], rest[29:31])
+    local, halo_send, halo_recv = rest[31:]
+    row = lax.axis_index("rows")
+    behind, ahead = lax.rem(row + devices[1] - 1, devices[1]), lax.rem(row + 1, devices[1])
+    matrices = (dwa, up_ref, out_ref)
+
+    def fetch(m):
+        return [
+            pltpu.make_async_copy(
+                big.rows_of(matrices[m], z, big.core), own1.at[m - 1, z], local.at[m - 1, z]
+            )
+            for z in range(big.chips)
+        ]
+
+    def mixed_copy():
+        return remote(mixed_ref, mixed_halo_ref, halo_send.at[0], halo_recv.at[0], {"rows": ahead})
+
+    def patch_copy(p):
+        return remote(
+            edge.at[p], patch_halo_ref.at[p], halo_send.at[1 + p], halo_recv.at[1 + p], {"rows": ahead}
+        )
+
+    def moment(at_sweep, at_step):
+        return jnp.logical_and(sweep == at_sweep, step == at_step)
+
+    @pl.when(moment(0, 0))
     def _():
-        for ref in (bdq, bdk, bdo, stacked, beside, gbp, dwq, dwp, dbqkv_ref, dscore_ref, sums_ref):
+        barrier = pltpu.get_barrier_semaphore()
+        peers = [{"rows": big.other}, {"rows": behind}, {"rows": ahead}]
+        peers += [{"page": big.page_peer(d)} for d in range(1, big.pages)]
+        peers += [big.along(d) for d in range(1, big.chips)]
+        for peer in peers:
+            pl.semaphore_signal(barrier, inc=1, device_id=peer, device_id_type=MESH)
+        pl.semaphore_wait(barrier, len(peers))
+        for m in (1, 2):
+            big.start_one(m, matrices[m])
+            start(fetch(m))
+        mixed_copy().start()
+        for ref in (bdq, bdk, bdo, stacked, beside, gbp, dwq, dwp, dbqkv, dscore, sums):
             ref[...] = jnp.zeros_like(ref)
 
-    for w in range(QUAD):
-        gbp[SLOT * w : SLOT * w + slots, :] = gf_ref[slots * w : slots * w + slots, :].astype(B16)
-    datt[...] = dot(wproj_ref[...], gbp[...], "NT").astype(B16)
-    dwp[...] += dot(att_ref[...], gbp[...])
-
-    @pl.when(quad * QUAD >= live)
+    last = pages * (width // window // QUAD) - 1
+    for m, (at_two, at_three, at_four) in ((1, (1, 3, 4)), (2, (1, 4, 5))):
+
+        @pl.when(moment(0, at_two))
+        def _():
+            wait(fetch(m))
+            big.start_two(m, matrices[m], lambda z: own1.at[m - 1, z])
+
+        @pl.when(moment(0, at_three))
+        def _():
+            big.start_three(m)
+
+        @pl.when(moment(0, at_four))
+        def _():
+            big.start_four(m)
+
+    @pl.when(sweep == 0)
     def _():
-        dqkv[...] = jnp.zeros_like(dqkv)
-
-    @pl.when(quad * QUAD < live)
-    def _():
+        for w in range(QUAD):
+            gbp[SLOT * w : SLOT * w + slots, :] = gf_ref[slots * w : slots * w + slots, :].astype(B16)
+        datt[...] = dot(wproj_ref[...], gbp[...], "NT").astype(B16)
+        dwp[...] += dot(att_ref[...], gbp[...])
         ratio = size_head**-0.5
+        target = dqkv.at[step]
 
         def score(w, g):
             low = pair * g
@@ -584,419 +851,247 @@
             probs = probs_ref[w, g, :KEYS, :].astype(F32)
             term = probs * dprobs[w % 2, g]
             grad = term - probs * jnp.sum(term, axis=0, keepdims=True)
-            dscore_ref[g] += grad
             low_grad = grad.astype(B16)
             beside[w % 2, g, :KEYS, :] = low_grad
             for j in range(2):
-                stacked[w % 2, g, SLOT * j : SLOT * j + KEYS, :] = low_grad[:, SLOT * j : SLOT * j + SLOT]
+                cols = slice(SLOT * j, SLOT * j + SLOT)
+                dscore[2 * g + j] += grad[:, cols]
+                stacked[w % 2, g, SLOT * j : SLOT * j + KEYS, :] = low_grad[:, cols]
 
         def attend(w, g):
             low = pair * g
             lanes = slice(SLOT * w, SLOT * w + SLOT)
             rows = slice(low, low + pair)
             got = dot(bdk[w % 3, rows, :], stacked[w % 2, g]) * ratio
-            dqkv[low : low + pair, lanes] = got.astype(B16)
+            target[low : low + pair, lanes] = got.astype(B16)
             got = dot(bdq[w % 3, rows, :], beside[w % 2, g], "NT") * (1.0 / LOG2E)
-            dqkv[model + low : model + low + pair, lanes] = got.astype(B16)
+            target[model + low : model + low + pair, lanes] = got.astype(B16)
             got = dot(bdo[w % 3, rows, :], probs_ref[w, g], "NT")
-            dqkv[2 * model + low : 2 * model + low + pair, lanes] = got.astype(B16)
-
-        for step in range(QUAD + 2):
+            target[2 * model + low : 2 * model + low + pair, lanes] = got.astype(B16)
+
+        for stage in range(QUAD + 2):
             for g in range(pairs):
-                if step < QUAD:
-                    score(step, g)
-                if 1 <= step <= QUAD:
-                    soften(step - 1, g)
-                if step >= 2:
-                    attend(step - 2, g)
-
-    n1 = n1_ref[...]
-    for part in range(3):
-        rows = slice(part * model, part * model + model)
-        grad = dqkv[rows, :]
-        dwq[rows, :] += dot(grad, n1)
-        wide = grad.astype(F32)
-        both = wide[:, :SLOT]
-        for w in range(1, QUAD):
-            both = both + wide[:, SLOT * w : SLOT * w + SLOT]
-        dbqkv_ref[rows, :] += both
-    dn1 = dot(dqkv[...], wqkv_ref[...], "TN")
-    for w in range(QUAD):
-        compact[slots * w : slots * w + slots, :] = dn1[SLOT * w : SLOT * w + slots, :]
-    grad = compact[...]
-    xhat, spread = norm_stats(x_ref[...].astype(F32))
-    scaled = grad * vec_ref[0:1, :]
-    mean_one = jnp.mean(scaled, axis=-1, keepdims=True)
-    mean_two = jnp.mean(scaled * xhat, axis=-1, keepdims=True)
-    sums_ref[0:8, :] += fold(grad * xhat)
-    sums_ref[8:16, :] += fold(grad)
-    compact[...] = gf_ref[...] + spread * (scaled - mean_one - xhat * mean_two)
-    for w in range(QUAD):
-        for r in range(window):
-            ref, skip = piece(band, r, quad * QUAD * window, w, window, half)
-            at = slots * w + window * r
-            ref[skip : skip + window, :] = compact[at : at + window, :]
-
-    @pl.when(quad == pl.num_programs(1) - 1)
-    def _():
-        unwrap_band(band, live, half, width, window, least)
-        own_ref[0] = band[:half, :width].astype(B16)
-        next_ref[0] = band[half:, :width].astype(B16)
-
-    @pl.when(jnp.logical_and(page == pl.num_programs(0) - 1, quad == pl.num_programs(1) - 1))
-    def _():
-        dwa_ref[:, 3 * model :] = dwp[...].astype(B16)
+                if stage < QUAD:
+                    score(stage, g)
+                if 1 <= stage <= QUAD:
+                    soften(stage - 1, g)
+                if stage >= 2:
+                    attend(stage - 2, g)
+
+        n1 = n1_ref[...]
         for part in range(3):
             rows = slice(part * model, part * model + model)
-            dwa_ref[:, rows] = dwq[rows, :].T.astype(B16)
-
-
-def attn_backward(live, gf, x, n1, qkv, probs, att, wproj, wqkv, vecs, shape, heads, least):
+            grad = dqkv[step, rows, :]
+            dwq[rows, :] += dot(grad, n1)
+            wide = grad.astype(F32)
+            both = wide[:, :SLOT]
+            for w in range(1, QUAD):
+                both = both + wide[:, SLOT * w : SLOT * w + SLOT]
+            dbqkv[rows, :] += both
+
+    @pl.when(moment(1, 0))
+    def _():
+        dwa[:, 3 * model :] = dwp[...].astype(B16)
+        for part in range(3):
+            rows = slice(part * model, part * model + model)
+            dwa[:, rows] = dwq[rows, :].T.astype(B16)
+        big.start_one(0, dwa)
+        early.mine[...] = early_ref[...]
+        lines = model // 128
+        for k, part in enumerate((0, 2)):
+            total = jnp.sum(dbqkv[part * model : part * model + model, :].T, axis=0, keepdims=True)
+            for i in range(lines):
+                early.mine[lines * k + i : lines * k + i + 1, :] = total[:, 128 * i : 128 * i + 128]
+
+    @pl.when(moment(1, 1))
+    def _():
+        big.start_two(0, dwa, lambda z: big.rows_of(dwa, z, big.core))
+
+    @pl.when(moment(1, 2))
+    def _():
+        chunks = -(-(2 * window - 1) ** 2 // 128)
+        table_sum(off_ref, dscore, early.mine, early.mine.shape[0] - heads * chunks, heads, chunks)
+        early.start_one()
+
+    @pl.when(moment(1, 3))
+    def _():
+        early.start_two()
+
+    @pl.when(moment(1, 4))
+    def _():
+        early.start_three()
+
+    @pl.when(sweep == 1)
+    def _():
+        dn1 = dot(dqkv[step], wqkv_ref[...], "TN")
+        for w in range(QUAD):
+            compact[slots * w : slots * w + slots, :] = dn1[SLOT * w : SLOT * w + slots, :]
+        grad = compact[...]
+        xhat, spread = norm_stats(x_ref[...].astype(F32))
+        scaled = grad * vec_ref[0:1, :]
+        mean_one = jnp.mean(scaled, axis=-1, keepdims=True)
+        mean_two = jnp.mean(scaled * xhat, axis=-1, keepdims=True)
+        sums[0:8, :] += fold(grad * xhat)
+        sums[8:16, :] += fold(grad)
+        compact[...] = gf_ref[...] + spread * (scaled - mean_one - xhat * mean_two)
+        for w in range(QUAD):
+            for r in range(window):
+                ref, skip = piece(band, r, quad * QUAD * window, w, window, half)
+                at = slots * w + window * r
+                ref[skip : skip + window, :] = compact[at : at + window, :]
+
+    for p in range(pages):
+
+        @pl.when(jnp.logical_and(sweep == 1, jnp.logical_and(page == p, quad == quads - 1)))
+        def _():
+            unwrap_band(band, live, half, width, window, least)
+            edge[p] = band[half:, :width].astype(B16)
+            patch_copy(p).start()
+            own_ref[0] = band[:half, :width].astype(B16)
+
+    @pl.when(moment(1, last))
+    def _():
+        big.start_three(0)
+        lines = model // 128
+        for k in range(2):
+            total = jnp.sum(sums[8 * k : 8 * k + 8, :], axis=0, keepdims=True)
+            for i in range(lines):
+                late.mine[lines * k + i : lines * k + i + 1, :] = total[:, 128 * i : 128 * i + 128]
+        late.start_one()
+        for m, ref in ((1, sumu_ref), (2, sumo_ref)):
+            big.finish(m, ref)
+        late.start_two()
+        early.finish(small_ref, LATE)
+        big.start_four(0)
+        late.start_three()
+        mixed_copy().wait()
+        late.finish(small_ref, 0)
+        big.finish(0, suma_ref)
+        for p in range(pages):
+            patch_copy(p).wait()
+
+
+def attn_backward(
+    live, dwup, dwout, mixed_next, gf, x, n1, qkv, probs, att, wproj, wqkv, vecs, off, early, shape, heads, least, share
+):
     pages, window, width, model = shape
     half = window // 2
     quads = width // window // QUAD
     slots = window * window
+    pairs = heads // 2
+    devices = (lax.axis_size("page"), lax.axis_size("rows"))
+    chips = devices[1] // 2
+    hidden = dwup.shape[1]
+    cols = hidden // devices[0]
     once = pl.Buffered(1)
-    whole = lambda a: pl.BlockSpec(a.shape, lambda p, j: (0,) * a.ndim, pipeline_mode=once)
-    held = lambda s: pl.BlockSpec(s, lambda p, j: (0,) * len(s), pipeline_mode=once)
+    whole = lambda a: pl.BlockSpec(a.shape, lambda s, p, j: (0,) * a.ndim, pipeline_mode=once)
+    held = lambda dims: pl.BlockSpec(dims, lambda s, p, j: (0,) * len(dims), pipeline_mode=once)
+    anywhere = pl.BlockSpec(memory_space=pl.ANY)
     at = lambda p, j: p * quads + j
-    pairs = heads // 2
+    last = pages * quads - 1
+    first = lambda s, p, j: jnp.where(s == 0, at(p, j), last)
+    second = lambda s, p, j: jnp.where(s == 0, 0, at(p, j))
+    own_at = lambda s, p, j: (jnp.where(s == 0, 0, p), 1, 0, 0)
+    dma = pltpu.SemaphoreType.DMA
+    vmem = pltpu.VMEM
+    n = 3
+    lines = early.shape[0]
+
+    def small_scratch(rows):
+        return [
+            vmem((rows, 128), F32),
+            vmem((rows, 128), F32),
+            vmem((rows, 128), F32),
+            vmem((devices[0], rows, 128), F32),
+            vmem((rows, 128), F32),
+            vmem((chips, rows, 128), F32),
+            dma((devices[0] + chips,)),
+            dma((devices[0] + chips,)),
+        ]
+
     return pl.pallas_call(
-        functools.partial(attn_backward_kernel, (window, half, width, model, heads, least)),
-        grid=(pages, quads),
+        functools.partial(
+            attn_backward_kernel, (window, half, width, model, heads, least, pages, devices, share)
+        ),
+        grid=(2, pages, quads),
         in_specs=[
             pl.BlockSpec(memory_space=pltpu.SMEM),
-            pl.BlockSpec((QUAD * slots, model), lambda p, j: (at(p, j), 0)),
-            pl.BlockSpec((QUAD * slots, model), lambda p, j: (at(p, j), 0)),
-            pl.BlockSpec((QUAD * SLOT, model), lambda p, j: (at(p, j), 0)),
-            pl.BlockSpec((3 * model, QUAD * SLOT), lambda p, j: (0, at(p, j))),
-            pl.BlockSpec((QUAD, pairs, SLOT, 2 * SLOT), lambda p, j: (at(p, j), 0, 0, 0)),
-            pl.BlockSpec((model, QUAD * SLOT), lambda p, j: (0, at(p, j))),
+            anywhere,
+            anywhere,
+            anywhere,
+            pl.BlockSpec((QUAD * slots, model), lambda s, p, j: (at(p, j), 0)),
+            pl.BlockSpec((QUAD * slots, model), lambda s, p, j: (second(s, p, j), 0)),
+            pl.BlockSpec((QUAD * SLOT, model), lambda s, p, j: (first(s, p, j), 0)),
+            pl.BlockSpec((3 * model, QUAD * SLOT), lambda s, p, j: (0, first(s, p, j))),
+            pl.BlockSpec((QUAD, pairs, SLOT, 2 * SLOT), lambda s, p, j: (first(s, p, j), 0, 0, 0)),
+            pl.BlockSpec((model, QUAD * SLOT), lambda s, p, j: (0, first(s, p, j))),
             whole(wproj),
             whole(wqkv),
             whole(vecs),
+            whole(off),
+            whole(early),
         ],
         out_specs=[
-            held((model, 4 * model)),
-            held((3 * model, SLOT)),
-            held((pairs, KEYS, 2 * SLOT)),
-            held((16, model)),
-            pl.BlockSpec((1, half, width, model), lambda p, j: (p, 1, 0, 0)),
-            pl.BlockSpec((1, half, width, model), lambda p, j: (p, 0, 0, 0)),
+            held((share, hidden)),
+            held((share, hidden)),
+            held((share, hidden)),
+            held((LATE + lines, 128)),
+            pl.BlockSpec((1, half, width, model), own_at),
+            anywhere,
+            anywhere,
         ],
         out_shape=[
-            jax.ShapeDtypeStruct((model, 4 * model), B16),
-            jax.ShapeDtypeStruct((3 * model, SLOT), F32),
-            jax.ShapeDtypeStruct((pairs, KEYS, 2 * SLOT), F32),
-            jax.ShapeDtypeStruct((16, model), F32),
+            jax.ShapeDtypeStruct((share, hidden), B16),
+            jax.ShapeDtypeStruct((share, hidden), B16),
+            jax.ShapeDtypeStruct((share, hidden), B16),
+            jax.ShapeDtypeStruct((LATE + lines, 128), F32),
             jax.ShapeDtypeStruct(shape, B16),
+            jax.ShapeDtypeStruct((pages, half, width, model), B16),
             jax.ShapeDtypeStruct((pages, half, width, model), B16),
         ],
         scratch_shapes=[
-            pltpu.VMEM((window, width + 8, model), F32),
-            pltpu.VMEM((QUAD * SLOT, model), B16),
-            pltpu.VMEM((model, QUAD * SLOT), B16),
-            pltpu.VMEM((2, pairs, KEYS, 2 * SLOT), F32),
-            pltpu.VMEM((3, model, 2 * SLOT), B16),
-            pltpu.VMEM((3, model, 2 * SLOT), B16),
-            pltpu.VMEM((3, model, 2 * SLOT), B16),
-            pltpu.VMEM((2, pairs, 2 * SLOT, SLOT), B16),
-            pltpu.VMEM((2, pairs, SLOT, 2 * SLOT), B16),
-            pltpu.VMEM((3 * model, QUAD * SLOT), B16),
-            pltpu.VMEM((3 * model, model), F32),
-            pltpu.VMEM((model, model), F32),
-            pltpu.VMEM((QUAD * slots, model), F32),
-        ],
-        compiler_params=pltpu.CompilerParams(vmem_limit_bytes=VMEM_LIMIT),
-    )(live, gf, x, n1, qkv, probs, att, wproj, wqkv, vecs)
-
-
-def table_sum(off_ref, grad_ref, out_ref):
-    heads = grad_ref.shape[0]
-    chunks = out_ref.shape[0] // heads
-    rows = 128 * chunks
-    step = 1024
-    names = lax.broadcasted_iota(jnp.int32, (rows, step), 0)
-    total = jnp.zeros((3 * heads, rows), F32)
-    for i in range(off_ref.shape[1] // step):
-        at = slice(step * i, step * i + step)
-        hot = jnp.where(names == off_ref[:, at], 1.0, 0.0).astype(B16)
-        value = grad_ref[:, at]
-        high = value.astype(B16)
-        rest = value - high.astype(F32)
-        middle = rest.astype(B16)
-        low = (rest - middle.astype(F32)).astype(B16)
-        total += dot(jnp.concatenate([high, middle, low], axis=0), hot, "NT")
-    total = total[:heads] + total[heads : 2 * heads] + total[2 * heads :]
-    for c in range(chunks):
-        out_ref[heads * c : heads * c + heads, :] = total[:, 128 * c : 128 * c + 128]
-
-
-def sums_kernel(
-    peers,
-    ga_ref,
-    gb_ref,
-    gc_ref,
-    small_ref,
-    mixed_ref,
-    patch_ref,
-    off_ref,
-    dscore_ref,
-    outa_ref,
-    outb_ref,
-    outc_ref,
-    small_out_ref,
-    mixed_out_ref,
-    patch_out_ref,
-    own1,
-    rec1,
-    s1,
-    rec2,
-    s2,
-    rec3,
-    s3,
-    rec4,
-    small_all,
-    small1,
-    small2,
-    small2s,
-    small3,
-    small3s,
-    local,
-    send1,
-    recv1,
-    send2,
-    recv2,
-    send3,
-    recv3,
-    send4,
-    recv4,
-    tiny_send,
-    tiny_recv,
-    halo_send,
-    halo_recv,
-):
-    pages, chips, table_at, heads = peers
-    grads = (ga_ref, gb_ref, gc_ref)
-    outs = (outa_ref, outb_ref, outc_ref)
-    page, row = lax.axis_index("page"), lax.axis_index("rows")
-    chip, core = row // 2, row % 2
-    other = 2 * chip + 1 - core
-    share, cols = outa_ref.shape
-    piece_cols = cols // pages
-
-    def page_peer(d):
-        return lax.rem(page + d, pages)
-
-    def chip_peer(d):
-        return lax.rem(chip + d, chips)
-
-    barrier = pltpu.get_barrier_semaphore()
-    pl.semaphore_signal(barrier, inc=1, device_id={"rows": other}, device_id_type=MESH)
-    for d in range(1, pages):
-        pl.semaphore_signal(barrier, inc=1, device_id={"page": page_peer(d)}, device_id_type=MESH)
-    for d in range(1, chips):
-        pl.semaphore_signal(
-            barrier, inc=1, device_id={"rows": 2 * chip_peer(d) + core}, device_id_type=MESH
-        )
-    behind, ahead = lax.rem(row + 2 * chips - 1, 2 * chips), lax.rem(row + 1, 2 * chips)
-    for neighbour in (behind, ahead):
-        pl.semaphore_signal(barrier, inc=1, device_id={"rows": neighbour}, device_id_type=MESH)
-    pl.semaphore_wait(barrier, pages + chips + 1)
-
-    def rows_of(ref, z, c):
-        return ref.at[pl.ds(pl.multiple_of((2 * z + c) * share, 16), share), :]
-
-    started = {}
-
-    def phase_one(m):
-        copies = []
-        for z in range(chips):
-            copy = remote(
-                rows_of(grads[m], z, 1 - core),
-                rec1.at[m, z],
-                send1.at[m, z],
-                recv1.at[m, z],
-                {"rows": other},
-            )
-            copy.start()
-            mine = pltpu.make_async_copy(rows_of(grads[m], z, core), own1.at[m, z], local.at[m, z])
-            mine.start()
-            copies += [copy, mine]
-        started[1, m] = copies
-
-    def phase_two(m):
-        for copy in started[1, m]:
-            copy.wait()
-        for q in range(pages):
-            at = slice(piece_cols * q, piece_cols * q + piece_cols)
-            total = own1[m, :, :, at].astype(F32) + rec1[m, :, :, at].astype(F32)
-            s1[m, q] = total.astype(B16)
-        copies = []
-        for d in range(1, pages):
-            copy = remote(
-                s1.at[m, page_peer(d)],
-                rec2.at[m, page],
-                send2.at[m, d],
-                recv2.at[m, d],
-                {"page": page_peer(d)},
-            )
-            copy.start()
-            copies.append(copy)
-        rec2[m, page] = s1[m, page]
-        started[2, m] = copies
-
-    def phase_three(m):
-        for copy in started[2, m]:
-            copy.wait()
-        total = rec2[m, 0].astype(F32)
-        for q in range(1, pages):
-            total = total + rec2[m, q].astype(F32)
-        s2[m] = total.astype(B16)
-        copies = []
-        for d in range(1, chips):
-            copy = remote(
-                s2.at[m, chip_peer(d)],
-                rec3.at[m, chip],
-                send3.at[m, d],
-                recv3.at[m, d],
-                {"rows": 2 * chip_peer(d) + core},
-            )
-            copy.start()
-            copies.append(copy)
-        rec3[m, chip] = s2[m, chip]
-        started[3, m] = copies
-
-    def phase_four(m):
-        for copy in started[3, m]:
-            copy.wait()
-        total = rec3[m, 0].astype(F32)
-        for z in range(1, chips):
-            total = total + rec3[m, z].astype(F32)
-        s3[m] = total.astype(B16)
-        copies = []
-        for d in range(1, pages):
-            copy = remote(
-                s3.at[m], rec4.at[m, page], send4.at[m, d], recv4.at[m, d], {"page": page_peer(d)}
-            )
-            copy.start()
-            copies.append(copy)
-        rec4[m, page] = s3[m]
-        started[4, m] = copies
-
-    def finish(m):
-        for copy in started[4, m]:
-            copy.wait()
-        for q in range(pages):
-            outs[m][:, piece_cols * q : piece_cols * q + piece_cols] = rec4[m, q].astype(F32)
-
-    count = len(grads)
-    for m in range(count):
-        phase_one(m)
-    halos = [
-        remote(mixed_ref, mixed_out_ref, halo_send.at[0], halo_recv.at[0], {"rows": ahead}),
-        remote(patch_ref, patch_out_ref, halo_send.at[1], halo_recv.at[1], {"rows": ahead}),
-    ]
-    for copy in halos:
-        copy.start()
-    phase_two(0)
-    small_all[...] = small_ref[...]
-    table_sum(off_ref, dscore_ref, small_all.at[pl.ds(table_at, small_all.shape[0] - table_at), :])
-    tiny = remote(small_all, small1, tiny_send.at[0], tiny_recv.at[0], {"rows": other})
-    tiny.start()
-    for m in range(1, count):
-        phase_two(m)
-    tiny.wait()
-    small2s[...] = small_all[...] + small1[...]
-    small2[page] = small2s[...]
-    tinies = []
-    for d in range(1, pages):
-        copy = remote(small2s, small2.at[page], tiny_send.at[d], tiny_recv.at[d], {"page": page_peer(d)})
-        copy.start()
-        tinies.append(copy)
-    for m in range(count):
-        phase_three(m)
-    for copy in tinies:
-        copy.wait()
-    total = small2[0]
-    for q in range(1, pages):
-        total = total + small2[q]
-    small3s[...] = total
-    small3[chip] = total
-    tinies = []
-    for d in range(1, chips):
-        copy = remote(
-            small3s,
-            small3.at[chip],
-            tiny_send.at[pages + d],
-            tiny_recv.at[pages + d],
-            {"rows": 2 * chip_peer(d) + core},
-        )
-        copy.start()
-        tinies.append(copy)
-    for m in range(count):
-        phase_four(m)
-    for copy in tinies:
-        copy.wait()
-    total = small3[0]
-    for z in range(1, chips):
-        total = total + small3[z]
-    small_out_ref[...] = total
-    for m in range(count):
-        finish(m)
-    for copy in halos:
-        copy.wait()
-
-
-def sums(grads, small, mixed, patch, off, dscore, table_at, pages, rows):
-    chips = rows // 2
-    model, cols = grads[0].shape
-    share, piece_cols = model // rows, cols // pages
-    n = len(grads)
-    vmem = pl.BlockSpec(memory_space=pltpu.VMEM)
-    dma = pltpu.SemaphoreType.DMA
-    return pl.pallas_call(
-        functools.partial(sums_kernel, (pages, chips, table_at, dscore.shape[0])),
-        in_specs=[pl.BlockSpec(memory_space=pl.ANY)] * n
-        + [vmem]
-        + [pl.BlockSpec(memory_space=pl.ANY)] * 2
-        + [vmem] * 2,
-        out_specs=[vmem] * (n + 1) + [pl.BlockSpec(memory_space=pl.ANY)] * 2,
-        out_shape=[jax.ShapeDtypeStruct((share, cols), F32)] * n
-        + [jax.ShapeDtypeStruct(a.shape, a.dtype) for a in (small, mixed, patch)],
-        scratch_shapes=[
-            pltpu.VMEM((n, chips, share, cols), B16),
-            pltpu.VMEM((n, chips, share, cols), B16),
-            pltpu.VMEM((n, pages, chips, share, piece_cols), B16),
-            pltpu.VMEM((n, pages, chips, share, piece_cols), B16),
-            pltpu.VMEM((n, chips, share, piece_cols), B16),
-            pltpu.VMEM((n, chips, share, piece_cols), B16),
-            pltpu.VMEM((n, share, piece_cols), B16),
-            pltpu.VMEM((n, pages, share, piece_cols), B16),
-            pltpu.VMEM(small.shape, F32),
-            pltpu.VMEM(small.shape, F32),
-            pltpu.VMEM((pages,) + small.shape, F32),
-            pltpu.VMEM(small.shape, F32),
-            pltpu.VMEM((chips,) + small.shape, F32),
-            pltpu.VMEM(small.shape, F32),
+            vmem((window, width + 8, model), F32),
+            vmem((QUAD * SLOT, model), B16),
+            vmem((model, QUAD * SLOT), B16),
+            vmem((2, pairs, KEYS, 2 * SLOT), F32),
+            vmem((3, model, 2 * SLOT), B16),
+            vmem((3, model, 2 * SLOT), B16),
+            vmem((3, model, 2 * SLOT), B16),
+            vmem((2, pairs, 2 * SLOT, SLOT), B16),
+            vmem((2, pairs, SLOT, 2 * SLOT), B16),
+            vmem((pages * quads, 3 * model, QUAD * SLOT), B16),
+            vmem((3 * model, model), F32),
+            vmem((model, model), F32),
+            vmem((QUAD * slots, model), F32),
+            vmem((heads, KEYS, SLOT), F32),
+            vmem((3 * model, SLOT), F32),
+            vmem((16, model), F32),
+            vmem((model, hidden), B16),
+            vmem((pages, half, width, model), B16),
+            vmem((2, chips, share, hidden), B16),
+            vmem((n, chips, share, hidden), B16),
+            vmem((n, devices[0], chips, share, cols), B16),
+            vmem((n, devices[0], chips, share, cols), B16),
+            vmem((n, chips, share, cols), B16),
+            vmem((n, chips, share, cols), B16),
+            vmem((n, share, cols), B16),
+            vmem((n, devices[0], share, cols), B16),
             dma((n, chips)),
             dma((n, chips)),
-            dma((n, chips)),
-            dma((n, pages)),
-            dma((n, pages)),
+            dma((n, devices[0])),
+            dma((n, devices[0])),
             dma((n, chips)),
             dma((n, chips)),
-            dma((n, pages)),
-            dma((n, pages)),
-            dma((pages + chips,)),
-            dma((pages + chips,)),
-            dma((2,)),
-            dma((2,)),
-        ],
+            dma((n, devices[0])),
+            dma((n, devices[0])),
+        ]
+        + small_scratch(lines)
+        + small_scratch(LATE)
+        + [dma((2, chips)), dma((1 + pages,)), dma((1 + pages,))],
         compiler_params=pltpu.CompilerParams(
-            vmem_limit_bytes=VMEM_LIMIT, collective_id=0, has_side_effects=True
+            vmem_limit_bytes=63 * 2**20, collective_id=0, has_side_effects=True
         ),
-    )(*grads, small, mixed, patch, off, dscore)
+    )(live, dwup, dwout, mixed_next, gf, x, n1, qkv, probs, att, wproj, wqkv, vecs, off, early)
 
 
 def adam_update(master, first, second, grad):
@@ -1043,7 +1138,7 @@
     labels = jnp.pad(labels, ((0, 0), (0, 8 - QUAD), (0, SLOT - slots)), constant_values=-1.0)
     off = offset_index.T
     off_gather = jnp.pad(off, ((0, KEYS - slots), (0, SLOT - slots)))
-    off_scatter = jnp.pad(off, ((0, KEYS - slots), (0, SLOT - slots)), constant_values=-1).reshape(1, -1)
+    off_scatter = jnp.pad(off, ((0, KEYS - slots), (0, SLOT - slots)), constant_values=-1)
     table_lanes = -(-table_rows // 128) * 128
     tab = jnp.pad(bias_table.T * LOG2E, ((0, 0), (0, table_lanes - table_rows)))
     wqkv = weights_in[:, : 3 * model].T
@@ -1073,47 +1168,31 @@
         page_windows, out_grad, below_grad, n2, first, weights_in, weights_out,
         biases[None, 6 * model :], vec_two, least, master_in.shape[0],
     )
-    dwa, dbqkv, dscore, sums_one, patch_own, patch_next = attn_backward(
-        page_windows, gf, x, n1, qkv, probs, att, wproj, wqkv, vec_one, patches.shape, heads, least
+    sums_two = sums_two.reshape(4, 8, model).sum(1)
+    lines = model // 128
+    early = jnp.concatenate(
+        [
+            jnp.zeros((2 * lines, 128), F32),
+            sums_two[jnp.array([0, 3, 1, 2])].reshape(4 * lines, 128),
+            dbup.reshape(-1, 128),
+            jnp.zeros((table_lanes * heads // 128, 128), F32),
+        ]
     )
-    dscore = dscore.reshape(heads // 2, KEYS, 2, SLOT).transpose(0, 2, 1, 3).reshape(heads, KEYS * SLOT)
-    sums_one = sums_one.reshape(2, 8, model).sum(1)
-    sums_two = sums_two.reshape(4, 8, model).sum(1)
-    dbqkv = dbqkv.sum(1)
-    grad_small = jnp.concatenate(
-        [
-            sums_one[0],
-            sums_two[0],
-            sums_one[1],
-            dbqkv[:model],
-            dbqkv[2 * model :],
-            sums_two[3],
-            sums_two[1],
-            sums_two[2],
-            dbup.reshape(-1),
-            jnp.zeros((table_lanes * heads,), F32),
-        ]
-    ).reshape(-1, 128)
-    table_at = grad_small.shape[0] - table_lanes * heads // 128
-    total_a, total_up, total_out, total_small, above, above_grad = sums(
-        [dwa, dwup, dwout],
-        grad_small,
-        mixed_next,
-        patch_next,
-        off_scatter,
-        dscore,
-        table_at,
-        lax.axis_size("page"),
-        lax.axis_size("rows"),
+    total_a, total_up, total_out, small, patch_own, above, above_grad = attn_backward(
+        page_windows, dwup, dwout, mixed_next, gf, x, n1, qkv, probs, att, wproj, wqkv, vec_one,
+        off_scatter, early, patches.shape, heads, least, master_in.shape[0],
     )
     mixed = lax.dynamic_update_slice(mixed_own, above, (0, 0, 0, 0))
     patch_grad = lax.dynamic_update_slice(patch_own, above_grad, (0, 0, 0, 0))
-    total_table = total_small[table_at:].reshape(table_lanes // 128, heads, 128).transpose(0, 2, 1)
+    small_at = [0, 4, 1, 2, 3, 5, 6, 7]
+    table_at = small.shape[0] - table_lanes * heads // 128
+    total_table = small[table_at:].reshape(table_lanes // 128, heads, 128).transpose(0, 2, 1)
     total_table = total_table.reshape(table_lanes, heads)[:table_rows]
-    total_small = jnp.concatenate([total_small[:table_at].reshape(-1), total_table.reshape(-1)])
-    part_in = jnp.concatenate([total_a, total_up], axis=1)
+    head = [small[lines * k : lines * k + lines] for k in small_at] + [small[8 * lines : table_at]]
+    total_small = jnp.concatenate([jnp.concatenate(head).reshape(-1), total_table.reshape(-1)])
+    part_in = jnp.concatenate([total_a, total_up], axis=1).astype(F32)
     ratio = hidden // model
-    total_out = total_out.reshape(-1, ratio, model).transpose(1, 0, 2).reshape(-1, model)
+    total_out = total_out.reshape(-1, ratio, model).transpose(1, 0, 2).reshape(-1, model).astype(F32)
     small_master = jnp.concatenate([norm_gains.reshape(-1), biases, bias_table.reshape(-1)])
     new_in, moment_in, square_in = adam_update(master_in, first_in, second_in, part_in)
     new_out, moment_out, square_out = adam_update(master_out, first_out, second_out, total_out)

time: 227 us -> 220 us (0.969)
  Pallas kernels: 199 us -> 190 us
  other arithmetic: 5.35 us -> 10.6 us
  local copies, waits for them, and re-layouts: 21.2 us -> 18.1 us
    pallas_call x1 -> x0, Pallas kernels: 65 us -> none  [sums(): pl.pallas_call(functools.partial(sums_kernel, (pages, chips, table_at, ds...]
    pallas_call x1, Pallas kernels: 36.1 us -> 91.3 us  [attn_backward(): pl.pallas_call(functools.partial(attn_backward_kernel, (window, half, wid...]
    unnamed x68 -> x32, local copies, waits for them, and re-layouts: 8.43 us -> 3.29 us
    sub x3, other arithmetic: 4.33 us -> 7.65 us  [adam_update(): master - LEARN_RATE * (moment / fix_one / (jnp.sqrt(square / fix_two) + A...]
    slice x2 -> x4, local copies, waits for them, and re-layouts: 0.02 us -> 2.86 us  [the longest x3 2.12 us: shards(): small[lines * k:lines * k + lines]]
    reshape x4 -> x2, local copies, waits for them, and re-layouts: 2.56 us -> 0.03 us  [the longest x1 0.02 us: shards(): small[table_at:].reshape(table_lanes // 128, heads, 128).transpose(0, 2, 1)]
where the time goes in v2:
time: 220 us
  Pallas kernels  190 us (86%)
  local copies, waits for them, and re-layouts  18.1 us (8%)
  other arithmetic  10.6 us (5%)
    pallas_call x1, Pallas kernels, attn_backward(): pl.pallas_call(functools.partial(attn_backward_kernel, (window, half, wid...  91.3 us
    pallas_call x1, Pallas kernels, mlp(): pl.pallas_call(functools.partial(mlp_kernel, (window, half, width, model,...  57.4 us
    pallas_call x1, Pallas kernels, attn_forward(): pl.pallas_call(functools.partial(attn_forward_kernel, (window, half, widt...  41.1 us
    sub x3, other arithmetic, adam_update(): master - LEARN_RATE * (moment / fix_one / (jnp.sqrt(square / fix_two) + A...  7.65 us

profile of v2, /device:TPU:0, one launch (start us, length us, event | category | flops | bytes accessed | tf_op | source)
XLA Modules:
  0.0 219.6 jit_solution(12358828585066112033)
XLA Ops:
  0.7 0.9 fusion.12
  1.5 0.8 fusion.13
  2.3 0.6 stack.24.vec_ref
  3.0 1.2 broadcast_in_dim.24.bqkv_ref
  4.1 1.6 copy.42
  5.7 1.9 slice.62.wproj_ref
  7.7 0.7 fusion.10
  8.7 0.6 pad.15.label_ref
  9.3 0.6 pad.17.tab_ref
  9.9 41.1 %shard_map.266 = (bf16[2400,512]{1,0:T(8,128)(2,1)}, bf16[3072,512]{1,0:T(8,128)(2,1)}, bf16[1536,3072]{1,0:T(8,128)(2,1)}, bf16[24,8,128,256]{3,2,1,0:T(8,128)(...) custom-call(s32[2]{0:T(128)} %live_ref.5, ...), custom_call_target="tpu_custom_call" | custom-call | tf_op jit(solution)/shard_map/pallas_call | solution.py:274
  51.2 0.7 maximum_maximum_fusion.1.vec_ref
  51.8 0.6 slice.68
  52.4 57.4 %shard_map.267 = (bf16[512,2048]{1,0:T(8,128)(2,1)}, bf16[512,2048]{1,0:T(8,128)(2,1)}, f32[1,2048]{1,0:T(1,128)}, f32[2400,512]{1,0:T(8,128)}, bf16[2,10,120,51...) custom-call(s32[2]{0:T(128)} %live_ref.5, bf16[2,10,120,512]{3,2,1,0:T(8,128)(2,1)} %low_ref.3, ...), custom_call_target="tpu_custom_call" | custom-call | tf_op jit(solution)/shard_map/pallas_call | solution.py:469
  109.9 0.9 bitcast_reduce_fusion
  110.8 0.6 gather_fusion
  111.5 1.4 maximum_maximum_fusion.early_ref
  112.9 91.3 %shard_map.268 = (bf16[64,2048]{1,0:T(8,128)(2,1)}, bf16[64,2048]{1,0:T(8,128)(2,1)}, bf16[64,2048]{1,0:T(8,128)(2,1)}, f32[96,128]{1,0:T(8,128)}, bf16[2,10,120...) custom-call(s32[2]{0:T(128)} %live_ref.5, ...), custom_call_target="tpu_custom_call" | custom-call | tf_op jit(solution)/shard_map/pallas_call | solution.py:1012
  204.2 0.7 slice.73
  204.9 0.7 slice.72
  205.6 0.7 fusion.11
  206.3 0.7 slice.74
  207.1 0.1 copy.41
  207.2 0.1 reshape.67
  207.4 0.1 copy.39
  207.5 0.1 reshape.63
  207.7 0.7 multiply_subtract_fusion.2
  208.4 4.3 %multiply_subtract_fusion = (f32[64,4096]{1,0:T(8,128)}, f32[64,4096]{1,0:T(8,128)}, f32[64,4096]{1,0:T(8,128)}) fusion(f32[64,4096]{1,0:T(8,128)} %param.29, bf16[64,2048]{1,0:T(8,128)(2,1)} %get-tuple-element.52, bf16[64,2048]{1,0:T(8,128)(2,1)} %get-tuple-element.51, f32[64,4096]{1,0:T(8,128)} %param.31, f32[64,4096]{1,0:T(8,128)} %param.32), kind=kLoop, calls=%fused_computation.5 | loop fusion | flops 4980736 | bytes 6815744 | tf_op jit(solution)/shard_map/sub | solution.py:1102
  212.7 1.2 constant_dynamic-update-slice_fusion.3
  213.9 1.4 reshape.69
  215.3 0.2 copy.38
  215.5 2.6 %multiply_subtract_fusion.1 = (f32[256,512]{1,0:T(8,128)}, f32[256,512]{1,0:T(8,128)}, f32[256,512]{1,0:T(8,128)}) fusion(f32[256,512]{1,0:T(8,128)S(1)} %copy-done.3, f32[4,64,512]{2,1,0:T(8,128)S(1)} %copy.38, f32[256,512]{1,0:T(8,128)} %param.33, f32[256,512]{1,0:T(8,128)} %param.34), kind=kLoop, calls=%fused_computation.11 | loop fusion | flops 1966080 | bytes 3670016 | tf_op jit(solution)/shard_map/sub | solution.py:1102
  218.1 1.4 copy.52
  (51 shorter events, 0.7 us)
Async XLA Ops:
  0.6 3.5 %slice-start = ((bf16[512,4096]{1,0:T(8,128)(2,1)}), bf16[512,1536]{1,0:T(8,128)(2,1)S(1)}, s32[]{:S(2)}) async-start(bf16[512,4096]{1,0:T(8,128)(2,1)} %wup_ref.1), calls=%async_computation | async-start | bytes 3145728 | tf_op jit(solution)/shard_map/slice | solution.py:1144
  4.1 3.5 %copy-start.6 = (s32[100,100]{1,0:T(8,128)S(1)}, s32[100,100]{1,0:T(8,128)}, u32[]{:S(2)}) copy-start(s32[100,100]{1,0:T(8,128)} %param.23) | copy-start | bytes 120004
  4.1 4.2 %copy-start.10 = (s32[2,10,120]{2,0,1:T(2,128)S(1)}, s32[2,10,120]{2,0,1:T(2,128)}, u32[]{:S(2)}) copy-start(s32[2,10,120]{2,0,1:T(2,128)} %param.22) | copy-start | bytes 28804
  4.1 5.2 %copy-start.4 = (f32[361,16]{0,1:T(8,128)S(1)}, f32[361,16]{0,1:T(8,128)}, u32[]{:S(2)}) copy-start(f32[361,16]{0,1:T(8,128)} %param.28) | copy-start | bytes 69316
  9.9 41.9 %copy-start.5 = (f32[5120]{0:T(1024)S(1)}, f32[5120]{0:T(1024)}, u32[]{:S(2)}) copy-start(f32[5120]{0:T(1024)} %param.27) | copy-start | bytes 61444
  52.4 58.3 %copy-start.11 = (s32[4]{0:T(128)S(1)}, s32[4]{0:T(128)}, u32[]{:S(2)}) copy-start(s32[4]{0:T(128)} %constant.40) | copy-start | bytes 52
  112.9 94.7 %copy-start.9 = (f32[2,512]{1,0:T(2,128)S(1)}, f32[2,512]{1,0:T(2,128)}, u32[]{:S(2)}) copy-start(f32[2,512]{1,0:T(2,128)} %param.26) | copy-start | bytes 12292
  112.9 94.8 %copy-start.7 = (f32[11920]{0:T(1024)S(1)}, f32[11920]{0:T(1024)}, u32[]{:S(2)}) copy-start(f32[11920]{0:T(1024)} %param.35) | copy-start | bytes 143044
  112.9 94.8 %copy-start.8 = (f32[11920]{0:T(1024)S(1)}, f32[11920]{0:T(1024)}, u32[]{:S(2)}) copy-start(f32[11920]{0:T(1024)} %param.36) | copy-start | bytes 143044
  208.4 4.3 %copy-start = (bf16[2,10,120,512]{3,2,1,0:T(8,128)(2,1)S(1)}, bf16[2,10,120,512]{3,2,1,0:T(8,128)(2,1)}, u32[]{:S(2)}) copy-start(bf16[2,10,120,512]{3,2,1,0:T(8,128)(2,1)} %get-tuple-element.49) | copy-start | bytes 7372804
  208.4 4.3 %copy-start.1 = (bf16[2,5,120,512]{3,2,1,0:T(8,128)(2,1)S(1)}, bf16[2,5,120,512]{3,2,1,0:T(8,128)(2,1)}, u32[]{:S(2)}) copy-start(bf16[2,5,120,512]{3,2,1,0:T(8,128)(2,1)} %get-tuple-element.48) | copy-start | bytes 3686404
  208.4 4.3 %copy-start.2 = (bf16[2,5,120,512]{3,2,1,0:T(8,128)(2,1)S(1)}, bf16[2,5,120,512]{3,2,1,0:T(8,128)(2,1)}, u32[]{:S(2)}) copy-start(bf16[2,5,120,512]{3,2,1,0:T(8,128)(2,1)} %get-tuple-element.50) | copy-start | bytes 3686404
  212.7 2.8 %copy-start.3 = (f32[256,512]{1,0:T(8,128)S(1)}, f32[256,512]{1,0:T(8,128)}, u32[]{:S(2)}) copy-start(f32[256,512]{1,0:T(8,128)} %param.30) | copy-start | bytes 1572868

commit v3 on v2

--- a/solution.py
+++ b/solution.py
@@ -56,7 +56,8 @@
         front = jnp.where(live == count, band[:, at], front)
     band[:, :half] = front
     edge = least * window // 8 * 8
-    columns = lax.broadcasted_iota(jnp.int32, (window, width - edge, band.shape[2]), 1) + edge
+    shape = (band.shape[0], width - edge, band.shape[2])
+    columns = lax.broadcasted_iota(jnp.int32, shape, 1) + edge
     band[:, edge:width] = jnp.where(columns < live * window, band[:, edge:width], 0.0)
 
 
@@ -96,6 +97,16 @@
     return pltpu.make_async_remote_copy(
         src_ref=src, dst_ref=dst, send_sem=send, recv_sem=recv, device_id=device, device_id_type=MESH
     )
+
+
+def lay_lines(lines_ref, at, row):
+    for i in range(row.shape[1] // 128):
+        lines_ref[at + i : at + i + 1, :] = row[:, 128 * i : 128 * i + 128]
+
+
+def lay_row(ref, row, lines_ref, at, count):
+    for i in range(count):
+        ref[row : row + 1, 128 * i : 128 * i + 128] = lines_ref[at + i : at + i + 1, :]
 
 
 def attn_forward_kernel(
@@ -108,9 +119,9 @@
     off_ref,
     tab_ref,
     wqkv_ref,
-    bqkv_ref,
     wproj_ref,
-    vec_ref,
+    gains_ref,
+    biases_ref,
     x_ref,
     n1_ref,
     qkv_ref,
@@ -119,6 +130,8 @@
     first_ref,
     n2_ref,
     grad_halo_ref,
+    turned_ref,
+    places_ref,
     halo,
     send,
     recv,
@@ -130,6 +143,11 @@
     stacked,
     xs,
     ns,
+    vecs,
+    column,
+    square,
+    tall,
+    flat,
 ):
     window, half, width, model, heads, least, pages, rows_count = sizes
     slots = window * window
@@ -137,6 +155,8 @@
     page, quad = pl.program_id(0), pl.program_id(1)
     live = live_ref[page]
     pairs = heads // 2
+    part_rows = model // 2
+    lines = model // 128
     row = lax.axis_index("rows")
     behind, ahead = lax.rem(row + rows_count - 1, rows_count), lax.rem(row + 1, rows_count)
 
@@ -164,12 +184,38 @@
             halo_copy(p).start()
         for p in range(pages):
             grad_copy(p).start()
-        off = off_ref[...]
+        vecs[...] = jnp.zeros_like(vecs)
+        vecs[0:1, :] = gains_ref[0:1, :]
+        lay_row(vecs, 1, biases_ref, 0, lines)
+        lay_row(vecs, 2, biases_ref, 3 * lines, lines)
+        vecs[3:4, :] = gains_ref[1:2, :]
+        lay_row(vecs, 4, biases_ref, 4 * lines, lines)
+        column[...] = jnp.zeros_like(column)
+        for h in range(2):
+            for part in range(3):
+                rows = slice(part * part_rows, part * part_rows + part_rows)
+                cols = slice(part * model + h * part_rows, part * model + (h + 1) * part_rows)
+                turned_ref[h, rows, :] = wqkv_ref[:, cols].T
+                if part != 1:
+                    for i in range(part_rows // 128):
+                        line = lines * (1 + part // 2) + h * (part_rows // 128) + i
+                        spread = jnp.broadcast_to(biases_ref[line : line + 1, :], (128, 128))
+                        at = part * part_rows + 128 * i
+                        column[h, at : at + 128, :] = spread.T
+        square[...] = jnp.full_like(square, -1)
+        square[:slots, :slots] = off_ref[...]
+        places = square[...].T[:KEYS]
+        places_ref[...] = places
+        off = jnp.maximum(places, 0)
+        tall[...] = jnp.zeros_like(tall)
+        tall[: tab_ref.shape[0], :heads] = tab_ref[...] * LOG2E
+        for c in range(tall.shape[0] // 128):
+            flat[:, 128 * c : 128 * c + 128] = tall[128 * c : 128 * c + 128, :].T[:heads]
         low, high = jnp.bitwise_and(off, 127), jnp.right_shift(off, 7)
         for h in range(heads):
             got = jnp.zeros((KEYS, SLOT), F32)
-            for c in range(tab_ref.shape[1] // 128):
-                source = jnp.broadcast_to(tab_ref[h : h + 1, 128 * c : 128 * c + 128], (KEYS, SLOT))
+            for c in range(tall.shape[0] // 128):
+                source = jnp.broadcast_to(flat[h : h + 1, 128 * c : 128 * c + 128], (KEYS, SLOT))
                 picked = jnp.take_along_axis(source, low, axis=1, mode="promise_in_bounds")
                 got = jnp.where(high == c, picked, got)
             bias[h] = got
@@ -197,18 +243,18 @@
     x = xs[...]
     x_ref[...] = x.astype(B16)
     xhat, _ = norm_stats(x)
-    ns[...] = xhat * vec_ref[0:1, :] + vec_ref[1:2, :]
+    ns[...] = xhat * vecs[0:1, :] + vecs[1:2, :]
     for w in range(QUAD):
         n1_ref[SLOT * w : SLOT * w + slots, :] = ns[slots * w : slots * w + slots, :].astype(B16)
         n1_ref[SLOT * w + slots : SLOT * w + SLOT, :] = jnp.zeros((SLOT - slots, model), B16)
     scale = size_head**-0.5 * LOG2E
     n1 = n1_ref[...]
-    for part in range(3):
-        rows = slice(part * model, part * model + model)
-        got = dot(wqkv_ref[rows, :], n1, "NT") + bqkv_ref[rows, :]
-        if part == 0:
-            got = got * scale
-        qkv_ref[rows, :] = got.astype(B16)
+    for h in range(2):
+        got = dot(turned_ref[h], n1, "NT") + column[h, :, 0:1]
+        at = slice(h * part_rows, h * part_rows + part_rows)
+        qkv_ref[0, at, :] = (got[:part_rows] * scale).astype(B16)
+        qkv_ref[1, at, :] = got[part_rows : 2 * part_rows].astype(B16)
+        qkv_ref[2, at, :] = got[2 * part_rows :].astype(B16)
 
     sames = []
     for w in range(QUAD):
@@ -222,10 +268,9 @@
         for j in range(2):
             at = slice(low + size_head * j, low + size_head * (j + 1))
             cols = slice(SLOT * j, SLOT * j + SLOT)
-            bdq[w % 2, at, cols] = qkv_ref[at, lanes]
-            values = slice(2 * model + low + size_head * j, 2 * model + low + size_head * (j + 1))
-            bdv[w % 3, at, cols] = qkv_ref[values, lanes]
-        keys = qkv_ref[model + low : model + low + pair, SLOT * w : SLOT * w + KEYS]
+            bdq[w % 2, at, cols] = qkv_ref[0, at, lanes]
+            bdv[w % 3, at, cols] = qkv_ref[2, at, lanes]
+        keys = qkv_ref[1, low : low + pair, SLOT * w : SLOT * w + KEYS]
         scores[w % 2, g] = dot(keys, bdq[w % 2, low : low + pair, :], "TN")
 
     def soften(w, g):
@@ -255,15 +300,16 @@
     branch = dot(att_ref[...], wproj_ref[...], "TN")
     for w in range(QUAD):
         rows = slice(slots * w, slots * w + slots)
-        first_ref[rows, :] = xs[rows, :] + branch[SLOT * w : SLOT * w + slots, :] + vec_ref[2:3, :]
+        first_ref[rows, :] = xs[rows, :] + branch[SLOT * w : SLOT * w + slots, :] + vecs[2:3, :]
     xhat, _ = norm_stats(first_ref[...])
-    n2_ref[...] = (xhat * vec_ref[3:4, :] + vec_ref[4:5, :]).astype(B16)
-
-
-def attn_forward(live, patches, out_grad, labels, off, tab, wqkv, bqkv, wproj, vecs, least):
+    n2_ref[...] = (xhat * vecs[3:4, :] + vecs[4:5, :]).astype(B16)
+
+
+def attn_forward(live, patches, out_grad, labels, off, tab, weights_in, gains, biases, least):
     pages, window, width, model = patches.shape
     half = window // 2
-    heads = tab.shape[0]
+    table_rows, heads = tab.shape
+    table_lanes = -(-table_rows // 128) * 128
     quads = width // window // QUAD
     tokens = pages * window * width
     slots = window * window
@@ -285,30 +331,34 @@
             pl.BlockSpec((1, 8, SLOT), lambda p, j: (at(p, j), 0, 0)),
             whole(off),
             whole(tab),
-            whole(wqkv),
-            whole(bqkv),
-            whole(wproj),
-            whole(vecs),
+            pl.BlockSpec((model, 3 * model), lambda p, j: (0, 0), pipeline_mode=pl.Buffered(1)),
+            pl.BlockSpec((model, model), lambda p, j: (0, 3), pipeline_mode=pl.Buffered(1)),
+            whole(gains),
+            whole(biases),
         ],
         out_specs=[
             pl.BlockSpec((QUAD * slots, model), lambda p, j: (at(p, j), 0)),
             pl.BlockSpec((QUAD * SLOT, model), lambda p, j: (at(p, j), 0)),
-            pl.BlockSpec((3 * model, QUAD * SLOT), lambda p, j: (0, at(p, j))),
+            pl.BlockSpec((3, model, QUAD * SLOT), lambda p, j: (0, 0, at(p, j))),
             pl.BlockSpec((QUAD, heads // 2, SLOT, 2 * SLOT), lambda p, j: (at(p, j), 0, 0, 0)),
             pl.BlockSpec((model, QUAD * SLOT), lambda p, j: (0, at(p, j))),
             pl.BlockSpec((QUAD * slots, model), lambda p, j: (at(p, j), 0)),
             pl.BlockSpec((QUAD * slots, model), lambda p, j: (at(p, j), 0)),
             pl.BlockSpec(memory_space=pl.ANY),
+            pl.BlockSpec((2, 3 * model // 2, model), lambda p, j: (0, 0, 0), pipeline_mode=pl.Buffered(1)),
+            pl.BlockSpec((KEYS, SLOT), lambda p, j: (0, 0)),
         ],
         out_shape=[
             jax.ShapeDtypeStruct((tokens, model), B16),
             jax.ShapeDtypeStruct((padded, model), B16),
-            jax.ShapeDtypeStruct((3 * model, padded), B16),
+            jax.ShapeDtypeStruct((3, model, padded), B16),
             jax.ShapeDtypeStruct((pages * quads * QUAD, heads // 2, SLOT, 2 * SLOT), B16),
             jax.ShapeDtypeStruct((model, padded), B16),
             jax.ShapeDtypeStruct((tokens, model), F32),
             jax.ShapeDtypeStruct((tokens, model), B16),
             jax.ShapeDtypeStruct((pages, half, width, model), B16),
+            jax.ShapeDtypeStruct((2, 3 * model // 2, model), B16),
+            jax.ShapeDtypeStruct((KEYS, SLOT), jnp.int32),
         ],
         scratch_shapes=[
             pltpu.VMEM((pages, half, width, model), B16),
@@ -322,15 +372,22 @@
             pltpu.VMEM((2, heads // 2, 2 * SLOT, SLOT), B16),
             pltpu.VMEM((QUAD * slots, model), F32),
             pltpu.VMEM((QUAD * slots, model), F32),
+            pltpu.VMEM((8, model), F32),
+            pltpu.VMEM((2, 3 * model // 2, 128), F32),
+            pltpu.VMEM((SLOT, SLOT), jnp.int32),
+            pltpu.VMEM((table_lanes, 128), F32),
+            pltpu.VMEM((heads, table_lanes), F32),
         ],
         compiler_params=pltpu.CompilerParams(
             vmem_limit_bytes=VMEM_LIMIT, collective_id=1, has_side_effects=True
         ),
-    )(live, patches, out_grad, patches, labels, off, tab, wqkv, bqkv, wproj, vecs)
+    )(live, patches, out_grad, patches, labels, off, tab, weights_in, weights_in, gains, biases)
 
 
 MLP_COLS = 512
+MLP_CHUNKS = 4
 MLP_ROWS = 480
+EARLY_UP = 6
 
 
 def mlp_kernel(
@@ -342,15 +399,17 @@
     first_ref,
     wup_ref,
     wout_ref,
-    bup_ref,
-    vec_ref,
+    gains_ref,
+    biases_ref,
     dwup_ref,
     dwout_ref,
-    dbup_ref,
     gf_ref,
     own_ref,
     next_ref,
-    sums_ref,
+    early_ref,
+    bup,
+    vecs,
+    sums,
     band,
     cot,
     res,
@@ -366,9 +425,19 @@
     chunk = pl.program_id(0)
     tokens = n2_ref.shape[0]
     cols = wup_ref.shape[1]
+    lines = model // 128
+
+    for c in range(MLP_CHUNKS):
+
+        @pl.when(chunk == c)
+        def _():
+            lay_row(bup, 0, biases_ref, 6 * lines + c * (cols // 128), cols // 128)
 
     @pl.when(chunk == 0)
     def _():
+        early_ref[...] = jnp.zeros_like(early_ref)
+        vecs[0:1, :] = gains_ref[1:2, :]
+        lay_row(vecs, 1, biases_ref, 5 * lines, lines)
         for page in range(pages):
             live = live_ref[page]
             load_band(band, low_ref.at[page], high_ref.at[page], live, half, width, window, least)
@@ -388,7 +457,7 @@
     def body(i, total):
         rows = pl.ds(pl.multiple_of(i * MLP_ROWS, 16), MLP_ROWS)
         grad = cot[rows, :]
-        pre = dot(n2_ref[rows, :], wup_ref[...]) + bup_ref[...]
+        pre = dot(n2_ref[rows, :], wup_ref[...]) + bup[0:1, :]
         grad_act = dot(grad, wout_ref[...], "NT")
         share = 0.5 * (1.0 + lax.erf(pre * 0.5**0.5))
         act = (pre * share).astype(B16)
@@ -412,7 +481,13 @@
         return total + fold(grad_pre.astype(F32))
 
     total = lax.fori_loop(0, tokens // MLP_ROWS, body, jnp.zeros((8, cols), F32))
-    dbup_ref[...] = jnp.sum(total, axis=0, keepdims=True)
+    total = jnp.sum(total, axis=0, keepdims=True)
+    for c in range(MLP_CHUNKS):
+
+        @pl.when(chunk == c)
+        def _():
+            lay_lines(early_ref, EARLY_UP * lines + c * (cols // 128), total)
+
     grad_out = dot(act_all[...], cot[...], "TN").astype(B16)
     for s in range(dwout_ref.shape[0] // share):
         for a in range(dwout_ref.shape[1] // model):
@@ -422,7 +497,7 @@
 
     @pl.when(chunk == pl.num_programs(0) - 1)
     def _():
-        sums_ref[...] = jnp.zeros_like(sums_ref)
+        sums[...] = jnp.zeros_like(sums)
         for page in range(pages):
             live = live_ref[page]
 
@@ -430,19 +505,19 @@
                 at = pl.multiple_of((page * quads + j) * QUAD * slots, 16)
                 rows = pl.ds(at, QUAD * slots)
                 first = first_ref[rows, :]
-                res[rows, :] += first + vec_ref[1:2, :]
+                res[rows, :] += first + vecs[1:2, :]
                 xhat, spread = norm_stats(first)
                 grad = dn2[rows, :]
                 given = cot[rows, :].astype(F32)
-                scaled = grad * vec_ref[0:1, :]
+                scaled = grad * vecs[0:1, :]
                 mean_one = jnp.mean(scaled, axis=-1, keepdims=True)
                 mean_two = jnp.mean(scaled * xhat, axis=-1, keepdims=True)
                 whole = given + spread * (scaled - mean_one - xhat * mean_two)
                 gf_ref[rows, :] = whole
-                sums_ref[0:8, :] += fold(grad * xhat)
-                sums_ref[8:16, :] += fold(grad)
-                sums_ref[16:24, :] += fold(given)
-                sums_ref[24:32, :] += fold(whole)
+                sums[0:8, :] += fold(grad * xhat)
+                sums[8:16, :] += fold(whole)
+                sums[16:24, :] += fold(grad)
+                sums[24:32, :] += fold(given)
                 for w in range(QUAD):
                     for r in range(window):
                         ref, skip = piece(band, r, j * QUAD * window, w, window, half)
@@ -455,9 +530,11 @@
             unwrap_band(band, live, half, width, window, least)
             own_ref[page] = band[:half, :width].astype(B16)
             next_ref[page] = band[half:, :width].astype(B16)
-
-
-def mlp(live, out_grad, halo, n2, first, weights_in, weights_out, bup, vecs, least, share):
+        for k in range(4):
+            lay_lines(early_ref, (2 + k) * lines, jnp.sum(sums[8 * k : 8 * k + 8, :], axis=0, keepdims=True))
+
+
+def mlp(live, out_grad, halo, n2, first, weights_in, weights_out, gains, biases, least, share, lines):
     pages, window, width, model = out_grad.shape
     half = window // 2
     tokens = n2.shape[0]
@@ -477,28 +554,29 @@
             whole(first),
             pl.BlockSpec((model, MLP_COLS), lambda c: (0, c + skip)),
             pl.BlockSpec((MLP_COLS, model), lambda c: (c, 0)),
-            pl.BlockSpec((1, MLP_COLS), lambda c: (0, c)),
-            whole(vecs),
+            whole(gains),
+            whole(biases),
         ],
         out_specs=[
             pl.BlockSpec((model, MLP_COLS), lambda c: (0, c)),
             pl.BlockSpec((model * MLP_COLS // hidden, hidden), lambda c: (c, 0)),
-            pl.BlockSpec((1, MLP_COLS), lambda c: (0, c)),
             pl.BlockSpec((tokens, model), lambda c: (0, 0), pipeline_mode=once),
             pl.BlockSpec(band_block, lambda c: (0, 1, 0, 0), pipeline_mode=once),
             pl.BlockSpec(band_block, lambda c: (0, 0, 0, 0), pipeline_mode=once),
-            pl.BlockSpec((32, model), lambda c: (0, 0)),
+            pl.BlockSpec((lines, 128), lambda c: (0, 0)),
         ],
         out_shape=[
             jax.ShapeDtypeStruct((model, hidden), B16),
             jax.ShapeDtypeStruct((model, hidden), B16),
-            jax.ShapeDtypeStruct((1, hidden), F32),
             jax.ShapeDtypeStruct((tokens, model), F32),
             jax.ShapeDtypeStruct(out_grad.shape, B16),
             jax.ShapeDtypeStruct(band_block, B16),
-            jax.ShapeDtypeStruct((32, model), F32),
+            jax.ShapeDtypeStruct((lines, 128), F32),
         ],
         scratch_shapes=[
+            pltpu.VMEM((8, MLP_COLS), F32),
+            pltpu.VMEM((8, model), F32),
+            pltpu.VMEM((32, model), F32),
             pltpu.VMEM((window, width + 8, model), F32),
             pltpu.VMEM((tokens, model), B16),
             pltpu.VMEM((tokens, model), F32),
@@ -507,7 +585,7 @@
             pltpu.VMEM((tokens, MLP_COLS), B16),
         ],
         compiler_params=pltpu.CompilerParams(vmem_limit_bytes=VMEM_LIMIT),
-    )(live, out_grad, halo, n2, first, weights_in, weights_out, bup, vecs)
+    )(live, out_grad, halo, n2, first, weights_in, weights_out, gains, biases)
 
 
 def table_sum(off_ref, grad_ref, out_ref, at, heads, chunks):
@@ -725,13 +803,11 @@
     probs_ref,
     att_ref,
     wproj_ref,
-    wqkv_ref,
-    vec_ref,
-    off_ref,
+    turned_ref,
+    gains_ref,
+    places_ref,
     early_ref,
-    suma_ref,
-    sumu_ref,
-    sumo_ref,
+    sum_ref,
     small_ref,
     own_ref,
     mixed_halo_ref,
@@ -750,6 +826,7 @@
     dwp,
     compact,
     dscore,
+    dscores,
     dbqkv,
     sums,
     dwa,
@@ -761,23 +838,30 @@
     slots = window * window
     size_head = model // heads
     sweep, page, quad = pl.program_id(0), pl.program_id(1), pl.program_id(2)
-    quads = pl.num_programs(2)
+    quads = width // window // QUAD
     step = page * quads + quad
     live = live_ref[page]
-    pairs = heads // 2
+    pairs = heads // 4
     pair = 2 * size_head
+    part_rows = model // 2
+    lines = model // 128
+    cols = 2 * model
     big = Exchange(devices[0], devices[1] // 2, share, rest[:7], rest[7:15])
     early = SmallExchange(big, (rest[15],) + rest[16:21], rest[21:23])
     late = SmallExchange(big, (rest[23],) + rest[24:29], rest[29:31])
     local, halo_send, halo_recv = rest[31:]
     row = lax.axis_index("rows")
     behind, ahead = lax.rem(row + devices[1] - 1, devices[1]), lax.rem(row + 1, devices[1])
-    matrices = (dwa, up_ref, out_ref)
+    matrices = [dwa.at[0], dwa.at[1]]
+    for ref in (up_ref, out_ref):
+        for h in range(ref.shape[1] // cols):
+            matrices.append(ref.at[:, pl.ds(h * cols, cols)])
+    outer = range(2, len(matrices))
 
     def fetch(m):
         return [
             pltpu.make_async_copy(
-                big.rows_of(matrices[m], z, big.core), own1.at[m - 1, z], local.at[m - 1, z]
+                big.rows_of(matrices[m], z, big.core), own1.at[m - 2, z], local.at[m - 2, z]
             )
             for z in range(big.chips)
         ]
@@ -785,9 +869,14 @@
     def mixed_copy():
         return remote(mixed_ref, mixed_halo_ref, halo_send.at[0], halo_recv.at[0], {"rows": ahead})
 
-    def patch_copy(p):
+    def edge_at(j):
+        return 0 if j == 0 else width + 8 if j == quads else (j * QUAD * window + half) // 16 * 16
+
+    def patch_copy(p, j):
+        cut = pl.ds(edge_at(j), edge_at(j + 1) - edge_at(j))
+        k = 1 + p * quads + j
         return remote(
-            edge.at[p], patch_halo_ref.at[p], halo_send.at[1 + p], halo_recv.at[1 + p], {"rows": ahead}
+            edge.at[p, :, cut, :], patch_halo_ref.at[p, :, cut, :], halo_send.at[k], halo_recv.at[k], {"rows": ahead}
         )
 
     def moment(at_sweep, at_step):
@@ -802,49 +891,83 @@
         for peer in peers:
             pl.semaphore_signal(barrier, inc=1, device_id=peer, device_id_type=MESH)
         pl.semaphore_wait(barrier, len(peers))
-        for m in (1, 2):
+        for m in outer:
             big.start_one(m, matrices[m])
             start(fetch(m))
         mixed_copy().start()
+        early.mine[...] = early_ref[...]
         for ref in (bdq, bdk, bdo, stacked, beside, gbp, dwq, dwp, dbqkv, dscore, sums):
             ref[...] = jnp.zeros_like(ref)
 
-    last = pages * (width // window // QUAD) - 1
-    for m, (at_two, at_three, at_four) in ((1, (1, 3, 4)), (2, (1, 4, 5))):
-
-        @pl.when(moment(0, at_two))
+    def flush(h):
+        for part in range(3):
+            rows = slice(part * part_rows, part * part_rows + part_rows)
+            dwa[h, :, rows] = dwq[rows, :].T.astype(B16)
+        dwa[h, :, 3 * part_rows :] = dwp[:, h * part_rows : (h + 1) * part_rows].astype(B16)
+        big.start_one(h, matrices[h])
+        for k, part in enumerate((0, 2)):
+            total = jnp.sum(dbqkv[part * part_rows : (part + 1) * part_rows, :].T, axis=0, keepdims=True)
+            lay_lines(early.mine, lines * k + h * (lines // 2), total)
+        dscores[h * heads // 2 : (h + 1) * heads // 2] = dscore[...]
+        if h == 0:
+            for ref in (dwq, dbqkv, dscore):
+                ref[...] = jnp.zeros_like(ref)
+
+    def two(m):
+        if m >= 2:
+            wait(fetch(m))
+            big.start_two(m, matrices[m], lambda z: own1.at[m - 2, z])
+        else:
+            big.start_two(m, matrices[m], lambda z: big.rows_of(matrices[m], z, big.core))
+
+    def table():
+        chunks = -(-((2 * window - 1) ** 2) // 128)
+        table_sum(places_ref, dscores, early.mine, early.mine.shape[0] - heads * chunks, heads, chunks)
+        early.start_one()
+
+    plan = {
+        (0, 2): [(two, 2), (two, 3)],
+        (0, 4): [(two, 4), (two, 5)],
+        (1, 0): [(flush, 0)],
+        (1, 1): [(big.start_three, 2), (big.start_three, 3), (two, 0)],
+        (1, 4): [(big.start_three, 4), (big.start_three, 5)],
+        (2, 0): [(flush, 1), (big.start_four, 2), (big.start_four, 3), (big.start_three, 0)],
+        (2, 1): [(two, 1), (big.start_four, 4), (big.start_four, 5)],
+        (2, 2): [(lambda _: table(), 0)],
+        (2, 3): [(big.start_four, 0)],
+        (2, 4): [(lambda _: early.start_two(), 0)],
+    }
+    for (at_sweep, at_step), acts in plan.items():
+
+        @pl.when(moment(at_sweep, at_step))
         def _():
-            wait(fetch(m))
-            big.start_two(m, matrices[m], lambda z: own1.at[m - 1, z])
-
-        @pl.when(moment(0, at_three))
-        def _():
-            big.start_three(m)
-
-        @pl.when(moment(0, at_four))
-        def _():
-            big.start_four(m)
-
-    @pl.when(sweep == 0)
+            for act, m in acts:
+                act(m)
+
+    @pl.when(sweep < 2)
     def _():
         for w in range(QUAD):
             gbp[SLOT * w : SLOT * w + slots, :] = gf_ref[slots * w : slots * w + slots, :].astype(B16)
-        datt[...] = dot(wproj_ref[...], gbp[...], "NT").astype(B16)
-        dwp[...] += dot(att_ref[...], gbp[...])
+        mine = pl.ds(pl.multiple_of(jnp.minimum(sweep, 1) * part_rows, part_rows), part_rows)
+        datt[...] = dot(wproj_ref[mine, :], gbp[...], "NT").astype(B16)
+
+        @pl.when(sweep == 0)
+        def _():
+            dwp[...] += dot(att_ref[...], gbp[...])
+
         ratio = size_head**-0.5
-        target = dqkv.at[step]
+        target = dqkv.at[step, jnp.minimum(sweep, 1)]
 
         def score(w, g):
             low = pair * g
             lanes = slice(SLOT * w, SLOT * w + SLOT)
             for j in range(2):
                 at = slice(low + size_head * j, low + size_head * (j + 1))
-                keys = slice(model + low + size_head * j, model + low + size_head * (j + 1))
                 cols = slice(SLOT * j, SLOT * j + SLOT)
                 bdo[w % 3, at, cols] = datt[at, lanes]
-                bdq[w % 3, at, cols] = qkv_ref[at, lanes]
-                bdk[w % 3, at, cols] = qkv_ref[keys, lanes]
-            values = qkv_ref[2 * model + low : 2 * model + low + pair, SLOT * w : SLOT * w + KEYS]
+                bdq[w % 3, at, cols] = qkv_ref[0, at, lanes]
+                bdk[w % 3, at, cols] = qkv_ref[1, at, lanes]
+            values = qkv_ref[2, low : low + pair, SLOT * w : SLOT * w + KEYS]
             dprobs[w % 2, g] = dot(values, bdo[w % 3, low : low + pair, :], "TN")
 
         def soften(w, g):
@@ -865,9 +988,9 @@
             got = dot(bdk[w % 3, rows, :], stacked[w % 2, g]) * ratio
             target[low : low + pair, lanes] = got.astype(B16)
             got = dot(bdq[w % 3, rows, :], beside[w % 2, g], "NT") * (1.0 / LOG2E)
-            target[model + low : model + low + pair, lanes] = got.astype(B16)
+            target[part_rows + low : part_rows + low + pair, lanes] = got.astype(B16)
             got = dot(bdo[w % 3, rows, :], probs_ref[w, g], "NT")
-            target[2 * model + low : 2 * model + low + pair, lanes] = got.astype(B16)
+            target[2 * part_rows + low : 2 * part_rows + low + pair, lanes] = got.astype(B16)
 
         for stage in range(QUAD + 2):
             for g in range(pairs):
@@ -878,57 +1001,22 @@
                 if stage >= 2:
                     attend(stage - 2, g)
 
-        n1 = n1_ref[...]
-        for part in range(3):
-            rows = slice(part * model, part * model + model)
-            grad = dqkv[step, rows, :]
-            dwq[rows, :] += dot(grad, n1)
-            wide = grad.astype(F32)
-            both = wide[:, :SLOT]
-            for w in range(1, QUAD):
-                both = both + wide[:, SLOT * w : SLOT * w + SLOT]
-            dbqkv[rows, :] += both
-
-    @pl.when(moment(1, 0))
+        grad = target[...]
+        dwq[...] += dot(grad, n1_ref[...])
+        wide = grad.astype(F32)
+        both = wide[:, :SLOT]
+        for w in range(1, QUAD):
+            both = both + wide[:, SLOT * w : SLOT * w + SLOT]
+        dbqkv[...] += both
+
+    @pl.when(sweep == 2)
     def _():
-        dwa[:, 3 * model :] = dwp[...].astype(B16)
-        for part in range(3):
-            rows = slice(part * model, part * model + model)
-            dwa[:, rows] = dwq[rows, :].T.astype(B16)
-        big.start_one(0, dwa)
-        early.mine[...] = early_ref[...]
-        lines = model // 128
-        for k, part in enumerate((0, 2)):
-            total = jnp.sum(dbqkv[part * model : part * model + model, :].T, axis=0, keepdims=True)
-            for i in range(lines):
-                early.mine[lines * k + i : lines * k + i + 1, :] = total[:, 128 * i : 128 * i + 128]
-
-    @pl.when(moment(1, 1))
-    def _():
-        big.start_two(0, dwa, lambda z: big.rows_of(dwa, z, big.core))
-
-    @pl.when(moment(1, 2))
-    def _():
-        chunks = -(-(2 * window - 1) ** 2 // 128)
-        table_sum(off_ref, dscore, early.mine, early.mine.shape[0] - heads * chunks, heads, chunks)
-        early.start_one()
-
-    @pl.when(moment(1, 3))
-    def _():
-        early.start_two()
-
-    @pl.when(moment(1, 4))
-    def _():
-        early.start_three()
-
-    @pl.when(sweep == 1)
-    def _():
-        dn1 = dot(dqkv[step], wqkv_ref[...], "TN")
+        dn1 = dot(dqkv[step, 0], turned_ref[0], "TN") + dot(dqkv[step, 1], turned_ref[1], "TN")
         for w in range(QUAD):
             compact[slots * w : slots * w + slots, :] = dn1[SLOT * w : SLOT * w + slots, :]
         grad = compact[...]
         xhat, spread = norm_stats(x_ref[...].astype(F32))
-        scaled = grad * vec_ref[0:1, :]
+        scaled = grad * gains_ref[0:1, :]
         mean_one = jnp.mean(scaled, axis=-1, keepdims=True)
         mean_two = jnp.mean(scaled * xhat, axis=-1, keepdims=True)
         sums[0:8, :] += fold(grad * xhat)
@@ -941,60 +1029,67 @@
                 ref[skip : skip + window, :] = compact[at : at + window, :]
 
     for p in range(pages):
-
-        @pl.when(jnp.logical_and(sweep == 1, jnp.logical_and(page == p, quad == quads - 1)))
-        def _():
-            unwrap_band(band, live, half, width, window, least)
-            edge[p] = band[half:, :width].astype(B16)
-            patch_copy(p).start()
-            own_ref[0] = band[:half, :width].astype(B16)
-
-    @pl.when(moment(1, last))
+        for j in range(quads):
+
+            @pl.when(moment(2, p * quads + j))
+            def _():
+                cut = slice(edge_at(j), edge_at(j + 1))
+                edge[p, :, cut, :] = band[half:, cut, :].astype(B16)
+                patch_copy(p, j).start()
+                if j == quads - 1:
+                    unwrap_band(band, live, half, width, window, least)
+                    own_ref[0] = band[:half, :width].astype(B16)
+
+    @pl.when(moment(2, pages * quads - 1))
     def _():
-        big.start_three(0)
-        lines = model // 128
+        big.start_three(1)
         for k in range(2):
-            total = jnp.sum(sums[8 * k : 8 * k + 8, :], axis=0, keepdims=True)
-            for i in range(lines):
-                late.mine[lines * k + i : lines * k + i + 1, :] = total[:, 128 * i : 128 * i + 128]
+            lay_lines(late.mine, lines * k, jnp.sum(sums[8 * k : 8 * k + 8, :], axis=0, keepdims=True))
         late.start_one()
-        for m, ref in ((1, sumu_ref), (2, sumo_ref)):
-            big.finish(m, ref)
+        early.start_three()
+        for m in outer:
+            big.finish(m, sum_ref.at[m])
+        big.finish(0, sum_ref.at[0])
         late.start_two()
+        big.start_four(1)
+        late.start_three()
         early.finish(small_ref, LATE)
-        big.start_four(0)
-        late.start_three()
         mixed_copy().wait()
         late.finish(small_ref, 0)
-        big.finish(0, suma_ref)
+        big.finish(1, sum_ref.at[1])
         for p in range(pages):
-            patch_copy(p).wait()
+            for j in range(quads):
+                patch_copy(p, j).wait()
 
 
 def attn_backward(
-    live, dwup, dwout, mixed_next, gf, x, n1, qkv, probs, att, wproj, wqkv, vecs, off, early, shape, heads, least, share
+    live, dwup, dwout, mixed_next, gf, x, n1, qkv, probs, att, weights_in, turned, gains, places, early, shape, heads, least, share
 ):
     pages, window, width, model = shape
     half = window // 2
     quads = width // window // QUAD
     slots = window * window
-    pairs = heads // 2
+    pairs = heads // 4
+    part_rows = model // 2
     devices = (lax.axis_size("page"), lax.axis_size("rows"))
     chips = devices[1] // 2
     hidden = dwup.shape[1]
-    cols = hidden // devices[0]
+    wide = 2 * model
+    cols = wide // devices[0]
     once = pl.Buffered(1)
     whole = lambda a: pl.BlockSpec(a.shape, lambda s, p, j: (0,) * a.ndim, pipeline_mode=once)
     held = lambda dims: pl.BlockSpec(dims, lambda s, p, j: (0,) * len(dims), pipeline_mode=once)
     anywhere = pl.BlockSpec(memory_space=pl.ANY)
     at = lambda p, j: p * quads + j
     last = pages * quads - 1
+    both = lambda s, p, j: jnp.where(s < 2, at(p, j), last)
     first = lambda s, p, j: jnp.where(s == 0, at(p, j), last)
-    second = lambda s, p, j: jnp.where(s == 0, 0, at(p, j))
-    own_at = lambda s, p, j: (jnp.where(s == 0, 0, p), 1, 0, 0)
+    third = lambda s, p, j: jnp.where(s == 2, at(p, j), 0)
+    side = lambda s: jnp.minimum(s, 1)
+    own_at = lambda s, p, j: (jnp.where(s == 2, p, 0), 0, 0, 0)
     dma = pltpu.SemaphoreType.DMA
     vmem = pltpu.VMEM
-    n = 3
+    n = 2 + 2 * hidden // wide
     lines = early.shape[0]
 
     def small_scratch(rows):
@@ -1013,63 +1108,60 @@
         functools.partial(
             attn_backward_kernel, (window, half, width, model, heads, least, pages, devices, share)
         ),
-        grid=(2, pages, quads),
+        grid=(3, pages, quads),
         in_specs=[
             pl.BlockSpec(memory_space=pltpu.SMEM),
             anywhere,
             anywhere,
             anywhere,
             pl.BlockSpec((QUAD * slots, model), lambda s, p, j: (at(p, j), 0)),
-            pl.BlockSpec((QUAD * slots, model), lambda s, p, j: (second(s, p, j), 0)),
-            pl.BlockSpec((QUAD * SLOT, model), lambda s, p, j: (first(s, p, j), 0)),
-            pl.BlockSpec((3 * model, QUAD * SLOT), lambda s, p, j: (0, first(s, p, j))),
-            pl.BlockSpec((QUAD, pairs, SLOT, 2 * SLOT), lambda s, p, j: (first(s, p, j), 0, 0, 0)),
+            pl.BlockSpec((QUAD * slots, model), lambda s, p, j: (third(s, p, j), 0)),
+            pl.BlockSpec((QUAD * SLOT, model), lambda s, p, j: (both(s, p, j), 0)),
+            pl.BlockSpec((3, part_rows, QUAD * SLOT), lambda s, p, j: (0, side(s), both(s, p, j))),
+            pl.BlockSpec((QUAD, pairs, SLOT, 2 * SLOT), lambda s, p, j: (both(s, p, j), side(s), 0, 0)),
             pl.BlockSpec((model, QUAD * SLOT), lambda s, p, j: (0, first(s, p, j))),
-            whole(wproj),
-            whole(wqkv),
-            whole(vecs),
-            whole(off),
+            pl.BlockSpec((model, model), lambda s, p, j: (0, 3), pipeline_mode=once),
+            whole(turned),
+            whole(gains),
+            whole(places),
             whole(early),
         ],
         out_specs=[
-            held((share, hidden)),
-            held((share, hidden)),
-            held((share, hidden)),
+            held((n, share, wide)),
             held((LATE + lines, 128)),
             pl.BlockSpec((1, half, width, model), own_at),
             anywhere,
             anywhere,
         ],
         out_shape=[
-            jax.ShapeDtypeStruct((share, hidden), B16),
-            jax.ShapeDtypeStruct((share, hidden), B16),
-            jax.ShapeDtypeStruct((share, hidden), B16),
+            jax.ShapeDtypeStruct((n, share, wide), B16),
             jax.ShapeDtypeStruct((LATE + lines, 128), F32),
-            jax.ShapeDtypeStruct(shape, B16),
             jax.ShapeDtypeStruct((pages, half, width, model), B16),
             jax.ShapeDtypeStruct((pages, half, width, model), B16),
+            jax.ShapeDtypeStruct((pages, half, width + 8, model), B16),
         ],
         scratch_shapes=[
             vmem((window, width + 8, model), F32),
             vmem((QUAD * SLOT, model), B16),
-            vmem((model, QUAD * SLOT), B16),
+            vmem((part_rows, QUAD * SLOT), B16),
             vmem((2, pairs, KEYS, 2 * SLOT), F32),
-            vmem((3, model, 2 * SLOT), B16),
-            vmem((3, model, 2 * SLOT), B16),
-            vmem((3, model, 2 * SLOT), B16),
+            vmem((3, part_rows, 2 * SLOT), B16),
+            vmem((3, part_rows, 2 * SLOT), B16),
+            vmem((3, part_rows, 2 * SLOT), B16),
             vmem((2, pairs, 2 * SLOT, SLOT), B16),
             vmem((2, pairs, SLOT, 2 * SLOT), B16),
-            vmem((pages * quads, 3 * model, QUAD * SLOT), B16),
-            vmem((3 * model, model), F32),
+            vmem((pages * quads, 2, 3 * part_rows, QUAD * SLOT), B16),
+            vmem((3 * part_rows, model), F32),
             vmem((model, model), F32),
             vmem((QUAD * slots, model), F32),
+            vmem((heads // 2, KEYS, SLOT), F32),
             vmem((heads, KEYS, SLOT), F32),
-            vmem((3 * model, SLOT), F32),
+            vmem((3 * part_rows, SLOT), F32),
             vmem((16, model), F32),
-            vmem((model, hidden), B16),
-            vmem((pages, half, width, model), B16),
-            vmem((2, chips, share, hidden), B16),
-            vmem((n, chips, share, hidden), B16),
+            vmem((2, model, wide), B16),
+            vmem((pages, half, width + 8, model), B16),
+            vmem((n - 2, chips, share, wide), B16),
+            vmem((n, chips, share, wide), B16),
             vmem((n, devices[0], chips, share, cols), B16),
             vmem((n, devices[0], chips, share, cols), B16),
             vmem((n, chips, share, cols), B16),
@@ -1087,11 +1179,114 @@
         ]
         + small_scratch(lines)
         + small_scratch(LATE)
-        + [dma((2, chips)), dma((1 + pages,)), dma((1 + pages,))],
+        + [dma((n - 2, chips)), dma((1 + pages * quads,)), dma((1 + pages * quads,))],
         compiler_params=pltpu.CompilerParams(
-            vmem_limit_bytes=63 * 2**20, collective_id=0, has_side_effects=True
+            vmem_limit_bytes=62 * 2**20, collective_id=0, has_side_effects=True
         ),
-    )(live, dwup, dwout, mixed_next, gf, x, n1, qkv, probs, att, wproj, wqkv, vecs, off, early)
+    )(live, dwup, dwout, mixed_next, gf, x, n1, qkv, probs, att, weights_in, turned, gains, places, early)
+
+
+def finish_kernel(
+    sizes,
+    live_ref,
+    sum_ref,
+    min_ref,
+    fin_ref,
+    sin_ref,
+    mout_ref,
+    fout_ref,
+    sout_ref,
+    above_ref,
+    own_ref,
+    edge_ref,
+    _,
+    mixed_ref,
+    patch_ref,
+    new_in_ref,
+    moment_in_ref,
+    square_in_ref,
+    new_out_ref,
+    moment_out_ref,
+    square_out_ref,
+    band,
+    grad_in,
+):
+    window, half, width, least = sizes
+    step = pl.program_id(0)
+    model = band.shape[2]
+    part_rows = model // 2
+    for s in range(FINISH_STEPS):
+
+        @pl.when(step == s)
+        def _():
+            if s < 2:
+                for h in range(2):
+                    for part in range(2):
+                        at = part * model + h * part_rows
+                        from_at = (2 * s + part) * part_rows
+                        grad_in[:, at : at + part_rows] = sum_ref[h, :, from_at : from_at + part_rows].astype(F32)
+            else:
+                grad_in[...] = sum_ref[s].astype(F32)
+            cols = slice(model * (s % 2), model * (s % 2 + 1))
+            grad = sum_ref[4 + s // 2, :, cols].astype(F32)
+            new, moment, square = adam_update(mout_ref[...], fout_ref[...], sout_ref[...], grad)
+            new_out_ref[...], moment_out_ref[...], square_out_ref[...] = new, moment, square
+            if s % 2 == 0:
+                mixed_ref[...] = above_ref[...]
+                band[...] = edge_ref[0].astype(F32)
+                unwrap_band(band, live_ref[s // 2], half, width, window, least)
+                patch_ref[0] = band[:, :width].astype(B16)
+            else:
+                patch_ref[0] = own_ref[0]
+
+    new, moment, square = adam_update(min_ref[...], fin_ref[...], sin_ref[...], grad_in[...])
+    new_in_ref[...], moment_in_ref[...], square_in_ref[...] = new, moment, square
+
+
+FINISH_STEPS = 4
+
+
+def finish(live, sums, master_in, first_in, second_in, master_out, first_out, second_out, above, own, edge, mixed, least):
+    pages, window, width, model = mixed.shape
+    half = window // 2
+    share, wide = master_in.shape
+    tall = master_out.shape[0]
+    cols = pl.BlockSpec((share, wide // FINISH_STEPS), lambda s: (0, s))
+    rows = pl.BlockSpec((tall // FINISH_STEPS, model), lambda s: (s, 0))
+    page = lambda s: (s // 2, 0, 0, 0)
+    band = (1, half, width, model)
+    like = lambda a: jax.ShapeDtypeStruct(a.shape, a.dtype)
+    return pl.pallas_call(
+        functools.partial(finish_kernel, (window, half, width, least)),
+        grid=(FINISH_STEPS,),
+        in_specs=[
+            pl.BlockSpec(memory_space=pltpu.SMEM),
+            pl.BlockSpec(sums.shape, lambda s: (0, 0, 0), pipeline_mode=pl.Buffered(1)),
+            cols,
+            cols,
+            cols,
+            rows,
+            rows,
+            rows,
+            pl.BlockSpec(band, page),
+            pl.BlockSpec(band, page),
+            pl.BlockSpec((1, half, width + 8, model), page),
+            pl.BlockSpec(memory_space=pl.ANY),
+        ],
+        out_specs=[
+            pl.BlockSpec(band, page),
+            pl.BlockSpec(band, lambda s: (s // 2, s % 2, 0, 0)),
+        ]
+        + [cols] * 3
+        + [rows] * 3,
+        out_shape=[like(mixed), like(mixed)] + [like(master_in)] * 3 + [like(master_out)] * 3,
+        scratch_shapes=[
+            pltpu.VMEM((half, width + 8, model), F32),
+            pltpu.VMEM((share, wide // FINISH_STEPS), F32),
+        ],
+        input_output_aliases={11: 0},
+        compiler_params=pltpu.CompilerParams(vmem_limit_bytes=VMEM_LIMIT),
+    )(live, sums, master_in, first_in, second_in, master_out, first_out, second_out, above, own, edge, mixed)
 
 
 def adam_update(master, first, second, grad):
@@ -1136,66 +1331,33 @@
     labels = region_ids.reshape(pages, window, count, window).transpose(0, 2, 1, 3)
     labels = labels.reshape(pages * count // QUAD, QUAD, slots).astype(F32)
     labels = jnp.pad(labels, ((0, 0), (0, 8 - QUAD), (0, SLOT - slots)), constant_values=-1.0)
-    off = offset_index.T
-    off_gather = jnp.pad(off, ((0, KEYS - slots), (0, SLOT - slots)))
-    off_scatter = jnp.pad(off, ((0, KEYS - slots), (0, SLOT - slots)), constant_values=-1)
+    bias_lines = biases.reshape(-1, 128)
+    lines = model // 128
     table_lanes = -(-table_rows // 128) * 128
-    tab = jnp.pad(bias_table.T * LOG2E, ((0, 0), (0, table_lanes - table_rows)))
-    wqkv = weights_in[:, : 3 * model].T
-    wproj = weights_in[:, 3 * model : 4 * model]
-    bias_qkv = jnp.concatenate(
-        [biases[model : 2 * model], jnp.zeros((model,), F32), biases[2 * model : 3 * model]]
-    )[:, None]
-    zero = jnp.zeros((model,), F32)
-    vec_one = jnp.stack(
-        [
-            norm_gains[0],
-            biases[:model],
-            biases[3 * model : 4 * model],
-            norm_gains[1],
-            biases[4 * model : 5 * model],
-            zero,
-            zero,
-            zero,
-        ]
+    early_lines = EARLY_UP * lines + hidden // 128 + table_lanes * heads // 128
+
+    x, n1, qkv, probs, att, first, n2, below_grad, turned, places = attn_forward(
+        page_windows, patches, out_grad, labels, offset_index, bias_table, weights_in, norm_gains, bias_lines, least
     )
-    vec_two = jnp.stack([norm_gains[1], biases[5 * model : 6 * model]] + [zero] * 6)
-
-    x, n1, qkv, probs, att, first, n2, below_grad = attn_forward(
-        page_windows, patches, out_grad, labels, off_gather, tab, wqkv, bias_qkv, wproj, vec_one, least
+    dwup, dwout, gf, mixed_own, mixed_next, early = mlp(
+        page_windows, out_grad, below_grad, n2, first, weights_in, weights_out, norm_gains, bias_lines,
+        least, master_in.shape[0], early_lines,
     )
-    dwup, dwout, dbup, gf, mixed_own, mixed_next, sums_two = mlp(
-        page_windows, out_grad, below_grad, n2, first, weights_in, weights_out,
-        biases[None, 6 * model :], vec_two, least, master_in.shape[0],
+    sums, small, patch_own, above, edge = attn_backward(
+        page_windows, dwup, dwout, mixed_next, gf, x, n1, qkv, probs, att, weights_in, turned, norm_gains,
+        places, early, patches.shape, heads, least, master_in.shape[0],
     )
-    sums_two = sums_two.reshape(4, 8, model).sum(1)
-    lines = model // 128
-    early = jnp.concatenate(
-        [
-            jnp.zeros((2 * lines, 128), F32),
-            sums_two[jnp.array([0, 3, 1, 2])].reshape(4 * lines, 128),
-            dbup.reshape(-1, 128),
-            jnp.zeros((table_lanes * heads // 128, 128), F32),
-        ]
+    mixed, patch_grad, new_in, moment_in, square_in, new_out, moment_out, square_out = finish(
+        page_windows, sums, master_in, first_in, second_in, master_out, first_out, second_out, above, patch_own,
+        edge, mixed_own, least,
     )
-    total_a, total_up, total_out, small, patch_own, above, above_grad = attn_backward(
-        page_windows, dwup, dwout, mixed_next, gf, x, n1, qkv, probs, att, wproj, wqkv, vec_one,
-        off_scatter, early, patches.shape, heads, least, master_in.shape[0],
-    )
-    mixed = lax.dynamic_update_slice(mixed_own, above, (0, 0, 0, 0))
-    patch_grad = lax.dynamic_update_slice(patch_own, above_grad, (0, 0, 0, 0))
     small_at = [0, 4, 1, 2, 3, 5, 6, 7]
     table_at = small.shape[0] - table_lanes * heads // 128
     total_table = small[table_at:].reshape(table_lanes // 128, heads, 128).transpose(0, 2, 1)
     total_table = total_table.reshape(table_lanes, heads)[:table_rows]
     head = [small[lines * k : lines * k + lines] for k in small_at] + [small[8 * lines : table_at]]
     total_small = jnp.concatenate([jnp.concatenate(head).reshape(-1), total_table.reshape(-1)])
-    part_in = jnp.concatenate([total_a, total_up], axis=1).astype(F32)
-    ratio = hidden // model
-    total_out = total_out.reshape(-1, ratio, model).transpose(1, 0, 2).reshape(-1, model).astype(F32)
     small_master = jnp.concatenate([norm_gains.reshape(-1), biases, bias_table.reshape(-1)])
-    new_in, moment_in, square_in = adam_update(master_in, first_in, second_in, part_in)
-    new_out, moment_out, square_out = adam_update(master_out, first_out, second_out, total_out)
     new_small, moment_small, square_small = adam_update(
         small_master, first_small, second_small, total_small
     )

time: 220 us -> 194 us (0.88)
  local copies, waits for them, and re-layouts: 18.1 us -> 6.97 us
  other arithmetic: 10.6 us -> 1.39 us
  Pallas kernels: 190 us -> 183 us
    pallas_call x1, Pallas kernels: 91.3 us -> 74.5 us  [attn_backward(): pl.pallas_call(functools.partial(attn_backward_kernel, (window, half, wid...]
    pallas_call x0 -> x1, Pallas kernels: none -> 9.02 us  [finish(): pl.pallas_call(functools.partial(finish_kernel, (window, half, width, lea...]
    sub x3 -> x1, other arithmetic: 7.65 us -> 0.68 us  [adam_update(): master - LEARN_RATE * (moment / fix_one / (jnp.sqrt(square / fix_two) + A...]
    slice x6 -> x0, local copies, waits for them, and re-layouts: 4.13 us -> none  [the longest x1 1.87 us: shards(): wproj = weights_in[:, 3 * model:4 * model]]
where the time goes in v3:
time: 194 us; the launch traced here: 192 us
  Pallas kernels  183 us (94%)
  local copies, waits for them, and re-layouts  6.97 us (4%)
    pallas_call x1, Pallas kernels, attn_backward(): pl.pallas_call(functools.partial(attn_backward_kernel, (window, half, wid...  74.5 us
    pallas_call x1, Pallas kernels, mlp(): pl.pallas_call(functools.partial(mlp_kernel, (window, half, width, model,...  58 us
    pallas_call x1, Pallas kernels, attn_forward(): pl.pallas_call(functools.partial(attn_forward_kernel, (window, half, widt...  41.6 us
    pallas_call x1, Pallas kernels, finish(): pl.pallas_call(functools.partial(finish_kernel, (window, half, width, lea...  9.02 us

profile of v3, /device:TPU:0, one launch (start us, length us, event | category | flops | bytes accessed | tf_op | source)
XLA Modules:
  0.0 192.4 jit_solution(2642195152066411930)
XLA Ops:
  0.6 0.7 copy.37
  1.3 0.7 convert_element_type.12
  2.0 0.7 constant_dynamic-update-slice_fusion.1
  2.8 0.1 convert_element_type.13
  2.9 0.1 copy.32
  3.0 0.1 convert_element_type.15
  3.1 0.6 pad.4.label_ref
  3.7 0.9 copy.33.tab_ref
  4.6 0.0 copy-start
  4.6 0.1 reshape.49
  4.7 0.5 copy-done
  5.2 41.6 %shard_map.257 = (bf16[2400,512]{1,0:T(8,128)(2,1)}, bf16[3072,512]{1,0:T(8,128)(2,1)}, bf16[3,512,3072]{2,1,0:T(8,128)(2,1)}, bf16[24,8,128,256]{3,2,1,0:T(8,12...) custom-call(s32[2]{0:T(128)} %live_ref.7, ...), custom_call_target="tpu_custom_call" | custom-call | tf_op jit(solution)/shard_map/pallas_call | solution.py:320
  46.9 58.0 %shard_map.258 = (bf16[512,2048]{1,0:T(8,128)(2,1)}, bf16[512,2048]{1,0:T(8,128)(2,1)}, f32[2400,512]{1,0:T(8,128)}, bf16[2,10,120,512]{3,2,1,0:T(8,128)(2,1)}, ...) custom-call(s32[2]{0:T(128)} %live_ref.7, bf16[2,10,120,512]{3,2,1,0:T(8,128)(2,1)} %low_ref.3, ...), custom_call_target="tpu_custom_call" | custom-call | tf_op jit(solution)/shard_map/pallas_call | solution.py:546
  104.8 0.0 copy-start.1
  104.8 0.0 copy-start.2
  104.8 74.5 %shard_map.259 = (bf16[6,64,1024]{2,1,0:T(8,128)(2,1)}, f32[96,128]{1,0:T(8,128)}, bf16[2,5,120,512]{3,2,1,0:T(8,128)(2,1)}, bf16[2,5,120,512]{3,2,1,0:T(8,128)(2,1)}, bf16[2,5,128,512]{3,2,1,0:T(8,128)(2,1)}) custom-call(s32[2]{0:T(128)} %live_ref.7, bf16[512,2048]{1,0:T(8,128)(2,1)} %get-tuple-element.43.up_ref, ...), custom_call_target="tpu_custom_call" | custom-call | tf_op jit(solution)/shard_map/pallas_call | solution.py:1107
  179.3 0.7 fusion.2
  180.0 0.7 slice.27
  180.7 0.7 slice.28
  181.4 0.7 slice.29
  182.2 0.1 copy.36
  182.4 0.1 reshape.53
  182.5 0.0 copy-done.1
  182.5 0.0 copy-done.2
  182.5 0.7 multiply_subtract_fusion
  183.2 9.0 %shard_map.260 = (bf16[2,10,120,512]{3,2,1,0:T(8,128)(2,1)}, bf16[2,10,120,512]{3,2,1,0:T(8,128)(2,1)}, f32[64,4096]{1,0:T(8,128)}, f32[64,4096]{1,0:T(8,128)}, ...) custom-call(s32[2]{0:T(128)} %live_ref.7, ...), custom_call_target="tpu_custom_call", output_to_operand_aliasing={{0}: (11, {})} | custom-call | tf_op jit(solution)/shard_map/pallas_call | solution.py:1259
  (5 shorter events, 0.0 us)
Async XLA Ops:
  4.6 0.7 copy-start
  104.8 77.7 %copy-start.1 = (f32[11920]{0:T(1024)S(1)}, f32[11920]{0:T(1024)}, u32[]{:S(2)}) copy-start(f32[11920]{0:T(1024)} %param.34) | copy-start | bytes 143044
  104.8 77.7 %copy-start.2 = (f32[11920]{0:T(1024)S(1)}, f32[11920]{0:T(1024)}, u32[]{:S(2)}) copy-start(f32[11920]{0:T(1024)} %param.35) | copy-start | bytes 143044

commit v4 on v3

--- a/solution.py
+++ b/solution.py
@@ -36,17 +36,15 @@
     return lax.dot_general(left, right, (sides, ((), ())), preferred_element_type=F32)
 
 
-def load_band(band, low_ref, high_ref, live, half, width, window, least):
-    band[:half, :width] = low_ref[...].astype(F32)
-    band[half:, :width] = high_ref[...].astype(F32)
-    band[:, width:] = jnp.zeros((window, band.shape[1] - width, band.shape[2]), F32)
-    wrap_band(band, live, half, width, window, least)
-
-
-def wrap_band(band, live, half, width, window, least):
-    for count in range(least, width // window + 1):
-        at = slice(count * window, count * window + half)
-        band[:, at] = jnp.where(live == count, band[:, :half], band[:, at])
+def load_band(band, low_ref, high_ref, live, half, width, window, least, start=0, end=None):
+    end = width if end is None else end
+    band[:half, start:end] = low_ref[:, start:end].astype(F32)
+    band[half:, start:end] = high_ref[:, start:end].astype(F32)
+    if end == width:
+        band[:, width:] = jnp.zeros((window, band.shape[1] - width, band.shape[2]), F32)
+        for count in range(least, width // window + 1):
+            at = slice(count * window, count * window + half)
+            band[:, at] = jnp.where(live == count, band[:, :half], band[:, at])
 
 
 def unwrap_band(band, live, half, width, window, least):
@@ -160,17 +158,24 @@
     row = lax.axis_index("rows")
     behind, ahead = lax.rem(row + rows_count - 1, rows_count), lax.rem(row + 1, rows_count)
 
-    def halo_copy(p):
+    cut = -(-(QUAD * window + half) // 16) * 16
+
+    def halo_copy(p, k):
+        at = (pl.ds(0, cut), pl.ds(cut, width - cut))[k]
         return remote(
-            patches_ref.at[p, pl.ds(0, half)], halo.at[p], send.at[p], recv.at[p], {"rows": behind}
+            patches_ref.at[p, pl.ds(0, half), at],
+            halo.at[p, :, at],
+            send.at[pages * (1 + k) + p],
+            recv.at[pages * (1 + k) + p],
+            {"rows": behind},
         )
 
     def grad_copy(p):
         return remote(
             grads_ref.at[p, pl.ds(0, half)],
             grad_halo_ref.at[p],
-            send.at[pages + p],
-            recv.at[pages + p],
+            send.at[p],
+            recv.at[p],
             {"rows": behind},
         )
 
@@ -180,10 +185,7 @@
         for neighbour in (behind, ahead):
             pl.semaphore_signal(barrier, inc=1, device_id={"rows": neighbour}, device_id_type=MESH)
         pl.semaphore_wait(barrier, 2)
-        for p in range(pages):
-            halo_copy(p).start()
-        for p in range(pages):
-            grad_copy(p).start()
+        halo_copy(0, 0).start()
         vecs[...] = jnp.zeros_like(vecs)
         vecs[0:1, :] = gains_ref[0:1, :]
         lay_row(vecs, 1, biases_ref, 0, lines)
@@ -202,6 +204,7 @@
                         spread = jnp.broadcast_to(biases_ref[line : line + 1, :], (128, 128))
                         at = part * part_rows + 128 * i
                         column[h, at : at + 128, :] = spread.T
+        halo_copy(0, 1).start()
         square[...] = jnp.full_like(square, -1)
         square[:slots, :slots] = off_ref[...]
         places = square[...].T[:KEYS]
@@ -227,8 +230,21 @@
 
         @pl.when(jnp.logical_and(page == p, quad == 0))
         def _():
-            halo_copy(p).wait()
-            load_band(band, low_ref.at[0], halo.at[p], live, half, width, window, least)
+            halo_copy(p, 0).wait()
+            load_band(band, low_ref.at[0], halo.at[p], live, half, width, window, least, 0, cut)
+
+        @pl.when(jnp.logical_and(page == p, quad == 1))
+        def _():
+            halo_copy(p, 1).wait()
+            if p + 1 < pages:
+                for k in range(2):
+                    halo_copy(p + 1, k).start()
+            load_band(band, low_ref.at[0], halo.at[p], live, half, width, window, least, cut)
+
+    @pl.when(jnp.logical_and(page == (pages - 1) // 2, quad == 2))
+    def _():
+        for p in range(pages):
+            grad_copy(p).start()
 
     @pl.when(jnp.logical_and(page == pages - 1, quad == pl.num_programs(1) - 1))
     def _():
@@ -362,8 +378,8 @@
         ],
         scratch_shapes=[
             pltpu.VMEM((pages, half, width, model), B16),
-            pltpu.SemaphoreType.DMA((2 * pages,)),
-            pltpu.SemaphoreType.DMA((2 * pages,)),
+            pltpu.SemaphoreType.DMA((3 * pages,)),
+            pltpu.SemaphoreType.DMA((3 * pages,)),
             pltpu.VMEM((window, width + 8, model), F32),
             pltpu.VMEM((heads, KEYS, SLOT), F32),
             pltpu.VMEM((2, heads // 2, KEYS, 2 * SLOT), F32),
@@ -384,10 +400,10 @@
     )(live, patches, out_grad, patches, labels, off, tab, weights_in, weights_in, gains, biases)
 
 
-MLP_COLS = 512
-MLP_CHUNKS = 4
+MLP_COLS = 1024
+MLP_CHUNKS = 2
 MLP_ROWS = 480
-EARLY_UP = 6
+EARLY_UP = 8
 
 
 def mlp_kernel(
@@ -468,16 +484,8 @@
         up = dot(act, wout_ref[...])
         down = dot(grad_pre, wup_ref[...], "NT")
 
-        @pl.when(chunk == 0)
-        def _():
-            res[rows, :] = up
-            dn2[rows, :] = down
-
-        @pl.when(chunk > 0)
-        def _():
-            res[rows, :] += up
-            dn2[rows, :] += down
-
+        res[rows, :] = jnp.where(chunk == 0, 0.0, res[rows, :]) + up
+        dn2[rows, :] = jnp.where(chunk == 0, 0.0, dn2[rows, :]) + down
         return total + fold(grad_pre.astype(F32))
 
     total = lax.fori_loop(0, tokens // MLP_ROWS, body, jnp.zeros((8, cols), F32))
@@ -531,7 +539,7 @@
             own_ref[page] = band[:half, :width].astype(B16)
             next_ref[page] = band[half:, :width].astype(B16)
         for k in range(4):
-            lay_lines(early_ref, (2 + k) * lines, jnp.sum(sums[8 * k : 8 * k + 8, :], axis=0, keepdims=True))
+            lay_lines(early_ref, (4 + k) * lines, jnp.sum(sums[8 * k : 8 * k + 8, :], axis=0, keepdims=True))
 
 
 def mlp(live, out_grad, halo, n2, first, weights_in, weights_out, gains, biases, least, share, lines):
@@ -787,9 +795,6 @@
         copy.wait()
 
 
-LATE = 8
-
-
 def attn_backward_kernel(
     sizes,
     live_ref,
@@ -805,6 +810,7 @@
     wproj_ref,
     turned_ref,
     gains_ref,
+    biases_ref,
     places_ref,
     early_ref,
     sum_ref,
@@ -828,7 +834,7 @@
     dscore,
     dscores,
     dbqkv,
-    sums,
+    vecs,
     dwa,
     edge,
     own1,
@@ -848,8 +854,7 @@
     cols = 2 * model
     big = Exchange(devices[0], devices[1] // 2, share, rest[:7], rest[7:15])
     early = SmallExchange(big, (rest[15],) + rest[16:21], rest[21:23])
-    late = SmallExchange(big, (rest[23],) + rest[24:29], rest[29:31])
-    local, halo_send, halo_recv = rest[31:]
+    local, halo_send, halo_recv = rest[23:]
     row = lax.axis_index("rows")
     behind, ahead = lax.rem(row + devices[1] - 1, devices[1]), lax.rem(row + 1, devices[1])
     matrices = [dwa.at[0], dwa.at[1]]
@@ -896,7 +901,7 @@
             start(fetch(m))
         mixed_copy().start()
         early.mine[...] = early_ref[...]
-        for ref in (bdq, bdk, bdo, stacked, beside, gbp, dwq, dwp, dbqkv, dscore, sums):
+        for ref in (bdq, bdk, bdo, stacked, beside, gbp, dwq, dwp, dbqkv, dscore, vecs):
             ref[...] = jnp.zeros_like(ref)
 
     def flush(h):
@@ -907,7 +912,18 @@
         big.start_one(h, matrices[h])
         for k, part in enumerate((0, 2)):
             total = jnp.sum(dbqkv[part * part_rows : (part + 1) * part_rows, :].T, axis=0, keepdims=True)
-            lay_lines(early.mine, lines * k + h * (lines // 2), total)
+            lay_lines(early.mine, lines * (2 + k) + h * (lines // 2), total)
+        column = jnp.sum(dbqkv[...], axis=1, keepdims=True)
+        weights = turned_ref[h].astype(F32)
+        shifts = jnp.sum(weights * column, axis=0, keepdims=True)
+        gains = jnp.sum(weights * dwq[...], axis=0, keepdims=True)
+        vecs[0:1, :] += gains
+        vecs[1:2, :] += shifts
+        if h == 1:
+            lay_row(vecs, 2, biases_ref, 0, lines)
+            total = (vecs[0:1, :] - vecs[2:3, :] * vecs[1:2, :]) / gains_ref[0:1, :]
+            lay_lines(early.mine, 0, total)
+            lay_lines(early.mine, lines, vecs[1:2, :])
         dscores[h * heads // 2 : (h + 1) * heads // 2] = dscore[...]
         if h == 0:
             for ref in (dwq, dbqkv, dscore):
@@ -928,14 +944,12 @@
     plan = {
         (0, 2): [(two, 2), (two, 3)],
         (0, 4): [(two, 4), (two, 5)],
-        (1, 0): [(flush, 0)],
-        (1, 1): [(big.start_three, 2), (big.start_three, 3), (two, 0)],
-        (1, 4): [(big.start_three, 4), (big.start_three, 5)],
-        (2, 0): [(flush, 1), (big.start_four, 2), (big.start_four, 3), (big.start_three, 0)],
-        (2, 1): [(two, 1), (big.start_four, 4), (big.start_four, 5)],
-        (2, 2): [(lambda _: table(), 0)],
-        (2, 3): [(big.start_four, 0)],
-        (2, 4): [(lambda _: early.start_two(), 0)],
+        (1, 0): [(flush, 0), (big.start_three, 2), (big.start_three, 3)],
+        (1, 1): [(two, 0)],
+        (1, 4): [(big.start_three, 4), (big.start_three, 5), (big.start_four, 2), (big.start_four, 3)],
+        (2, 0): [(flush, 1), (big.start_three, 0)],
+        (2, 1): [(two, 1)],
+        (2, 5): [(big.start_four, 4), (big.start_four, 5), (big.start_four, 0)],
     }
     for (at_sweep, at_step), acts in plan.items():
 
@@ -1019,8 +1033,6 @@
         scaled = grad * gains_ref[0:1, :]
         mean_one = jnp.mean(scaled, axis=-1, keepdims=True)
         mean_two = jnp.mean(scaled * xhat, axis=-1, keepdims=True)
-        sums[0:8, :] += fold(grad * xhat)
-        sums[8:16, :] += fold(grad)
         compact[...] = gf_ref[...] + spread * (scaled - mean_one - xhat * mean_two)
         for w in range(QUAD):
             for r in range(window):
@@ -1042,20 +1054,16 @@
 
     @pl.when(moment(2, pages * quads - 1))
     def _():
+        table()
         big.start_three(1)
-        for k in range(2):
-            lay_lines(late.mine, lines * k, jnp.sum(sums[8 * k : 8 * k + 8, :], axis=0, keepdims=True))
-        late.start_one()
-        early.start_three()
+        early.start_two()
         for m in outer:
             big.finish(m, sum_ref.at[m])
         big.finish(0, sum_ref.at[0])
-        late.start_two()
+        early.start_three()
         big.start_four(1)
-        late.start_three()
-        early.finish(small_ref, LATE)
         mixed_copy().wait()
-        late.finish(small_ref, 0)
+        early.finish(small_ref, 0)
         big.finish(1, sum_ref.at[1])
         for p in range(pages):
             for j in range(quads):
@@ -1063,7 +1071,7 @@
 
 
 def attn_backward(
-    live, dwup, dwout, mixed_next, gf, x, n1, qkv, probs, att, weights_in, turned, gains, places, early, shape, heads, least, share
+    live, dwup, dwout, mixed_next, gf, x, n1, qkv, probs, att, weights_in, turned, gains, biases, places, early, shape, heads, least, share
 ):
     pages, window, width, model = shape
     half = window // 2
@@ -1123,19 +1131,20 @@
             pl.BlockSpec((model, model), lambda s, p, j: (0, 3), pipeline_mode=once),
             whole(turned),
             whole(gains),
+            whole(biases),
             whole(places),
             whole(early),
         ],
         out_specs=[
             held((n, share, wide)),
-            held((LATE + lines, 128)),
+            held((lines, 128)),
             pl.BlockSpec((1, half, width, model), own_at),
             anywhere,
             anywhere,
         ],
         out_shape=[
             jax.ShapeDtypeStruct((n, share, wide), B16),
-            jax.ShapeDtypeStruct((LATE + lines, 128), F32),
+            jax.ShapeDtypeStruct((lines, 128), F32),
             jax.ShapeDtypeStruct((pages, half, width, model), B16),
             jax.ShapeDtypeStruct((pages, half, width, model), B16),
             jax.ShapeDtypeStruct((pages, half, width + 8, model), B16),
@@ -1157,7 +1166,7 @@
             vmem((heads // 2, KEYS, SLOT), F32),
             vmem((heads, KEYS, SLOT), F32),
             vmem((3 * part_rows, SLOT), F32),
-            vmem((16, model), F32),
+            vmem((8, model), F32),
             vmem((2, model, wide), B16),
             vmem((pages, half, width + 8, model), B16),
             vmem((n - 2, chips, share, wide), B16),
@@ -1178,12 +1187,11 @@
             dma((n, devices[0])),
         ]
         + small_scratch(lines)
-        + small_scratch(LATE)
         + [dma((n - 2, chips)), dma((1 + pages * quads,)), dma((1 + pages * quads,))],
         compiler_params=pltpu.CompilerParams(
             vmem_limit_bytes=62 * 2**20, collective_id=0, has_side_effects=True
         ),
-    )(live, dwup, dwout, mixed_next, gf, x, n1, qkv, probs, att, weights_in, turned, gains, places, early)
+    )(live, dwup, dwout, mixed_next, gf, x, n1, qkv, probs, att, weights_in, turned, gains, biases, places, early)
 
 
 def finish_kernel(
@@ -1345,7 +1353,7 @@
     )
     sums, small, patch_own, above, edge = attn_backward(
         page_windows, dwup, dwout, mixed_next, gf, x, n1, qkv, probs, att, weights_in, turned, norm_gains,
-        places, early, patches.shape, heads, least, master_in.shape[0],
+        bias_lines, places, early, patches.shape, heads, least, master_in.shape[0],
     )
     mixed, patch_grad, new_in, moment_in, square_in, new_out, moment_out, square_out = finish(
         page_windows, sums, master_in, first_in, second_in, master_out, first_out, second_out, above, patch_own,

time: 194 us -> 185 us (0.954)
  Pallas kernels: 183 us -> 174 us
    pallas_call x1, Pallas kernels: 58 us -> 51.6 us  [mlp(): pl.pallas_call(functools.partial(mlp_kernel, (window, half, width, model,...]
    pallas_call x1, Pallas kernels: 74.5 us -> 71.8 us  [attn_backward(): pl.pallas_call(functools.partial(attn_backward_kernel, (window, half, wid...]
where the time goes in v4:
time: 185 us; the launch traced here: 184 us
  Pallas kernels  174 us (94%)
  local copies, waits for them, and re-layouts  6.97 us (4%)
    pallas_call x1, Pallas kernels, attn_backward(): pl.pallas_call(functools.partial(attn_backward_kernel, (window, half, wid...  71.8 us
    pallas_call x1, Pallas kernels, mlp(): pl.pallas_call(functools.partial(mlp_kernel, (window, half, width, model,...  51.6 us
    pallas_call x1, Pallas kernels, attn_forward(): pl.pallas_call(functools.partial(attn_forward_kernel, (window, half, widt...  42 us
    pallas_call x1, Pallas kernels, finish(): pl.pallas_call(functools.partial(finish_kernel, (window, half, width, lea...  9.02 us

profile of v4, /device:TPU:0, one launch (start us, length us, event | category | flops | bytes accessed | tf_op | source)
XLA Modules:
  0.0 183.7 jit_solution(2379444560770206134)
XLA Ops:
  0.6 0.7 copy.37
  1.3 0.7 convert_element_type.12
  2.0 0.7 constant_dynamic-update-slice_fusion.1
  2.8 0.1 convert_element_type.13
  2.9 0.1 copy.32
  3.0 0.1 convert_element_type.15
  3.1 0.6 pad.4.label_ref
  3.7 0.9 copy.33.tab_ref
  4.6 0.0 copy-start
  4.6 0.1 reshape.49
  4.7 0.5 copy-done
  5.2 42.0 %shard_map.257 = (bf16[2400,512]{1,0:T(8,128)(2,1)}, bf16[3072,512]{1,0:T(8,128)(2,1)}, bf16[3,512,3072]{2,1,0:T(8,128)(2,1)}, bf16[24,8,128,256]{3,2,1,0:T(8,12...) custom-call(s32[2]{0:T(128)} %live_ref.7, ...), custom_call_target="tpu_custom_call" | custom-call | tf_op jit(solution)/shard_map/pallas_call | solution.py:336
  47.2 51.6 %shard_map.258 = (bf16[512,2048]{1,0:T(8,128)(2,1)}, bf16[512,2048]{1,0:T(8,128)(2,1)}, f32[2400,512]{1,0:T(8,128)}, bf16[2,10,120,512]{3,2,1,0:T(8,128)(2,1)}, ...) custom-call(s32[2]{0:T(128)} %live_ref.7, bf16[2,10,120,512]{3,2,1,0:T(8,128)(2,1)} %low_ref.3, ...), custom_call_target="tpu_custom_call" | custom-call | tf_op jit(solution)/shard_map/pallas_call | solution.py:554
  98.8 0.0 copy-start.1
  98.8 0.0 copy-start.2
  98.8 71.8 %shard_map.259 = (bf16[6,64,1024]{2,1,0:T(8,128)(2,1)}, f32[96,128]{1,0:T(8,128)}, bf16[2,5,120,512]{3,2,1,0:T(8,128)(2,1)}, bf16[2,5,120,512]{3,2,1,0:T(8,128)(2,1)}, bf16[2,5,128,512]{3,2,1,0:T(8,128)(2,1)}) custom-call(s32[2]{0:T(128)} %live_ref.7, bf16[512,2048]{1,0:T(8,128)(2,1)} %get-tuple-element.43.up_ref, ...), custom_call_target="tpu_custom_call" | custom-call | tf_op jit(solution)/shard_map/pallas_call | solution.py:1115
  170.6 0.7 fusion.2
  171.3 0.7 slice.27
  172.0 0.7 slice.28
  172.8 0.7 slice.29
  173.6 0.1 copy.36
  173.7 0.1 reshape.53
  173.8 0.0 copy-done.1
  173.8 0.0 copy-done.2
  173.8 0.7 multiply_subtract_fusion
  174.5 9.0 %shard_map.260 = (bf16[2,10,120,512]{3,2,1,0:T(8,128)(2,1)}, bf16[2,10,120,512]{3,2,1,0:T(8,128)(2,1)}, f32[64,4096]{1,0:T(8,128)}, f32[64,4096]{1,0:T(8,128)}, ...) custom-call(s32[2]{0:T(128)} %live_ref.7, ...), custom_call_target="tpu_custom_call", output_to_operand_aliasing={{0}: (11, {})} | custom-call | tf_op jit(solution)/shard_map/pallas_call | solution.py:1267
  (5 shorter events, 0.0 us)
Async XLA Ops:
  4.6 0.7 copy-start
  98.8 75.0 %copy-start.1 = (f32[11920]{0:T(1024)S(1)}, f32[11920]{0:T(1024)}, u32[]{:S(2)}) copy-start(f32[11920]{0:T(1024)} %param.34) | copy-start | bytes 143044
  98.8 75.0 %copy-start.2 = (f32[11920]{0:T(1024)S(1)}, f32[11920]{0:T(1024)}, u32[]{:S(2)}) copy-start(f32[11920]{0:T(1024)} %param.35) | copy-start | bytes 143044

commit v5 on v4

--- a/solution.py
+++ b/solution.py
@@ -144,8 +144,8 @@
     vecs,
     column,
     square,
-    tall,
     flat,
+    marks,
 ):
     window, half, width, model, heads, least, pages, rows_count = sizes
     slots = window * window
@@ -210,14 +210,12 @@
         places = square[...].T[:KEYS]
         places_ref[...] = places
         off = jnp.maximum(places, 0)
-        tall[...] = jnp.zeros_like(tall)
-        tall[: tab_ref.shape[0], :heads] = tab_ref[...] * LOG2E
-        for c in range(tall.shape[0] // 128):
-            flat[:, 128 * c : 128 * c + 128] = tall[128 * c : 128 * c + 128, :].T[:heads]
+        flat[...] = jnp.zeros_like(flat)
+        flat[:, : tab_ref.shape[1]] = tab_ref[...] * LOG2E
         low, high = jnp.bitwise_and(off, 127), jnp.right_shift(off, 7)
         for h in range(heads):
             got = jnp.zeros((KEYS, SLOT), F32)
-            for c in range(tall.shape[0] // 128):
+            for c in range(flat.shape[1] // 128):
                 source = jnp.broadcast_to(flat[h : h + 1, 128 * c : 128 * c + 128], (KEYS, SLOT))
                 picked = jnp.take_along_axis(source, low, axis=1, mode="promise_in_bounds")
                 got = jnp.where(high == c, picked, got)
@@ -273,8 +271,21 @@
         qkv_ref[2, at, :] = got[2 * part_rows :].astype(B16)
 
     sames = []
+    lane = lax.broadcasted_iota(jnp.int32, (1, SLOT), 1)
+    for j in range(width // window // QUAD):
+
+        @pl.when(quad == j)
+        def _():
+            at = QUAD * window * j
+            marks[:, : QUAD * window] = label_ref[0, :, at : at + QUAD * window].astype(F32)
+
     for w in range(QUAD):
-        spread = jnp.broadcast_to(label_ref[0, w : w + 1, :], (SLOT, SLOT))
+        label = jnp.full((1, SLOT), -1.0, F32)
+        for r in range(window):
+            turned = pltpu.roll(marks[r : r + 1, :], (window * (r - w)) % SLOT, 1)
+            here = jnp.logical_and(lane >= window * r, lane < window * (r + 1))
+            label = jnp.where(here, turned, label)
+        spread = jnp.broadcast_to(label, (SLOT, SLOT))
         sames.append((spread == spread.T)[:KEYS])
     pair = 2 * size_head
 
@@ -324,7 +335,7 @@
 def attn_forward(live, patches, out_grad, labels, off, tab, weights_in, gains, biases, least):
     pages, window, width, model = patches.shape
     half = window // 2
-    table_rows, heads = tab.shape
+    heads, table_rows = tab.shape
     table_lanes = -(-table_rows // 128) * 128
     quads = width // window // QUAD
     tokens = pages * window * width
@@ -344,7 +355,7 @@
             pl.BlockSpec(memory_space=pl.ANY),
             pl.BlockSpec(memory_space=pl.ANY),
             pl.BlockSpec((1, half, width, model), lambda p, j: (p, 1, 0, 0)),
-            pl.BlockSpec((1, 8, SLOT), lambda p, j: (at(p, j), 0, 0)),
+            pl.BlockSpec((1, window, width), lambda p, j: (p, 0, 0)),
             whole(off),
             whole(tab),
             pl.BlockSpec((model, 3 * model), lambda p, j: (0, 0), pipeline_mode=pl.Buffered(1)),
@@ -391,8 +402,8 @@
             pltpu.VMEM((8, model), F32),
             pltpu.VMEM((2, 3 * model // 2, 128), F32),
             pltpu.VMEM((SLOT, SLOT), jnp.int32),
-            pltpu.VMEM((table_lanes, 128), F32),
             pltpu.VMEM((heads, table_lanes), F32),
+            pltpu.VMEM((window, SLOT), F32),
         ],
         compiler_params=pltpu.CompilerParams(
             vmem_limit_bytes=VMEM_LIMIT, collective_id=1, has_side_effects=True
@@ -538,8 +549,8 @@
             unwrap_band(band, live, half, width, window, least)
             own_ref[page] = band[:half, :width].astype(B16)
             next_ref[page] = band[half:, :width].astype(B16)
-        for k in range(4):
-            lay_lines(early_ref, (4 + k) * lines, jnp.sum(sums[8 * k : 8 * k + 8, :], axis=0, keepdims=True))
+        for k, place in enumerate((1, 5, 6, 7)):
+            lay_lines(early_ref, place * lines, jnp.sum(sums[8 * k : 8 * k + 8, :], axis=0, keepdims=True))
 
 
 def mlp(live, out_grad, halo, n2, first, weights_in, weights_out, gains, biases, least, share, lines):
@@ -815,6 +826,7 @@
     early_ref,
     sum_ref,
     small_ref,
+    table_ref,
     own_ref,
     mixed_halo_ref,
     patch_halo_ref,
@@ -912,7 +924,7 @@
         big.start_one(h, matrices[h])
         for k, part in enumerate((0, 2)):
             total = jnp.sum(dbqkv[part * part_rows : (part + 1) * part_rows, :].T, axis=0, keepdims=True)
-            lay_lines(early.mine, lines * (2 + k) + h * (lines // 2), total)
+            lay_lines(early.mine, lines * (3 + k) + h * (lines // 2), total)
         column = jnp.sum(dbqkv[...], axis=1, keepdims=True)
         weights = turned_ref[h].astype(F32)
         shifts = jnp.sum(weights * column, axis=0, keepdims=True)
@@ -923,7 +935,7 @@
             lay_row(vecs, 2, biases_ref, 0, lines)
             total = (vecs[0:1, :] - vecs[2:3, :] * vecs[1:2, :]) / gains_ref[0:1, :]
             lay_lines(early.mine, 0, total)
-            lay_lines(early.mine, lines, vecs[1:2, :])
+            lay_lines(early.mine, 2 * lines, vecs[1:2, :])
         dscores[h * heads // 2 : (h + 1) * heads // 2] = dscore[...]
         if h == 0:
             for ref in (dwq, dbqkv, dscore):
@@ -1063,7 +1075,11 @@
         early.start_three()
         big.start_four(1)
         mixed_copy().wait()
-        early.finish(small_ref, 0)
+        early.finish(early.mine, 0)
+        top = small_ref.shape[0]
+        small_ref[...] = early.mine[:top]
+        for c in range(table_ref.shape[0] // 128):
+            table_ref[128 * c : 128 * c + 128, :] = early.mine[top + heads * c : top + heads * (c + 1), :].T
         big.finish(1, sum_ref.at[1])
         for p in range(pages):
             for j in range(quads):
@@ -1099,6 +1115,7 @@
     vmem = pltpu.VMEM
     n = 2 + 2 * hidden // wide
     lines = early.shape[0]
+    chunks = -(-((2 * window - 1) ** 2) // 128)
 
     def small_scratch(rows):
         return [
@@ -1137,14 +1154,16 @@
         ],
         out_specs=[
             held((n, share, wide)),
-            held((lines, 128)),
+            held((lines - chunks * heads, 128)),
+            held((128 * chunks, heads)),
             pl.BlockSpec((1, half, width, model), own_at),
             anywhere,
             anywhere,
         ],
         out_shape=[
             jax.ShapeDtypeStruct((n, share, wide), B16),
-            jax.ShapeDtypeStruct((lines, 128), F32),
+            jax.ShapeDtypeStruct((lines - chunks * heads, 128), F32),
+            jax.ShapeDtypeStruct((128 * chunks, heads), F32),
             jax.ShapeDtypeStruct((pages, half, width, model), B16),
             jax.ShapeDtypeStruct((pages, half, width, model), B16),
             jax.ShapeDtypeStruct((pages, half, width + 8, model), B16),
@@ -1197,16 +1216,16 @@
 def finish_kernel(
     sizes,
     live_ref,
-    sum_ref,
-    min_ref,
-    fin_ref,
-    sin_ref,
-    mout_ref,
-    fout_ref,
-    sout_ref,
+    sum_hbm,
+    min_hbm,
+    fin_hbm,
+    sin_hbm,
+    mout_hbm,
+    fout_hbm,
+    sout_hbm,
     above_ref,
     own_ref,
-    edge_ref,
+    edge_hbm,
     _,
     mixed_ref,
     patch_ref,
@@ -1216,81 +1235,117 @@
     new_out_ref,
     moment_out_ref,
     square_out_ref,
+    sums,
+    olds_in,
+    news_in,
+    olds_out,
+    news_out,
+    edges,
+    tops,
+    passed,
     band,
-    grad_in,
+    sems,
+    frame_sems,
+    in_sems,
+    out_sems,
 ):
     window, half, width, least = sizes
-    step = pl.program_id(0)
     model = band.shape[2]
     part_rows = model // 2
-    for s in range(FINISH_STEPS):
-
-        @pl.when(step == s)
-        def _():
-            if s < 2:
-                for h in range(2):
-                    for part in range(2):
-                        at = part * model + h * part_rows
-                        from_at = (2 * s + part) * part_rows
-                        grad_in[:, at : at + part_rows] = sum_ref[h, :, from_at : from_at + part_rows].astype(F32)
-            else:
-                grad_in[...] = sum_ref[s].astype(F32)
-            cols = slice(model * (s % 2), model * (s % 2 + 1))
-            grad = sum_ref[4 + s // 2, :, cols].astype(F32)
-            new, moment, square = adam_update(mout_ref[...], fout_ref[...], sout_ref[...], grad)
-            new_out_ref[...], moment_out_ref[...], square_out_ref[...] = new, moment, square
-            if s % 2 == 0:
-                mixed_ref[...] = above_ref[...]
-                band[...] = edge_ref[0].astype(F32)
-                unwrap_band(band, live_ref[s // 2], half, width, window, least)
-                patch_ref[0] = band[:, :width].astype(B16)
-            else:
-                patch_ref[0] = own_ref[0]
-
-    new, moment, square = adam_update(min_ref[...], fin_ref[...], sin_ref[...], grad_in[...])
-    new_in_ref[...], moment_in_ref[...], square_in_ref[...] = new, moment, square
-
-
-FINISH_STEPS = 4
+    share = sums.shape[1]
+    pages = edges.shape[0]
+    pieces = olds_in.shape[2] // (2 * model)
+    tall = olds_out.shape[1] // pieces
+
+    def cut(ref, k):
+        return ref.at[:, pl.ds(2 * model * k, 2 * model)]
+
+    def stripe(ref, k):
+        return ref.at[pl.ds(tall * k, tall), :]
+
+    copy = pltpu.make_async_copy
+    passing = [copy(above_ref, passed.at[0], sems.at[2]), copy(own_ref, passed.at[1], sems.at[3])]
+    framed = [
+        copy(passed.at[0], mixed_ref.at[:, pl.ds(0, half)], frame_sems.at[0]),
+        copy(passed.at[1], patch_ref.at[:, pl.ds(half, half)], frame_sems.at[1]),
+    ]
+    fetched = [copy(sum_hbm, sums, sems.at[0]), copy(edge_hbm, edges, sems.at[1])]
+    laid = copy(tops, patch_ref.at[:, pl.ds(0, half)], frame_sems.at[2])
+    ins, outs = [], []
+    for k in range(pieces):
+        for i, (src, dst) in enumerate(zip((min_hbm, fin_hbm, sin_hbm), (new_in_ref, moment_in_ref, square_in_ref))):
+            ins.append(copy(cut(src, k), cut(olds_in.at[i], k), in_sems.at[6 * k + i]))
+            outs.append(copy(cut(news_in.at[i], k), cut(dst, k), out_sems.at[6 * k + i]))
+        for i, (src, dst) in enumerate(zip((mout_hbm, fout_hbm, sout_hbm), (new_out_ref, moment_out_ref, square_out_ref))):
+            ins.append(copy(stripe(src, k), stripe(olds_out.at[i], k), in_sems.at[6 * k + 3 + i]))
+            outs.append(copy(stripe(news_out.at[i], k), stripe(dst, k), out_sems.at[6 * k + 3 + i]))
+    start(fetched)
+    start(ins[:6])
+    start(passing)
+    start(ins[6:])
+    wait(fetched)
+    for p in range(pages):
+        band[...] = edges[p].astype(F32)
+        unwrap_band(band, live_ref[p], half, width, window, least)
+        tops[p] = band[:, :width].astype(B16)
+    laid.start()
+    wait(passing)
+    start(framed)
+    for k in range(pieces):
+        wait(ins[6 * k : 6 * k + 6])
+        at = slice(2 * model * k, 2 * model * (k + 1))
+        if k < 2:
+            grad = jnp.concatenate(
+                [
+                    sums[h, :, (2 * k + part) * part_rows : (2 * k + part + 1) * part_rows]
+                    for part in range(2)
+                    for h in range(2)
+                ],
+                axis=1,
+            )
+        else:
+            grad = sums[k]
+        updated = adam_update(olds_in[0, :, at], olds_in[1, :, at], olds_in[2, :, at], grad.astype(F32))
+        for i in range(3):
+            news_in[i, :, at] = updated[i]
+        start(outs[6 * k : 6 * k + 3])
+        rows = slice(tall * k, tall * (k + 1))
+        grad = sums[4 + k // 2, :, model * (k % 2) : model * (k % 2 + 1)]
+        updated = adam_update(olds_out[0, rows], olds_out[1, rows], olds_out[2, rows], grad.astype(F32))
+        for i in range(3):
+            news_out[i, rows] = updated[i]
+        start(outs[6 * k + 3 : 6 * k + 6])
+    wait(framed)
+    wait(outs)
+    laid.wait()
 
 
 def finish(live, sums, master_in, first_in, second_in, master_out, first_out, second_out, above, own, edge, mixed, least):
     pages, window, width, model = mixed.shape
     half = window // 2
-    share, wide = master_in.shape
-    tall = master_out.shape[0]
-    cols = pl.BlockSpec((share, wide // FINISH_STEPS), lambda s: (0, s))
-    rows = pl.BlockSpec((tall // FINISH_STEPS, model), lambda s: (s, 0))
-    page = lambda s: (s // 2, 0, 0, 0)
-    band = (1, half, width, model)
+    pieces = master_in.shape[1] // (2 * model)
+    anywhere = pl.BlockSpec(memory_space=pl.ANY)
     like = lambda a: jax.ShapeDtypeStruct(a.shape, a.dtype)
+    dma = pltpu.SemaphoreType.DMA
     return pl.pallas_call(
         functools.partial(finish_kernel, (window, half, width, least)),
-        grid=(FINISH_STEPS,),
-        in_specs=[
-            pl.BlockSpec(memory_space=pltpu.SMEM),
-            pl.BlockSpec(sums.shape, lambda s: (0, 0, 0), pipeline_mode=pl.Buffered(1)),
-            cols,
-            cols,
-            cols,
-            rows,
-            rows,
-            rows,
-            pl.BlockSpec(band, page),
-            pl.BlockSpec(band, page),
-            pl.BlockSpec((1, half, width + 8, model), page),
-            pl.BlockSpec(memory_space=pl.ANY),
-        ],
-        out_specs=[
-            pl.BlockSpec(band, page),
-            pl.BlockSpec(band, lambda s: (s // 2, s % 2, 0, 0)),
-        ]
-        + [cols] * 3
-        + [rows] * 3,
+        in_specs=[pl.BlockSpec(memory_space=pltpu.SMEM)] + [anywhere] * 11,
+        out_specs=[anywhere] * 8,
         out_shape=[like(mixed), like(mixed)] + [like(master_in)] * 3 + [like(master_out)] * 3,
         scratch_shapes=[
+            pltpu.VMEM(sums.shape, B16),
+            pltpu.VMEM((3,) + master_in.shape, F32),
+            pltpu.VMEM((3,) + master_in.shape, F32),
+            pltpu.VMEM((3,) + master_out.shape, F32),
+            pltpu.VMEM((3,) + master_out.shape, F32),
+            pltpu.VMEM(edge.shape, B16),
+            pltpu.VMEM(above.shape, B16),
+            pltpu.VMEM((2,) + above.shape, B16),
             pltpu.VMEM((half, width + 8, model), F32),
-            pltpu.VMEM((share, wide // FINISH_STEPS), F32),
+            dma((4,)),
+            dma((3,)),
+            dma((6 * pieces,)),
+            dma((6 * pieces,)),
         ],
         input_output_aliases={11: 0},
         compiler_params=pltpu.CompilerParams(vmem_limit_bytes=VMEM_LIMIT),
@@ -1336,22 +1391,19 @@
     table_rows, heads = bias_table.shape
     hidden = weights_out.shape[0]
 
-    labels = region_ids.reshape(pages, window, count, window).transpose(0, 2, 1, 3)
-    labels = labels.reshape(pages * count // QUAD, QUAD, slots).astype(F32)
-    labels = jnp.pad(labels, ((0, 0), (0, 8 - QUAD), (0, SLOT - slots)), constant_values=-1.0)
     bias_lines = biases.reshape(-1, 128)
     lines = model // 128
     table_lanes = -(-table_rows // 128) * 128
     early_lines = EARLY_UP * lines + hidden // 128 + table_lanes * heads // 128
 
     x, n1, qkv, probs, att, first, n2, below_grad, turned, places = attn_forward(
-        page_windows, patches, out_grad, labels, offset_index, bias_table, weights_in, norm_gains, bias_lines, least
+        page_windows, patches, out_grad, region_ids, offset_index, bias_table.T, weights_in, norm_gains, bias_lines, least
     )
     dwup, dwout, gf, mixed_own, mixed_next, early = mlp(
         page_windows, out_grad, below_grad, n2, first, weights_in, weights_out, norm_gains, bias_lines,
         least, master_in.shape[0], early_lines,
     )
-    sums, small, patch_own, above, edge = attn_backward(
+    sums, small, total_table, patch_own, above, edge = attn_backward(
         page_windows, dwup, dwout, mixed_next, gf, x, n1, qkv, probs, att, weights_in, turned, norm_gains,
         bias_lines, places, early, patches.shape, heads, least, master_in.shape[0],
     )
@@ -1359,12 +1411,7 @@
         page_windows, sums, master_in, first_in, second_in, master_out, first_out, second_out, above, patch_own,
         edge, mixed_own, least,
     )
-    small_at = [0, 4, 1, 2, 3, 5, 6, 7]
-    table_at = small.shape[0] - table_lanes * heads // 128
-    total_table = small[table_at:].reshape(table_lanes // 128, heads, 128).transpose(0, 2, 1)
-    total_table = total_table.reshape(table_lanes, heads)[:table_rows]
-    head = [small[lines * k : lines * k + lines] for k in small_at] + [small[8 * lines : table_at]]
-    total_small = jnp.concatenate([jnp.concatenate(head).reshape(-1), total_table.reshape(-1)])
+    total_small = jnp.concatenate([small.reshape(-1), total_table[:table_rows].reshape(-1)])
     small_master = jnp.concatenate([norm_gains.reshape(-1), biases, bias_table.reshape(-1)])
     new_small, moment_small, square_small = adam_update(
         small_master, first_small, second_small, total_small

time: 185 us -> 180 us (0.973)
  local copies, waits for them, and re-layouts: 6.97 us -> 2.64 us
    slice x5 -> x1, local copies, waits for them, and re-layouts: 2.98 us -> 0.94 us  [shards(): total_table[:table_rows].reshape(-1)]
where the time goes in v5:
time: 180 us
  Pallas kernels  175 us (97%)
  local copies, waits for them, and re-layouts  2.64 us (1%)
    pallas_call x1, Pallas kernels, attn_backward(): pl.pallas_call(functools.partial(attn_backward_kernel, (window, half, wid...  72.8 us
    pallas_call x1, Pallas kernels, mlp(): pl.pallas_call(functools.partial(mlp_kernel, (window, half, width, model,...  51.5 us
    pallas_call x1, Pallas kernels, attn_forward(): pl.pallas_call(functools.partial(attn_forward_kernel, (window, half, widt...  42.4 us
    pallas_call x1, Pallas kernels, finish(): pl.pallas_call(functools.partial(finish_kernel, (window, half, width, lea...  7.82 us

profile of v5, /device:TPU:0, one launch (start us, length us, event | category | flops | bytes accessed | tf_op | source)
XLA Modules:
  0.0 179.6 jit_solution(11299938329100601186)
XLA Ops:
  0.6 1.3 copy.31.label_ref
  2.0 42.4 %shard_map.257 = (bf16[2400,512]{1,0:T(8,128)(2,1)}, bf16[3072,512]{1,0:T(8,128)(2,1)}, bf16[3,512,3072]{2,1,0:T(8,128)(2,1)}, bf16[24,8,128,256]{3,2,1,0:T(8,12...) custom-call(s32[2]{0:T(128)} %live_ref.7, ...), custom_call_target="tpu_custom_call" | custom-call | tf_op jit(solution)/shard_map/pallas_call | solution.py:347
  44.4 51.5 %shard_map.258 = (bf16[512,2048]{1,0:T(8,128)(2,1)}, bf16[512,2048]{1,0:T(8,128)(2,1)}, f32[2400,512]{1,0:T(8,128)}, bf16[2,10,120,512]{3,2,1,0:T(8,128)(2,1)}, ...) custom-call(s32[2]{0:T(128)} %live_ref.7, bf16[2,10,120,512]{3,2,1,0:T(8,128)(2,1)} %low_ref.3, ...), custom_call_target="tpu_custom_call" | custom-call | tf_op jit(solution)/shard_map/pallas_call | solution.py:565
  95.9 0.0 copy-start.1
  95.9 0.0 copy-start.2
  96.0 0.0 copy-start
  96.0 0.0 copy-start.3
  96.0 0.0 copy-start.4
  96.0 72.8 %shard_map.259 = (bf16[6,64,1024]{2,1,0:T(8,128)(2,1)}, f32[48,128]{1,0:T(8,128)}, f32[384,16]{1,0:T(8,128)}, bf16[2,5,120,512]{3,2,1,0:T(8,128)(2,1)}, bf16[2,5...) custom-call(s32[2]{0:T(128)} %live_ref.7, bf16[512,2048]{1,0:T(8,128)(2,1)} %get-tuple-element.44.up_ref, ...), custom_call_target="tpu_custom_call" | custom-call | tf_op jit(solution)/shard_map/pallas_call | solution.py:1132
  168.8 0.9 slice.3
  169.7 0.1 reshape.41
  169.8 0.0 copy-done.1
  169.9 0.1 copy.32
  170.0 0.1 reshape.39
  170.1 0.0 copy-done.2
  170.1 0.0 copy-done
  170.2 0.0 copy-done.3
  170.2 0.0 copy-done.4
  170.2 1.4 multiply_subtract_fusion
  171.6 7.8 %shard_map.260 = (bf16[2,10,120,512]{3,2,1,0:T(8,128)(2,1)}, bf16[2,10,120,512]{3,2,1,0:T(8,128)(2,1)}, f32[64,4096]{1,0:T(8,128)}, f32[64,4096]{1,0:T(8,128)}, ...) custom-call(s32[2]{0:T(128)} %live_ref.7, ...), custom_call_target="tpu_custom_call", output_to_operand_aliasing={{0}: (11, {})} | custom-call | tf_op jit(solution)/shard_map/pallas_call | solution.py:1330
  (4 shorter events, 0.0 us)
Async XLA Ops:
  95.9 73.9 %copy-start.1 = (f32[361,16]{0,1:T(8,128)S(1)}, f32[361,16]{0,1:T(8,128)}, u32[]{:S(2)}) copy-start(f32[361,16]{0,1:T(8,128)} %param.27) | copy-start | bytes 69316
  95.9 74.2 %copy-start.2 = (f32[2,512]{1,0:T(2,128)S(1)}, f32[2,512]{1,0:T(2,128)}, u32[]{:S(2)}) copy-start(f32[2,512]{1,0:T(2,128)} %gains_ref.5) | copy-start | bytes 12292
  96.0 74.2 %copy-start = (f32[5120]{0:T(1024)S(1)}, f32[5120]{0:T(1024)}, u32[]{:S(2)}) copy-start(f32[5120]{0:T(1024)} %param.26) | copy-start | bytes 61444
  96.0 74.2 %copy-start.3 = (f32[11920]{0:T(1024)S(1)}, f32[11920]{0:T(1024)}, u32[]{:S(2)}) copy-start(f32[11920]{0:T(1024)} %param.34) | copy-start | bytes 143044
  96.0 74.2 %copy-start.4 = (f32[11920]{0:T(1024)S(1)}, f32[11920]{0:T(1024)}, u32[]{:S(2)}) copy-start(f32[11920]{0:T(1024)} %param.35) | copy-start | bytes 143044

commit v6 on v5

--- a/solution.py
+++ b/solution.py
@@ -413,7 +413,7 @@
 
 MLP_COLS = 1024
 MLP_CHUNKS = 2
-MLP_ROWS = 480
+MLP_ROWS = 800
 EARLY_UP = 8
 
 
@@ -423,16 +423,16 @@
     low_ref,
     high_ref,
     n2_ref,
-    first_ref,
+    first_hbm,
     wup_ref,
     wout_ref,
     gains_ref,
     biases_ref,
     dwup_ref,
     dwout_ref,
-    gf_ref,
-    own_ref,
-    next_ref,
+    gf_hbm,
+    own_hbm,
+    next_hbm,
     early_ref,
     bup,
     vecs,
@@ -443,6 +443,12 @@
     dn2,
     act_all,
     pre_all,
+    first_ref,
+    held,
+    frames,
+    first_sem,
+    gf_sems,
+    frame_sems,
 ):
     window, half, width, model, least, share = sizes
     pages = low_ref.shape[0]
@@ -460,8 +466,21 @@
         def _():
             lay_row(bup, 0, biases_ref, 6 * lines + c * (cols // 128), cols // 128)
 
+    first_copy = pltpu.make_async_copy(first_hbm, first_ref, first_sem)
+
+    def gf_copy(k):
+        rows = pl.ds(pl.multiple_of(k * QUAD * slots, 16), QUAD * slots)
+        return pltpu.make_async_copy(dn2.at[rows, :], gf_hbm.at[rows, :], gf_sems.at[k])
+
+    def frame_copies(page):
+        return [
+            pltpu.make_async_copy(frames.at[page, 0], own_hbm.at[page, pl.ds(half, half)], frame_sems.at[page, 0]),
+            pltpu.make_async_copy(frames.at[page, 1], next_hbm.at[page], frame_sems.at[page, 1]),
+        ]
+
     @pl.when(chunk == 0)
     def _():
+        first_copy.start()
         early_ref[...] = jnp.zeros_like(early_ref)
         vecs[0:1, :] = gains_ref[1:2, :]
         lay_row(vecs, 1, biases_ref, 5 * lines, lines)
@@ -474,9 +493,9 @@
                     alive = jnp.where(j * QUAD + w < live, 1.0, 0.0)
                     for r, part in enumerate(gather_window(band, j * QUAD * window, w, window, half)):
                         at = slots * w + window * r
-                        gf_ref[at : at + window, :] = part * alive
+                        held[at : at + window, :] = part * alive
                 rows = pl.ds(pl.multiple_of((page * quads + j) * QUAD * slots, 16), QUAD * slots)
-                cot[rows, :] = gf_ref[: QUAD * slots, :].astype(B16)
+                cot[rows, :] = held[...].astype(B16)
                 return carry
 
             lax.fori_loop(0, quads, body, 0)
@@ -517,6 +536,7 @@
     @pl.when(chunk == pl.num_programs(0) - 1)
     def _():
         sums[...] = jnp.zeros_like(sums)
+        first_copy.wait()
         for page in range(pages):
             live = live_ref[page]
 
@@ -532,7 +552,8 @@
                 mean_one = jnp.mean(scaled, axis=-1, keepdims=True)
                 mean_two = jnp.mean(scaled * xhat, axis=-1, keepdims=True)
                 whole = given + spread * (scaled - mean_one - xhat * mean_two)
-                gf_ref[rows, :] = whole
+                dn2[rows, :] = whole
+                gf_copy(page * quads + j).start()
                 sums[0:8, :] += fold(grad * xhat)
                 sums[8:16, :] += fold(whole)
                 sums[16:24, :] += fold(grad)
@@ -547,10 +568,15 @@
 
             lax.fori_loop(0, quads, body, 0)
             unwrap_band(band, live, half, width, window, least)
-            own_ref[page] = band[:half, :width].astype(B16)
-            next_ref[page] = band[half:, :width].astype(B16)
+            frames[page, 0] = band[:half, :width].astype(B16)
+            frames[page, 1] = band[half:, :width].astype(B16)
+            start(frame_copies(page))
         for k, place in enumerate((1, 5, 6, 7)):
             lay_lines(early_ref, place * lines, jnp.sum(sums[8 * k : 8 * k + 8, :], axis=0, keepdims=True))
+        for k in range(pages * quads):
+            gf_copy(k).wait()
+        for page in range(pages):
+            wait(frame_copies(page))
 
 
 def mlp(live, out_grad, halo, n2, first, weights_in, weights_out, gains, biases, least, share, lines):
@@ -570,7 +596,7 @@
             pl.BlockSpec(band_block, lambda c: (0, 1, 0, 0), pipeline_mode=once),
             pl.BlockSpec(band_block, lambda c: (0, 0, 0, 0), pipeline_mode=once),
             whole(n2),
-            whole(first),
+            pl.BlockSpec(memory_space=pl.ANY),
             pl.BlockSpec((model, MLP_COLS), lambda c: (0, c + skip)),
             pl.BlockSpec((MLP_COLS, model), lambda c: (c, 0)),
             whole(gains),
@@ -579,9 +605,9 @@
         out_specs=[
             pl.BlockSpec((model, MLP_COLS), lambda c: (0, c)),
             pl.BlockSpec((model * MLP_COLS // hidden, hidden), lambda c: (c, 0)),
-            pl.BlockSpec((tokens, model), lambda c: (0, 0), pipeline_mode=once),
-            pl.BlockSpec(band_block, lambda c: (0, 1, 0, 0), pipeline_mode=once),
-            pl.BlockSpec(band_block, lambda c: (0, 0, 0, 0), pipeline_mode=once),
+            pl.BlockSpec(memory_space=pl.ANY),
+            pl.BlockSpec(memory_space=pl.ANY),
+            pl.BlockSpec(memory_space=pl.ANY),
             pl.BlockSpec((lines, 128), lambda c: (0, 0)),
         ],
         out_shape=[
@@ -602,6 +628,12 @@
             pltpu.VMEM((tokens, model), F32),
             pltpu.VMEM((tokens, MLP_COLS), B16),
             pltpu.VMEM((tokens, MLP_COLS), B16),
+            pltpu.VMEM((tokens, model), F32),
+            pltpu.VMEM((QUAD * window * window, model), F32),
+            pltpu.VMEM((pages, 2, half, width, model), B16),
+            pltpu.SemaphoreType.DMA,
+            pltpu.SemaphoreType.DMA((tokens // (QUAD * window * window),)),
+            pltpu.SemaphoreType.DMA((pages, 2)),
         ],
         compiler_params=pltpu.CompilerParams(vmem_limit_bytes=VMEM_LIMIT),
     )(live, out_grad, halo, n2, first, weights_in, weights_out, gains, biases)

time: 180 us -> 176 us (0.978)
  Pallas kernels: 175 us -> 171 us
    pallas_call x1, Pallas kernels: 51.5 us -> 47.6 us  [mlp(): pl.pallas_call(functools.partial(mlp_kernel, (window, half, width, model,...]
where the time goes in v6:
time: 176 us
  Pallas kernels  171 us (97%)
  local copies, waits for them, and re-layouts  2.64 us (2%)
    pallas_call x1, Pallas kernels, attn_backward(): pl.pallas_call(functools.partial(attn_backward_kernel, (window, half, wid...  72.8 us
    pallas_call x1, Pallas kernels, mlp(): pl.pallas_call(functools.partial(mlp_kernel, (window, half, width, model,...  47.6 us
    pallas_call x1, Pallas kernels, attn_forward(): pl.pallas_call(functools.partial(attn_forward_kernel, (window, half, widt...  42.4 us
    pallas_call x1, Pallas kernels, finish(): pl.pallas_call(functools.partial(finish_kernel, (window, half, width, lea...  7.82 us

profile of v6, /device:TPU:0, one launch (start us, length us, event | category | flops | bytes accessed | tf_op | source)
XLA Modules:
  0.0 175.7 jit_solution(7080977341302249802)
XLA Ops:
  0.6 1.3 copy.31.label_ref
  2.0 42.4 %shard_map.257 = (bf16[2400,512]{1,0:T(8,128)(2,1)}, bf16[3072,512]{1,0:T(8,128)(2,1)}, bf16[3,512,3072]{2,1,0:T(8,128)(2,1)}, bf16[24,8,128,256]{3,2,1,0:T(8,12...) custom-call(s32[2]{0:T(128)} %live_ref.7, ...), custom_call_target="tpu_custom_call" | custom-call | tf_op jit(solution)/shard_map/pallas_call | solution.py:347
  44.4 47.6 %shard_map.258 = (bf16[512,2048]{1,0:T(8,128)(2,1)}, bf16[512,2048]{1,0:T(8,128)(2,1)}, f32[2400,512]{1,0:T(8,128)}, bf16[2,10,120,512]{3,2,1,0:T(8,128)(2,1)}, ...) custom-call(s32[2]{0:T(128)} %live_ref.7, bf16[2,10,120,512]{3,2,1,0:T(8,128)(2,1)} %low_ref.3, ...), custom_call_target="tpu_custom_call" | custom-call | tf_op jit(solution)/shard_map/pallas_call | solution.py:591
  92.0 0.0 copy-start.1
  92.0 0.0 copy-start.2
  92.0 0.0 copy-start
  92.0 0.0 copy-start.3
  92.0 0.0 copy-start.4
  92.0 72.8 %shard_map.259 = (bf16[6,64,1024]{2,1,0:T(8,128)(2,1)}, f32[48,128]{1,0:T(8,128)}, f32[384,16]{1,0:T(8,128)}, bf16[2,5,120,512]{3,2,1,0:T(8,128)(2,1)}, bf16[2,5...) custom-call(s32[2]{0:T(128)} %live_ref.7, bf16[512,2048]{1,0:T(8,128)(2,1)} %get-tuple-element.44.up_ref, ...), custom_call_target="tpu_custom_call" | custom-call | tf_op jit(solution)/shard_map/pallas_call | solution.py:1164
  164.8 0.9 slice.3
  165.8 0.1 reshape.41
  165.9 0.0 copy-done.1
  165.9 0.1 copy.32
  166.0 0.1 reshape.39
  166.2 0.0 copy-done.2
  166.2 0.0 copy-done
  166.2 0.0 copy-done.3
  166.2 0.0 copy-done.4
  166.2 1.4 multiply_subtract_fusion
  167.7 7.8 %shard_map.260 = (bf16[2,10,120,512]{3,2,1,0:T(8,128)(2,1)}, bf16[2,10,120,512]{3,2,1,0:T(8,128)(2,1)}, f32[64,4096]{1,0:T(8,128)}, f32[64,4096]{1,0:T(8,128)}, ...) custom-call(s32[2]{0:T(128)} %live_ref.7, ...), custom_call_target="tpu_custom_call", output_to_operand_aliasing={{0}: (11, {})} | custom-call | tf_op jit(solution)/shard_map/pallas_call | solution.py:1362
  (4 shorter events, 0.0 us)
Async XLA Ops:
  92.0 73.9 %copy-start.1 = (f32[361,16]{0,1:T(8,128)S(1)}, f32[361,16]{0,1:T(8,128)}, u32[]{:S(2)}) copy-start(f32[361,16]{0,1:T(8,128)} %param.27) | copy-start | bytes 69316
  92.0 74.2 %copy-start.2 = (f32[2,512]{1,0:T(2,128)S(1)}, f32[2,512]{1,0:T(2,128)}, u32[]{:S(2)}) copy-start(f32[2,512]{1,0:T(2,128)} %gains_ref.5) | copy-start | bytes 12292
  92.0 74.2 %copy-start = (f32[5120]{0:T(1024)S(1)}, f32[5120]{0:T(1024)}, u32[]{:S(2)}) copy-start(f32[5120]{0:T(1024)} %param.26) | copy-start | bytes 61444
  92.0 74.2 %copy-start.3 = (f32[11920]{0:T(1024)S(1)}, f32[11920]{0:T(1024)}, u32[]{:S(2)}) copy-start(f32[11920]{0:T(1024)} %param.34) | copy-start | bytes 143044
  92.0 74.2 %copy-start.4 = (f32[11920]{0:T(1024)S(1)}, f32[11920]{0:T(1024)}, u32[]{:S(2)}) copy-start(f32[11920]{0:T(1024)} %param.35) | copy-start | bytes 143044

commit v7 on v6

--- a/solution.py
+++ b/solution.py
@@ -986,8 +986,8 @@
         early.start_one()
 
     plan = {
-        (0, 2): [(two, 2), (two, 3)],
-        (0, 4): [(two, 4), (two, 5)],
+        (0, 1): [(two, 2), (two, 3)],
+        (0, 2): [(two, 4), (two, 5)],
         (1, 0): [(flush, 0), (big.start_three, 2), (big.start_three, 3)],
         (1, 1): [(two, 0)],
         (1, 4): [(big.start_three, 4), (big.start_three, 5), (big.start_four, 2), (big.start_four, 3)],

time: 176 us -> 174 us (0.989)
  Pallas kernels: 171 us -> 169 us
where the time goes in v7:
time: 174 us
  Pallas kernels  169 us (97%)
  local copies, waits for them, and re-layouts  2.64 us (2%)
    pallas_call x1, Pallas kernels, attn_backward(): pl.pallas_call(functools.partial(attn_backward_kernel, (window, half, wid...  71.2 us
    pallas_call x1, Pallas kernels, mlp(): pl.pallas_call(functools.partial(mlp_kernel, (window, half, width, model,...  47.6 us
    pallas_call x1, Pallas kernels, attn_forward(): pl.pallas_call(functools.partial(attn_forward_kernel, (window, half, widt...  42.4 us
    pallas_call x1, Pallas kernels, finish(): pl.pallas_call(functools.partial(finish_kernel, (window, half, width, lea...  7.82 us

profile of v7, /device:TPU:0, one launch (start us, length us, event | category | flops | bytes accessed | tf_op | source)
XLA Modules:
  0.0 174.1 jit_solution(463070800187670089)
XLA Ops:
  0.6 1.3 copy.31.label_ref
  2.0 42.4 %shard_map.257 = (bf16[2400,512]{1,0:T(8,128)(2,1)}, bf16[3072,512]{1,0:T(8,128)(2,1)}, bf16[3,512,3072]{2,1,0:T(8,128)(2,1)}, bf16[24,8,128,256]{3,2,1,0:T(8,12...) custom-call(s32[2]{0:T(128)} %live_ref.7, ...), custom_call_target="tpu_custom_call" | custom-call | tf_op jit(solution)/shard_map/pallas_call | solution.py:347
  44.4 47.6 %shard_map.258 = (bf16[512,2048]{1,0:T(8,128)(2,1)}, bf16[512,2048]{1,0:T(8,128)(2,1)}, f32[2400,512]{1,0:T(8,128)}, bf16[2,10,120,512]{3,2,1,0:T(8,128)(2,1)}, ...) custom-call(s32[2]{0:T(128)} %live_ref.7, bf16[2,10,120,512]{3,2,1,0:T(8,128)(2,1)} %low_ref.3, ...), custom_call_target="tpu_custom_call" | custom-call | tf_op jit(solution)/shard_map/pallas_call | solution.py:591
  92.0 0.0 copy-start.1
  92.0 0.0 copy-start.2
  92.0 0.0 copy-start
  92.0 0.0 copy-start.3
  92.0 0.0 copy-start.4
  92.0 71.2 %shard_map.259 = (bf16[6,64,1024]{2,1,0:T(8,128)(2,1)}, f32[48,128]{1,0:T(8,128)}, f32[384,16]{1,0:T(8,128)}, bf16[2,5,120,512]{3,2,1,0:T(8,128)(2,1)}, bf16[2,5...) custom-call(s32[2]{0:T(128)} %live_ref.7, bf16[512,2048]{1,0:T(8,128)(2,1)} %get-tuple-element.44.up_ref, ...), custom_call_target="tpu_custom_call" | custom-call | tf_op jit(solution)/shard_map/pallas_call | solution.py:1164
  163.2 0.9 slice.3
  164.2 0.1 reshape.41
  164.3 0.0 copy-done.1
  164.3 0.1 copy.32
  164.4 0.1 reshape.39
  164.5 0.0 copy-done.2
  164.6 0.0 copy-done
  164.6 0.0 copy-done.3
  164.6 0.0 copy-done.4
  164.6 1.4 multiply_subtract_fusion
  166.0 7.8 %shard_map.260 = (bf16[2,10,120,512]{3,2,1,0:T(8,128)(2,1)}, bf16[2,10,120,512]{3,2,1,0:T(8,128)(2,1)}, f32[64,4096]{1,0:T(8,128)}, f32[64,4096]{1,0:T(8,128)}, ...) custom-call(s32[2]{0:T(128)} %live_ref.7, ...), custom_call_target="tpu_custom_call", output_to_operand_aliasing={{0}: (11, {})} | custom-call | tf_op jit(solution)/shard_map/pallas_call | solution.py:1362
  (4 shorter events, 0.0 us)
Async XLA Ops:
  92.0 72.3 %copy-start.1 = (f32[361,16]{0,1:T(8,128)S(1)}, f32[361,16]{0,1:T(8,128)}, u32[]{:S(2)}) copy-start(f32[361,16]{0,1:T(8,128)} %param.27) | copy-start | bytes 69316
  92.0 72.5 %copy-start.2 = (f32[2,512]{1,0:T(2,128)S(1)}, f32[2,512]{1,0:T(2,128)}, u32[]{:S(2)}) copy-start(f32[2,512]{1,0:T(2,128)} %gains_ref.5) | copy-start | bytes 12292
  92.0 72.6 %copy-start = (f32[5120]{0:T(1024)S(1)}, f32[5120]{0:T(1024)}, u32[]{:S(2)}) copy-start(f32[5120]{0:T(1024)} %param.26) | copy-start | bytes 61444
  92.0 72.6 %copy-start.3 = (f32[11920]{0:T(1024)S(1)}, f32[11920]{0:T(1024)}, u32[]{:S(2)}) copy-start(f32[11920]{0:T(1024)} %param.34) | copy-start | bytes 143044
  92.0 72.6 %copy-start.4 = (f32[11920]{0:T(1024)S(1)}, f32[11920]{0:T(1024)}, u32[]{:S(2)}) copy-start(f32[11920]{0:T(1024)} %param.35) | copy-start | bytes 143044
